TPU v7x, 256 devices: a whole 4x4x8 slice. The times are simulated.
256 devices in a mesh: dp: 32 (over z_hi, y, core), seq: 8 (over z_lo, x).
Axes of the slice: x: 4, y: 4, z: 8 (z_hi: 4, z_lo: 2; z = z_hi * 2 + z_lo), core: 2. Of those that a mesh axis runs over, the one named last changes fastest.
Arguments:
- seq_in: bfloat16 [32, 2048, 768], P('dp', 'seq'), may hold values from -40 to 40
- bases: int32 [32, 131072], P('dp', 'seq'), may hold values from 0 to 3
- conv_weight: bfloat16 [3072, 768], P('dp'), may hold values from -0.109375 to 0.109375
- dna_weight: bfloat16 [512, 768], P('dp'), may hold values from -0.5 to 0.5
- qkv_weight: bfloat16 [768, 1536], P('dp'), may hold values from -12 to 12
- out_weight: bfloat16 [512, 768], P('dp'), may hold values from -0.25 to 0.25
- cotangent: bfloat16 [32, 1024, 768], P('dp', 'seq'), may hold values from -6 to 6
Outputs:
- seq_grad: bfloat16 [32, 2048, 768], P('dp', 'seq')
- conv_grad: float32 [3072, 768], P('dp')
- dna_grad: float32 [512, 768], P('dp')
- qkv_grad: float32 [768, 1536], P('dp')
- out_grad: float32 [512, 768], P('dp')
All inputs are finite; a program needn't handle non-finite values.
Results may differ from a plain program's by a relative error of at most 0.02.
Values may be sent and summed in bfloat16 or wider, within the bound.
A program may use at most 128 MiB of HBM per device.

v0:
```python
import math

import jax
import jax.numpy as jnp
from jax import lax
from jax.sharding import PartitionSpec as P

H = 4
BIN = 128


epsilon = 1e-06


def with_halo(shard, sides, width):
    for axis, dim in sides:
        peers, length = (lax.axis_size(axis), shard.shape[dim])
        up = [(i, (i + 1) % peers) for i in range(peers - 1)]
        down = [(j, i) for i, j in up]
        last = lax.slice_in_dim(shard, length - width, length, axis=dim)
        first = lax.slice_in_dim(shard, 0, width, axis=dim)
        before = lax.ppermute(last, axis, up)
        after = lax.ppermute(first, axis, down)
        shard = jnp.concatenate([before, shard, after], axis=dim)
    return shard


def unfold_rows(padded, length, channels):
    first_pair = padded[: 2 * length].reshape(length, 2 * channels)
    second_pair = padded[2:].reshape(length, 2 * channels)
    return jnp.concatenate([first_pair, second_pair], axis=1)


def row_product(left_rows, right_rows):
    return lax.dot_general(
        left_rows, right_rows, (((0,), (0,)), ((), ())), preferred_element_type=jnp.float32
    )


def right_product(left_rows, right_rows):
    return lax.dot_general(
        left_rows, right_rows, (((1,), (1,)), ((), ())), preferred_element_type=jnp.float32
    )


def data_shard(left_rows, right_rows):
    return lax.psum_scatter(
        row_product(left_rows, right_rows).astype(jnp.bfloat16),
        "dp",
        scatter_dimension=0,
        tiled=True,
    ).astype(jnp.float32)


def per_device(seq_in, bases, conv_weight, dna_weight, qkv_weight, out_weight, cotangent):
    rows_in = seq_in[0]
    upstream = cotangent[0]
    tokens_here = upstream.shape[0]
    channels = rows_in.shape[1]
    conv_full, dna_full, qkv_full, out_full = (
        lax.all_gather(conv_weight, "dp", axis=0, tiled=True),
        lax.all_gather(dna_weight, "dp", axis=0, tiled=True),
        lax.all_gather(qkv_weight, "dp", axis=0, tiled=True),
        lax.all_gather(out_weight, "dp", axis=0, tiled=True),
    )
    padded = with_halo(rows_in, (("seq", 0),), 1)
    unfolded = unfold_rows(padded, tokens_here, channels)
    letters = bases[0].reshape(tokens_here, BIN, 1)
    onehot = (
        (letters == jnp.arange(4, dtype=jnp.int32))
        .astype(jnp.bfloat16)
        .reshape(tokens_here, 4 * BIN)
    )
    pre_act = jnp.dot(unfolded, conv_full, preferred_element_type=jnp.float32) + jnp.dot(
        onehot, dna_full, preferred_element_type=jnp.float32
    )
    feature = jax.nn.gelu(pre_act).astype(jnp.bfloat16)
    feat_wide = feature.astype(jnp.float32)
    inverse = lax.rsqrt(jnp.mean(feat_wide * feat_wide, axis=1, keepdims=True) + epsilon)
    unit_rows = feat_wide * inverse
    normed = unit_rows.astype(jnp.bfloat16)
    projected = jnp.dot(normed, qkv_full, preferred_element_type=jnp.float32).astype(jnp.bfloat16)
    width = qkv_full.shape[1] // 3
    head_size = width // H
    scaling = 1.0 / math.sqrt(head_size)
    queries = projected[:, :width]
    local_keys = projected[:, width : 2 * width]
    local_values = projected[:, 2 * width :]
    keys_all, values_all = (
        lax.all_gather(local_keys, "seq", axis=0, tiled=True),
        lax.all_gather(local_values, "seq", axis=0, tiled=True),
    )
    d_attend = right_product(upstream, out_full).astype(jnp.bfloat16)
    attended = []
    query_grads = []
    weights_low = []
    score_grads = []
    log_totals = []
    inner_sums = []
    for head_index in range(H):
        columns = slice(head_index * head_size, (head_index + 1) * head_size)
        query_head = queries[:, columns]
        key_head = keys_all[:, columns]
        value_head = values_all[:, columns]
        scores = right_product(query_head, key_head) * scaling
        highest = jnp.max(scores, axis=1, keepdims=True)
        powers = jnp.exp(scores - highest)
        totals_row = jnp.sum(powers, axis=1, keepdims=True)
        probs = powers / totals_row
        probs_low = probs.astype(jnp.bfloat16)
        attended.append(
            jnp.dot(probs_low, value_head, preferred_element_type=jnp.float32).astype(jnp.bfloat16)
        )
        d_probs = right_product(d_attend[:, columns], value_head)
        inner = jnp.sum(probs * d_probs, axis=1, keepdims=True)
        d_scores = (probs * (d_probs - inner) * scaling).astype(jnp.bfloat16)
        query_grads.append(jnp.dot(d_scores, key_head, preferred_element_type=jnp.float32))
        weights_low.append(probs_low)
        score_grads.append(d_scores)
        log_totals.append(highest + jnp.log(totals_row))
        inner_sums.append(inner)
    prob_stack = jnp.stack(weights_low)
    grad_stack = jnp.stack(score_grads)
    query_heads = queries.reshape(tokens_here, H, head_size)
    attend_heads = d_attend.reshape(tokens_here, H, head_size)
    key_grad = jnp.einsum(
        "htk,thd->khd", grad_stack, query_heads, preferred_element_type=jnp.float32
    ).reshape(tokens_here * lax.axis_size("seq"), width)
    value_grad = jnp.einsum(
        "htk,thd->khd", prob_stack, attend_heads, preferred_element_type=jnp.float32
    ).reshape(tokens_here * lax.axis_size("seq"), width)
    key_sums = lax.psum_scatter(
        jnp.concatenate([key_grad, value_grad], axis=1), "seq", scatter_dimension=0, tiled=True
    )
    d_projected = jnp.concatenate([jnp.concatenate(query_grads, axis=1), key_sums], axis=1).astype(
        jnp.bfloat16
    )
    attend_all = jnp.concatenate(attended, axis=1)
    d_normed = right_product(d_projected, qkv_full)
    d_feature = upstream.astype(jnp.float32) + inverse * (
        d_normed - unit_rows * jnp.mean(d_normed * unit_rows, axis=1, keepdims=True)
    )
    d_pre = jax.vjp(jax.nn.gelu, pre_act)[1](d_feature)[0].astype(jnp.bfloat16)
    d_unfolded = right_product(d_pre, conv_full)
    lower_taps = d_unfolded[:, : 2 * channels].reshape(2 * tokens_here, channels)
    upper_taps = d_unfolded[:, 2 * channels :].reshape(2 * tokens_here, channels)
    d_padded = jnp.pad(lower_taps, ((0, 2), (0, 0))) + jnp.pad(upper_taps, ((2, 0), (0, 0)))
    rim_rows = jnp.stack([d_padded[0], d_padded[-1]])
    arrived = with_halo(rim_rows, (("seq", 0),), 1)
    middle_rows = d_padded[1:-1]
    middle_rows = middle_rows.at[0].add(arrived[0]).at[-1].add(arrived[3])
    seq_grad = middle_rows.astype(jnp.bfloat16)[None]
    pairs = ((unfolded, d_pre), (onehot, d_pre), (normed, d_projected), (attend_all, upstream))
    shards = tuple((data_shard(left_rows, right_rows) for left_rows, right_rows in pairs))
    totals = lax.psum(shards, "seq")
    return (seq_grad, totals[0], totals[1], totals[2], totals[3])


def solution(mesh):
    in_specs = (
        P("dp", "seq", None),
        P("dp", "seq"),
        P("dp", None),
        P("dp", None),
        P("dp", None),
        P("dp", None),
        P("dp", "seq", None),
    )
    out_specs = (P("dp", "seq", None), P("dp", None), P("dp", None), P("dp", None), P("dp", None))
    return jax.shard_map(
        per_device, mesh=mesh, in_specs=in_specs, out_specs=out_specs, check_vma=False
    )
```

profile of v0, /device:TPU:32, one launch (start us, length us, event | category | flops | bytes accessed | tf_op | source)
XLA Modules:
  0.0 708.9 jit_solution(11521479414240118855)
XLA Ops:
  9.4 4.2 collective-permute-start.1
  13.7 1.9 collective-permute-start
  16.8 54.1 %all_gather.19 = bf16[512,768]{1,0:T(8,128)(2,1)S(1)} all-gather(bf16[16,768]{1,0:T(8,128)(2,1)} %param.14), channel_id=1, replica_groups=mesh['dp'=32,'seq'=8] {'dp'}, dimensions={0}, use_global_device_ids=true | all-gather | bytes 811008 | tf_op jit(solution)/shard_map/all_gather | solution.py:62
  71.8 5.4 all-gather.5.cloned.1.call-done
  77.2 3.9 fusion.35
  81.1 49.9 %all-gather.7.cloned.1.call-done = bf16[768,1536]{1,0:T(8,128)(2,1)} async-done(((bf16[24,1536]{1,0:T(8,128)(2,1)}), bf16[768,1536]{1,0:T(8,128)(2,1)}) %all-gather.7.cloned.1.call-update) | async-done | bytes 2359312 | tf_op jit(solution)/shard_map/all_gather | solution.py:63
  131.0 2.2 convolution_convert_fusion.2
  134.7 45.4 %all_gather.22 = bf16[512,768]{1,0:T(8,128)(2,1)S(1)} all-gather(bf16[16,768]{1,0:T(8,128)(2,1)S(1)} %copy-done.16), channel_id=1, replica_groups=mesh['dp'=32,'seq'=8] {'dp'}, dimensions={0}, use_global_device_ids=true | all-gather | bytes 811008 | tf_op jit(solution)/shard_map/all_gather | solution.py:64
  182.1 1.3 fusion.101
  183.7 1.3 fusion.100
  188.1 29.0 %all-gather.11.cloned.1.call-done = bf16[1024,512]{1,0:T(8,128)(2,1)} async-done(((bf16[128,512]{1,0:T(8,128)(2,1)}), bf16[1024,512]{1,0:T(8,128)(2,1)}) %all-gather.11.cloned.1.call-update) | async-done | bytes 1048592 | tf_op jit(solution)/shard_map/all_gather | solution.py:91
  217.1 1.3 multiply_reduce_fusion
  222.7 2.6 pad_maximum_fusion
  225.9 1.3 convolution_convert_fusion.6
  228.2 1.3 convolution_convert_fusion.3
  229.6 1.9 fusion.3
  231.5 1.9 fusion.2
  233.5 1.9 fusion.1
  235.4 1.9 fusion
  237.3 42.8 %reduce-scatter.6.cloned.1.call-done = f32[128,1024]{0,1:T(8,128)} async-done(((f32[1024,1024]{0,1:T(8,128)}), f32[128,1024]{0,1:T(8,128)}) %reduce-scatter.6.cloned.1.call-update) | async-done | bytes 524304 | tf_op jit(solution)/shard_map/reduce_scatter | solution.py:132
  280.1 1.8 convert_dynamic-update-slice_fusion
  282.0 2.0 fusion.31
  285.9 3.3 convolution_convert_fusion.1
  289.3 3.6 convolution_convert_fusion
  292.9 4.0 fusion.103
  297.3 2.2 collective-permute-start.2
  299.5 72.0 %reduce-scatter.14.cloned.1.call-done = bf16[16,768]{1,0:T(8,128)(2,1)} async-done(((bf16[512,768]{1,0:T(8,128)(2,1)}), bf16[16,768]{1,0:T(8,128)(2,1)}) %reduce-scatter.14.cloned.1.call-update) | async-done | bytes 24592 | tf_op jit(solution)/shard_map/reduce_scatter | solution.py:47
  371.5 5.4 collective-permute-start.3
  379.1 82.5 %reduce-scatter.10.cloned.1.call-done = bf16[16,768]{1,0:T(8,128)(2,1)} async-done(((bf16[512,768]{1,0:T(8,128)(2,1)}), bf16[16,768]{1,0:T(8,128)(2,1)}) %reduce-scatter.10.cloned.1.call-update) | async-done | bytes 24592 | tf_op jit(solution)/shard_map/reduce_scatter | solution.py:47
  461.6 94.2 %reduce-scatter.12.cloned.1.call-done = bf16[24,1536]{1,0:T(8,128)(2,1)} async-done(((bf16[768,1536]{1,0:T(8,128)(2,1)}), bf16[24,1536]{1,0:T(8,128)(2,1)}) %reduce-scatter.12.cloned.1.call-update) | async-done | bytes 73744 | tf_op jit(solution)/shard_map/reduce_scatter | solution.py:47
  555.9 104.3 %reduce-scatter.8.cloned.1.call-done = bf16[96,768]{1,0:T(8,128)(2,1)} async-done(((bf16[3072,768]{1,0:T(8,128)(2,1)}), bf16[96,768]{1,0:T(8,128)(2,1)}) %reduce-scatter.8.cloned.1.call-update) | async-done | bytes 147472 | tf_op jit(solution)/shard_map/reduce_scatter | solution.py:47
  660.1 42.2 %all-reduce.4 = (f32[96,768]{1,0:T(8,128)}, f32[16,768]{1,0:T(8,128)}, f32[24,1536]{1,0:T(8,128)}, f32[16,768]{1,0:T(8,128)}) all-reduce(bf16[96,768]{1,0:T(8,128)(2,1)} %reduce-scatter.8.cloned.1.call-done, bf16[16,768]{1,0:T(8,128)(2,1)} %reduce-scatter.10.cloned.1.call-done, ...), channel_id=1, replica_groups=mesh['dp'=32,'seq'=8] {'seq'}, use_global_device_ids=true, to_apply=%region_16.17 | all-reduce | flops 135168 | bytes 811008 | tf_op jit(solution)/shard_map/psum | solution.py:155
  (131 shorter events, 21.0 us)
Async XLA Ops:
  7.2 64.1 %copy-start.13 = (bf16[1,256,768]{2,1,0:T(8,128)(2,1)S(1)}, bf16[1,256,768]{2,1,0:T(8,128)(2,1)}, u32[]{:S(2)}) copy-start(bf16[1,256,768]{2,1,0:T(8,128)(2,1)} %param.11) | copy-start | bytes 1179652
  7.2 70.0 %all-gather.5.cloned.1.call-start = ((), (), s32[]{:S(2)}) async-start(), calls=%async_computation.5 | async-start | bytes 4866048 | tf_op jit(solution)/shard_map/all_gather | solution.py:61
  7.9 123.1 %all-gather.7.cloned.1.call-start = ((), (), s32[]{:S(2)}) async-start(), calls=%async_computation.6 | async-start | bytes 2433024 | tf_op jit(solution)/shard_map/all_gather | solution.py:63
  8.7 173.4 %all-gather.9.cloned.1.call-start = ((), (), s32[]{:S(2)}) async-start(), calls=%async_computation.7 | async-start | bytes 1179648 | tf_op jit(solution)/shard_map/all_gather | solution.py:90
  9.4 61.8 %collective-permute-start.1 = (bf16[1,768]{1,0:T(2,128)(2,1)S(1)}, bf16[1,768]{1,0:T(2,128)(2,1)S(1)}, u32[]{:S(2)}, u32[]{:S(2)}) collective-permute-start(bf16[1,768]{1,0:T(2,128)(2,1)S(1)} %get-tuple-element.52), channel_id=1, source_target_pairs={{1,0},{2,1},{3,2},{4,3},{5,4},{6,5},{7,6},{9,8},{10,9},{11,10},{12... | collective-permute-start | bytes 4616 | tf_op jit(solution)/shard_map/ppermute | solution.py:23
  13.7 57.6 %collective-permute-start = (bf16[1,768]{1,0:T(2,128)(2,1)S(1)}, bf16[1,768]{1,0:T(2,128)(2,1)S(1)}, u32[]{:S(2)}, u32[]{:S(2)}) collective-permute-start(bf16[1,768]{1,0:T(2,128)(2,1)S(1)} %get-tuple-element.53), channel_id=1, source_target_pairs={{0,1},{1,2},{2,3},{3,4},{4,5},{5,6},{6,7},{8,9},{9,10},{10,11},{11... | collective-permute-start | bytes 4616 | tf_op jit(solution)/shard_map/ppermute | solution.py:22
  16.8 54.5 %copy-start.9 = (pred[128,512]{0,1:T(32,128)(4,1)}, pred[128,512]{0,1:T(32,128)(4,1)S(1)}, u32[]{:S(2)}) copy-start(pred[128,512]{0,1:T(32,128)(4,1)S(1)} %broadcast_compare_fusion) | copy-start | bytes 196612
  81.1 53.6 %copy-start.16 = (bf16[16,768]{1,0:T(8,128)(2,1)S(1)}, bf16[16,768]{1,0:T(8,128)(2,1)}, u32[]{:S(2)}) copy-start(bf16[16,768]{1,0:T(8,128)(2,1)} %param.16) | copy-start | bytes 73732
  131.0 49.1 %copy-start.3 = (bf16[1,128,768]{2,1,0:T(8,128)(2,1)S(1)}, bf16[1,128,768]{2,1,0:T(8,128)(2,1)}, u32[]{:S(2)}) copy-start(bf16[1,128,768]{2,1,0:T(8,128)(2,1)} %param.17) | copy-start | bytes 589828
  133.3 52.2 %copy-start.2 = (bf16[128,1536]{1,0:T(8,128)(2,1)}, bf16[128,1536]{1,0:T(8,128)(2,1)S(1)}, u32[]{:S(2)}) copy-start(bf16[128,1536]{1,0:T(8,128)(2,1)S(1)} %convolution_convert_fusion.2) | copy-start | bytes 1179652
  134.1 83.0 %all-gather.11.cloned.1.call-start = ((), (), s32[]{:S(2)}) async-start(), calls=%async_computation.8 | async-start | bytes 1179648 | tf_op jit(solution)/shard_map/all_gather | solution.py:91
  134.7 145.5 %reduce-scatter.6.cloned.1.call-start = ((), (), s32[]{:S(2)}) async-start(), calls=%async_computation.9 | async-start | bytes 4718592 | tf_op jit(solution)/shard_map/reduce_scatter | solution.py:132
  180.5 37.9 %copy-start.11 = (bf16[128,512]{1,0:T(8,128)(2,1)}, bf16[128,512]{1,0:T(8,128)(2,1)S(1)}, u32[]{:S(2)}) copy-start(bf16[128,512]{1,0:T(8,128)(2,1)S(1)} %convolution_convert_fusion.5) | copy-start | bytes 393220
  182.1 3.1 copy-start.1
  183.6 34.8 %copy-start.21 = (f32[128]{0:T(128)}, f32[128]{0:T(128)S(1)}, u32[]{:S(2)}) copy-start(f32[128]{0:T(128)S(1)} %fusion.30) | copy-start | bytes 1540
  185.2 33.3 %copy-start.23 = (f32[128]{0:T(128)}, f32[128]{0:T(128)S(1)}, u32[]{:S(2)}) copy-start(f32[128]{0:T(128)S(1)} %fusion.28) | copy-start | bytes 1540
  187.3 31.5 %copy-start.18 = (f32[128]{0:T(128)}, f32[128]{0:T(128)S(1)}, u32[]{:S(2)}) copy-start(f32[128]{0:T(128)S(1)} %get-tuple-element.55) | copy-start | bytes 1540
  220.0 1.7 copy-start.6
  220.0 2.6 copy-start.5
  221.1 1.6 copy-start.7
  225.2 2.0 copy-start.24
  225.2 2.3 copy-start.26
  225.2 146.3 %reduce-scatter.14.cloned.1.call-start = ((), (), s32[]{:S(2)}) async-start(), calls=%async_computation.13 | async-start | bytes 811008 | tf_op jit(solution)/shard_map/reduce_scatter | solution.py:47
  228.2 53.8 %copy-start = (bf16[768,1536]{1,0:T(8,128)(2,1)S(1)}, bf16[768,1536]{1,0:T(8,128)(2,1)}, u32[]{:S(2)}) copy-start(bf16[768,1536]{1,0:T(8,128)(2,1)} %all-gather.7.cloned.1.call-done) | copy-start | bytes 7077892
  229.5 232.1 %reduce-scatter.10.cloned.1.call-start = ((), (), s32[]{:S(2)}) async-start(), calls=%async_computation.11 | async-start | bytes 811008 | tf_op jit(solution)/shard_map/reduce_scatter | solution.py:47
  280.1 3.9 copy-start.4
  282.0 2.4 copy-start.10
  285.7 270.2 %reduce-scatter.12.cloned.1.call-start = ((), (), s32[]{:S(2)}) async-start(), calls=%async_computation.12 | async-start | bytes 2433024 | tf_op jit(solution)/shard_map/reduce_scatter | solution.py:47
  289.2 370.9 %reduce-scatter.8.cloned.1.call-start = ((), (), s32[]{:S(2)}) async-start(), calls=%async_computation.10 | async-start | bytes 4866048 | tf_op jit(solution)/shard_map/reduce_scatter | solution.py:47
  297.3 74.2 %collective-permute-start.2 = (f32[1,768]{1,0:T(1,128)S(1)}, f32[1,768]{1,0:T(1,128)S(1)}, u32[]{:S(2)}, u32[]{:S(2)}) collective-permute-start(f32[1,768]{1,0:T(1,128)S(1)} %fusion.86), channel_id=1, source_target_pairs={{0,1},{1,2},{2,3},{3,4},{4,5},{5,6},{6,7},{8,9},{9,10},{10,11},{11... | collective-permute-start | bytes 9224 | tf_op jit(solution)/shard_map/ppermute | solution.py:22
  371.5 288.6 %copy-start.17 = (bf16[16,768]{1,0:T(8,128)(2,1)S(1)}, bf16[16,768]{1,0:T(8,128)(2,1)}, u32[]{:S(2)}) copy-start(bf16[16,768]{1,0:T(8,128)(2,1)} %reduce-scatter.14.cloned.1.call-done) | copy-start | bytes 73732
  371.5 6.7 collective-permute-start.3
  (12 other events, 13.9 us)
Sparse Core Ops, SparseCore 0:
  10.6 66.6 all-gather.4
  79.8 51.2 all-gather.6
  134.2 39.8 all-gather.8
  176.3 40.7 all-gather.10
  225.4 54.7 reduce-scatter.5
  283.7 87.7 reduce-scatter.13
  375.3 86.3 reduce-scatter.9
  465.5 90.3 reduce-scatter.11
  560.4 99.6 reduce-scatter.7
where the time goes:
time: 710 us; the launch traced here: 709 us
  waiting for transfers between devices  483 us (68%)
  blocking collectives  142 us (20%)
  matrix products  39.3 us (6%)
  between operations  14.5 us (2%)
  starting transfers between devices  14.3 us (2%)
  other arithmetic  9.5 us (1%)
    reduce_scatter x4, waiting for transfers between devices, data_shard(): lax.psum_scatter(row_product(left_rows, right_rows).astype(jnp.bfloat16),...  353 us
    all_gather x1, blocking collectives, per_device(): lax.all_gather(dna_weight, 'dp', axis=0, tiled=True)  54.1 us
    all_gather x1, waiting for transfers between devices, per_device(): lax.all_gather(qkv_weight, 'dp', axis=0, tiled=True)  49.9 us
    all_gather x1, blocking collectives, per_device(): lax.all_gather(out_weight, 'dp', axis=0, tiled=True)  45.4 us
    reduce_scatter x1, waiting for transfers between devices, per_device(): lax.psum_scatter(jnp.concatenate([key_grad, value_grad], axis=1), 'seq',...  42.8 us
    psum x1, blocking collectives, per_device(): totals = lax.psum(shards, 'seq')  42.2 us
    all_gather x1, waiting for transfers between devices, per_device(): lax.all_gather(local_values, 'seq', axis=0, tiled=True)  29 us
  transfers between devices with their start and end apart: 13, of which 9 were waited for; matrix products, arithmetic and copies ran while one was open for 6% of the time, Pallas kernels for 0%

commit v1 on v0

v1 whole, which is shorter than its diff:
```python
import math

import jax
import jax.numpy as jnp
from jax import lax
from jax.experimental import pallas as pl
from jax.experimental.pallas import tpu as pltpu
from jax.sharding import PartitionSpec as P

H = 4
BIN = 128
BF16 = jnp.bfloat16
F32 = jnp.float32
MESH = pl.DeviceIdType.MESH
epsilon = 1e-06

SIZES = {"zh": 4, "y": 4, "c": 2, "zl": 2, "x": 4}
PEERS = [(a, k) for a in ("zh", "y", "x") for k in (1, 2, 3)] + [("zl", 1), ("c", 1)]


def here():
    dp = lax.axis_index("dp")
    sq = lax.axis_index("seq")
    return {"zh": dp // 8, "y": lax.rem(dp // 2, 4), "c": lax.rem(dp, 2), "zl": sq // 4, "x": lax.rem(sq, 4)}


def moved(at, **steps):
    to = dict(at)
    for axis, step in steps.items():
        to[axis] = lax.rem(at[axis] + step, SIZES[axis])
    return to


def device(at):
    return (at["zh"] * 8 + at["y"] * 2 + at["c"], at["zl"] * 4 + at["x"])


def meet(devices):
    barrier = pltpu.get_barrier_semaphore()
    for one in devices:
        pl.semaphore_signal(barrier, inc=1, device_id=one, device_id_type=MESH)
    pl.semaphore_wait(barrier, len(devices))


class Sender:
    def __init__(self, send_sems, recv_sems):
        self.send_sems, self.recv_sems, self.used, self.copies = send_sems, recv_sems, 0, []

    def __call__(self, src, dst, to):
        copy = pltpu.make_async_remote_copy(
            src_ref=src,
            dst_ref=dst,
            send_sem=self.send_sems.at[self.used],
            recv_sem=self.recv_sems.at[self.used],
            device_id=to,
            device_id_type=MESH,
        )
        copy.start()
        self.used += 1
        self.copies.append(copy)
        return copy

    def finish(self):
        for copy in self.copies:
            copy.wait_send()


def arrive(copies):
    for copy in copies:
        copy.wait_recv()


def rows16(index, base=0):
    return pl.ds(pl.multiple_of(index * 16 + base, 16), 16)


def half_columns(index):
    return pl.ds(pl.multiple_of(index * 384, 128), 384)


def gather_kernel(
    conv_s, do_s, qkv_s, rows_in, conv_g, do_g, qkv_g, before, after, send_sems, recv_sems, local_sems
):
    at = here()
    zh, y, c, zl, x = (at[a] for a in ("zh", "y", "c", "zl", "x"))
    sq = lax.axis_index("seq")
    dp = lax.axis_index("dp")
    behind, ahead = (dp, lax.rem(sq + 7, 8)), (dp, lax.rem(sq + 1, 8))
    meet([device(moved(at, **{a: k})) for a, k in PEERS] + [behind, ahead])
    send = Sender(send_sems, recv_sems)
    quarter = rows16(x)
    part, part_rows = x // 2, rows16(lax.rem(x, 2))
    half, other_half = half_columns(zl), half_columns(1 - zl)
    tail = pl.ds(64, 32)

    locals_ = [
        pltpu.make_async_copy(conv_s.at[quarter], conv_g.at[zh, y, c, quarter], local_sems.at[0]),
        pltpu.make_async_copy(conv_s.at[tail], conv_g.at[zh, y, c, tail], local_sems.at[1]),
        pltpu.make_async_copy(do_s, do_g.at[zh, y, c], local_sems.at[2]),
        pltpu.make_async_copy(
            qkv_s.at[part, part_rows, half], qkv_g.at[part, zh, y, c, part_rows, half], local_sems.at[3]
        ),
    ]
    for copy in locals_:
        copy.start()
    a1, b1, c1, a2, b2, c2, a3, c3 = ([] for _ in range(8))
    for k in (1, 2, 3):
        to = device(moved(at, zh=k))
        a1.append(send(conv_s.at[quarter], conv_g.at[zh, y, c, quarter], to))
    for k in (1, 2, 3):
        to = device(moved(at, zh=k))
        c1.append(
            send(qkv_s.at[part, part_rows, half], qkv_g.at[part, zh, y, c, part_rows, half], to)
        )
    for k in (1, 2, 3):
        to = device(moved(at, zh=k))
        b1.append(send(conv_s.at[tail], conv_g.at[zh, y, c, tail], to))
        b1.append(send(do_s, do_g.at[zh, y, c], to))
    halo = [
        send(rows_in.at[pl.ds(240, 16)], before, ahead),
        send(rows_in.at[pl.ds(0, 16)], after, behind),
    ]
    for copy in locals_:
        copy.wait()
    arrive(a1)
    for k in (1, 2, 3):
        block = conv_g.at[:, y, c, quarter]
        a2.append(send(block, block, device(moved(at, y=k))))
    arrive(c1)
    for k in (1, 2, 3):
        block = qkv_g.at[part, :, y, c, part_rows, half]
        c2.append(send(block, block, device(moved(at, y=k))))
    arrive(b1)
    for k in (1, 2, 3):
        to = device(moved(at, y=k))
        b2.append(
            (
                send(conv_g.at[:, y, c, tail], conv_g.at[:, y, c, tail], to),
                send(do_g.at[:, y, c], do_g.at[:, y, c], to),
            )
        )
    sibling = device(moved(at, c=1))
    core = []

    def pass_on(block):
        core.append(send(block, block, sibling))

    arrive(a2)
    for k in (1, 2, 3):
        block = conv_g.at[:, :, c, quarter]
        a3.append(send(block, block, device(moved(at, x=k))))
    arrive(c2)
    for k in (1, 2, 3):
        block = qkv_g.at[part, :, :, c, part_rows, half]
        c3.append(send(block, block, device(moved(at, x=k))))
    pass_on(conv_g.at[:, :, c, quarter])
    pass_on(conv_g.at[:, y, c, tail])
    pass_on(do_g.at[:, y, c])
    arrive(c3)
    block = qkv_g.at[:, :, :, c, :, half]
    c4 = send(block, block, device(moved(at, zl=1)))
    pass_on(block)
    for k in (1, 2, 3):
        arrive(b2[k - 1])
        from_y = lax.rem(y + 4 - k, 4)
        pass_on(conv_g.at[:, from_y, c, tail])
        pass_on(do_g.at[:, from_y, c])
    for k in (1, 2, 3):
        arrive([a3[k - 1]])
        pass_on(conv_g.at[:, :, c, rows16(lax.rem(x + 4 - k, 4))])
    arrive([c4])
    pass_on(qkv_g.at[:, :, :, c, :, other_half])
    arrive(halo)
    arrive(core)
    send.finish()


def gather_weights(conv_s, do_s, qkv_s, rows_in):
    any_spec = pl.BlockSpec(memory_space=pl.ANY)
    return pl.pallas_call(
        gather_kernel,
        name="gather_weights",
        out_shape=(
            jax.ShapeDtypeStruct((4, 4, 2, 96, 768), BF16),
            jax.ShapeDtypeStruct((4, 4, 2, 32, 768), BF16),
            jax.ShapeDtypeStruct((2, 4, 4, 2, 32, 768), BF16),
            jax.ShapeDtypeStruct((16, 768), BF16),
            jax.ShapeDtypeStruct((16, 768), BF16),
        ),
        in_specs=[any_spec] * 4,
        out_specs=(any_spec,) * 5,
        scratch_shapes=[
            pltpu.SemaphoreType.DMA((48,)),
            pltpu.SemaphoreType.DMA((48,)),
            pltpu.SemaphoreType.DMA((4,)),
        ],
        compiler_params=pltpu.CompilerParams(collective_id=1, has_side_effects=True),
    )(conv_s, do_s, qkv_s, rows_in)


def right_dot(left, right):
    return lax.dot_general(left, right, (((1,), (1,)), ((), ())), preferred_element_type=F32)


def row_dot(left, right):
    return lax.dot_general(left, right, (((0,), (0,)), ((), ())), preferred_element_type=F32)


def attention_kernel(
    mine, back, back_kv, got, got_kv, outgo, outgo_kv, d_kv, send_sems, recv_sems, local_sem
):
    at = here()
    x = at["x"]
    partners = [moved(at, x=k) for k in (1, 2, 3)]
    across = [moved(at, x=k, zl=1) for k in range(4)]
    meet([device(p) for p in partners] + [device(p) for p in across])
    send = Sender(send_sems, recv_sems)
    own = pltpu.make_async_copy(mine.at[x], got.at[x], local_sem.at[0])
    own.start()
    arriving = []
    for p in across:
        arriving.append(send(mine.at[p["x"], :, pl.ds(128, 256)], got_kv.at[x], device(p)))
    for p in partners:
        arriving.append(send(mine.at[p["x"]], got.at[x], device(p)))
    own.wait()
    arrive(arriving)

    scaling = 1.0 / math.sqrt(128)
    keys = jnp.concatenate([got[:, :, 128:256].reshape(512, 128), got_kv[:, :, :128].reshape(512, 128)], axis=0)
    values = jnp.concatenate([got[:, :, 256:384].reshape(512, 128), got_kv[:, :, 128:].reshape(512, 128)], axis=0)
    d_kv[...] = jnp.zeros_like(d_kv)

    def block(index, carry):
        queries = got[index, :, 0:128]
        upward = got[index, :, 384:512]
        scores = right_dot(queries, keys) * scaling
        powers = jnp.exp(scores - jnp.max(scores, axis=1, keepdims=True))
        probs = powers / jnp.sum(powers, axis=1, keepdims=True)
        probs_low = probs.astype(BF16)
        outgo[index, :, 0:128] = jnp.dot(probs_low, values, preferred_element_type=F32).astype(BF16)
        d_probs = right_dot(upward, values)
        inner = jnp.sum(probs * d_probs, axis=1, keepdims=True)
        d_scores = (probs * (d_probs - inner) * scaling).astype(BF16)
        outgo[index, :, 128:256] = jnp.dot(d_scores, keys, preferred_element_type=F32).astype(BF16)
        d_kv[:, 0:128] += row_dot(d_scores, queries)
        d_kv[:, 128:256] += row_dot(probs_low, upward)
        return carry

    lax.fori_loop(0, 4, block, 0)
    outgo[:, :, 256:512] = d_kv[0:512].astype(BF16).reshape(4, 128, 256)
    outgo_kv[...] = d_kv[512:1024].astype(BF16).reshape(4, 128, 256)
    own = pltpu.make_async_copy(outgo.at[x], back.at[x], local_sem.at[0])
    own.start()
    arriving = []
    for p in across:
        arriving.append(send(outgo_kv.at[p["x"]], back_kv.at[x], device(p)))
    for p in partners:
        arriving.append(send(outgo.at[p["x"]], back.at[x], device(p)))
    own.wait()
    arrive(arriving)
    send.finish()


def attention(mine):
    vmem = pl.BlockSpec(memory_space=pltpu.VMEM)
    return pl.pallas_call(
        attention_kernel,
        name="attention",
        out_shape=(
            jax.ShapeDtypeStruct((4, 128, 512), BF16),
            jax.ShapeDtypeStruct((4, 128, 256), BF16),
        ),
        in_specs=[vmem],
        out_specs=(vmem, vmem),
        scratch_shapes=[
            pltpu.VMEM((4, 128, 512), BF16),
            pltpu.VMEM((4, 128, 256), BF16),
            pltpu.VMEM((4, 128, 512), BF16),
            pltpu.VMEM((4, 128, 256), BF16),
            pltpu.VMEM((1024, 256), F32),
            pltpu.SemaphoreType.DMA((16,)),
            pltpu.SemaphoreType.DMA((16,)),
            pltpu.SemaphoreType.DMA((1,)),
        ],
        compiler_params=pltpu.CompilerParams(
            collective_id=2, has_side_effects=True, vmem_limit_bytes=40 * 2**20
        ),
    )(mine)


def reduce_kernel(
    conv_p, do_p, qkv_p,
    conv_o, dna_o, out_o, qkv_o,
    conv_r, do_r, qkv_r, conv_v, do_v, qkv_v,
    ra1, ra2, ra3, ra4, sa1, sa2, sa3,
    rb1, rb2, rb3, rb4, sb1, sb2, sb3,
    rc1, rc2, rc3, rc4, sc1, sc2, sc3,
    final,
    send_sems, recv_sems, local_sems,
):
    at = here()
    zh, y, c, zl, x = (at[a] for a in ("zh", "y", "c", "zl", "x"))
    meet([device(moved(at, **{a: k})) for a, k in PEERS])
    send = Sender(send_sems, recv_sems)
    sibling = device(moved(at, c=1))
    near = device(moved(at, zl=1))
    half, other_half = half_columns(zl), half_columns(1 - zl)
    tail = pl.ds(64, 32)
    locals_ = []

    def local(src, dst):
        copy = pltpu.make_async_copy(src, dst, local_sems.at[len(locals_)])
        copy.start()
        locals_.append(copy)

    local(conv_p.at[:, :, c], conv_v)
    local(qkv_p.at[:, :, :, c], qkv_v)
    local(do_p.at[:, :, c], do_v)

    order = [(1, 2, 3, 0)[i] for i in range(4)]
    xs = {k: lax.rem(x + k, 4) for k in order}
    ys = {k: lax.rem(y + k, 4) for k in order}
    zs = {k: lax.rem(zh + k, 4) for k in order}
    core_a, core_b, core_c = {}, {}, {}
    for k in order:
        core_a[k] = [send(conv_p.at[:, :, 1 - c, rows16(xs[k])], conv_r.at[:, :, rows16(xs[k])], sibling)]
        core_b[k] = [
            send(conv_p.at[:, ys[k], 1 - c, tail], conv_r.at[:, ys[k], tail], sibling),
            send(do_p.at[:, ys[k], 1 - c], do_r.at[:, ys[k]], sibling),
        ]
        if k == 1:
            core_c[1] = [send(qkv_p.at[:, :, :, 1 - c, :, other_half], qkv_r.at[:, :, :, :, other_half], sibling)]
    core_c[0] = [send(qkv_p.at[:, :, :, 1 - c, :, half], qkv_r.at[:, :, :, :, half], sibling)]
    for copy in locals_:
        copy.wait()

    def loop(n, body):
        def step(i, carry):
            body(i)
            return carry

        lax.fori_loop(0, n, step, 0)

    def add(target, *terms):
        total = terms[0].astype(F32)
        for term in terms[1:]:
            total += term.astype(F32)
        return total.astype(target.dtype)

    a1, b1, c1 = {}, {}, {}
    for k in order:
        arrive(core_a[k])
        rows = rows16(xs[k])

        def sum_a(i, rows=rows):
            conv_v[i, :, rows] = add(conv_v, conv_v[i, :, rows], conv_r[i, :, rows])

        loop(4, sum_a)
        if k:
            a1[k] = send(conv_v.at[:, :, rows], ra1.at[k - 1], device(moved(at, x=k)))
        arrive(core_b[k])
        ky = ys[k]

        def sum_b(i, ky=ky):
            conv_v[i, ky, 64:96] = add(conv_v, conv_v[i, ky, 64:96], conv_r[i, ky, 64:96])
            do_v[i, ky] = add(do_v, do_v[i, ky], do_r[i, ky])

        loop(4, sum_b)
        if k:
            to = device(moved(at, y=k))
            b1[k] = [
                send(conv_v.at[:, ky, tail], rb1.at[k - 1, :, pl.ds(0, 32)], to),
                send(do_v.at[:, ky], rb1.at[k - 1, :, pl.ds(32, 32)], to),
            ]
        if k in (1, 0):
            arrive(core_c[k])
            columns = other_half if k else half

            def sum_c(i, columns=columns):
                for part in range(2):
                    qkv_v[part, i, :, :, columns] = add(
                        qkv_v, qkv_v[part, i, :, :, columns], qkv_r[part, i, :, :, columns]
                    )

            loop(4, sum_c)
            if k:
                c1[1] = send(qkv_v.at[:, :, :, :, columns], rc1, near)

    arrive(a1.values())

    def first_a(i):
        sa1[i] = add(sa1, conv_v[i, :, rows16(x)], ra1[0, i], ra1[1, i], ra1[2, i])

    loop(4, first_a)
    a2 = [send(sa1.at[:, ys[k]], ra2.at[k - 1], device(moved(at, y=k))) for k in (1, 2, 3)]
    for k in (1, 2, 3):
        arrive(b1[k])

    def first_b(i):
        sb1[i, 0:32] = add(sb1, conv_v[i, y, 64:96], rb1[0, i, 0:32], rb1[1, i, 0:32], rb1[2, i, 0:32])
        sb1[i, 32:64] = add(sb1, do_v[i, y], rb1[0, i, 32:64], rb1[1, i, 32:64], rb1[2, i, 32:64])

    loop(4, first_b)
    b2 = [send(sb1.at[:, rows16(xs[k])], rb2.at[k - 1], device(moved(at, x=k))) for k in (1, 2, 3)]
    arrive(c1.values())

    def first_c(i):
        for part in range(2):
            sc1[part, i] = add(sc1, qkv_v[part, i, :, :, half], rc1[part, i])

    loop(4, first_c)
    c2 = [
        send(
            sc1.at[xs[k] // 2, :, :, rows16(lax.rem(xs[k], 2))],
            rc2.at[k - 1],
            device(moved(at, x=k)),
        )
        for k in (1, 2, 3)
    ]

    arrive(a2)

    def second_a(i):
        sa2[i] = add(sa2, sa1[i, y], ra2[0, i], ra2[1, i], ra2[2, i])

    loop(4, second_a)
    a3 = [send(sa2.at[zs[k]], ra3.at[k - 1], device(moved(at, zh=k))) for k in (1, 2, 3)]
    arrive(b2)

    def second_b(i):
        sb2[i] = add(sb2, sb1[i, rows16(x)], rb2[0, i], rb2[1, i], rb2[2, i])

    loop(4, second_b)
    b3 = [send(sb2.at[zs[k]], rb3.at[k - 1], device(moved(at, zh=k))) for k in (1, 2, 3)]
    arrive(c2)

    def second_c(i):
        own = sc1[x // 2, i, :, rows16(lax.rem(x, 2))]
        sc2[i] = add(sc2, own, rc2[0, i], rc2[1, i], rc2[2, i])

    loop(4, second_c)
    c3 = [send(sc2.at[:, ys[k]], rc3.at[k - 1], device(moved(at, y=k))) for k in (1, 2, 3)]

    arrive(a3)
    sa3[...] = add(sa3, sa2[zh], ra3[0], ra3[1], ra3[2])
    a4 = send(sa3, ra4, near)
    arrive(b3)
    sb3[...] = add(sb3, sb2[zh], rb3[0], rb3[1], rb3[2])
    b4 = send(sb3, rb4, near)
    arrive(c3)

    def third_c(i):
        sc3[i] = add(sc3, sc2[i, y], rc3[0, i], rc3[1, i], rc3[2, i])

    loop(4, third_c)
    c4 = [send(sc3.at[zs[k]], rc4.at[k - 1], device(moved(at, zh=k))) for k in (1, 2, 3)]

    arrive([a4])
    final[x, 0] = add(final, sa3[...], ra4[...])
    arrive([b4])
    final[x, 1] = add(final, sb3[...], rb4[...])
    share = [
        send(final.at[x, pl.ds(0, 2)], final.at[x, pl.ds(0, 2)], device(moved(at, x=k))) for k in (1, 2, 3)
    ]
    arrive(c4)
    final[x, 2, :, half] = add(final, sc3[zh], rc4[0], rc4[1], rc4[2])
    block = final.at[x, 2, :, half]
    arrive([send(block, block, near)])
    share += [send(final.at[x, 2], final.at[x, 2], device(moved(at, x=k))) for k in (1, 2, 3)]
    arrive(share)
    for q in range(4):
        conv_o[16 * q : 16 * q + 16] = final[q, 0].astype(F32)
    conv_o[64:80] = final[0, 1].astype(F32)
    conv_o[80:96] = final[1, 1].astype(F32)
    dna_o[...] = final[2, 1].astype(F32)
    out_o[...] = final[3, 1].astype(F32)
    qkv_o[0:16, 0:768] = final[0, 2].astype(F32)
    qkv_o[16:24, 0:768] = final[1, 2].astype(F32)[0:8]
    qkv_o[0:16, 768:1536] = final[2, 2].astype(F32)
    qkv_o[16:24, 768:1536] = final[3, 2].astype(F32)[0:8]
    send.finish()


def reduce_gradients(conv_p, do_p, qkv_p):
    any_spec = pl.BlockSpec(memory_space=pl.ANY)
    vmem = pl.BlockSpec(memory_space=pltpu.VMEM)
    shapes = [
        (4, 4, 96, 768), (4, 4, 32, 768), (2, 4, 4, 32, 768), (4, 4, 96, 768), (4, 4, 32, 768), (2, 4, 4, 32, 768),
        (3, 4, 4, 16, 768), (3, 4, 16, 768), (3, 16, 768), (16, 768), (4, 4, 16, 768), (4, 16, 768), (16, 768),
        (3, 4, 64, 768), (3, 4, 16, 768), (3, 16, 768), (16, 768), (4, 64, 768), (4, 16, 768), (16, 768),
        (2, 4, 4, 32, 384), (3, 4, 4, 16, 384), (3, 4, 16, 384), (3, 16, 384),
        (2, 4, 4, 32, 384), (4, 4, 16, 384), (4, 16, 384),
        (4, 3, 16, 768),
    ]
    return pl.pallas_call(
        reduce_kernel,
        name="reduce_gradients",
        out_shape=(
            jax.ShapeDtypeStruct((96, 768), F32),
            jax.ShapeDtypeStruct((16, 768), F32),
            jax.ShapeDtypeStruct((16, 768), F32),
            jax.ShapeDtypeStruct((24, 1536), F32),
        ),
        in_specs=[any_spec] * 3,
        out_specs=(vmem,) * 4,
        scratch_shapes=[pltpu.VMEM(shape, BF16) for shape in shapes]
        + [pltpu.SemaphoreType.DMA((64,)), pltpu.SemaphoreType.DMA((64,)), pltpu.SemaphoreType.DMA((3,))],
        compiler_params=pltpu.CompilerParams(
            collective_id=3, has_side_effects=True, vmem_limit_bytes=48 * 2**20
        ),
    )(conv_p, do_p, qkv_p)


def swap_rims(rim_rows):
    peers = lax.axis_size("seq")
    up = [(i, (i + 1) % peers) for i in range(peers - 1)]
    down = [(j, i) for i, j in up]
    return lax.ppermute(rim_rows[1:], "seq", up), lax.ppermute(rim_rows[:1], "seq", down)


def unfold_rows(padded, length, channels):
    first_pair = padded[: 2 * length].reshape(length, 2 * channels)
    second_pair = padded[2:].reshape(length, 2 * channels)
    return jnp.concatenate([first_pair, second_pair], axis=1)


def spread(columns):
    parts = columns.reshape(columns.shape[0], 32, 24)
    return jnp.pad(parts, ((0, 0), (0, 0), (0, 8))).reshape(columns.shape[0], 1024)


def gathered_in(columns):
    return columns.reshape(columns.shape[0], 32, 32)[:, :, :24].reshape(columns.shape[0], 768)


def per_device(seq_in, bases, conv_weight, dna_weight, qkv_weight, out_weight, cotangent):
    rows_in = seq_in[0]
    upstream = cotangent[0]
    tokens_here = upstream.shape[0]
    channels = rows_in.shape[1]
    place = lax.axis_index("seq")
    qkv_parts = jnp.pad(
        jnp.stack([qkv_weight[:, :768], qkv_weight[:, 768:]]), ((0, 0), (0, 8), (0, 0))
    )
    conv_g, do_g, qkv_g, before, after = gather_weights(
        conv_weight, jnp.concatenate([dna_weight, out_weight], axis=0), qkv_parts, rows_in
    )
    conv_full = conv_g.reshape(3072, 768)
    do_full = do_g.reshape(32, 2, 16, 768)
    dna_full = do_full[:, 0].reshape(512, 768)
    out_full = do_full[:, 1].reshape(512, 768)
    qkv_full = qkv_g.reshape(2, 1024, 768)

    first = jnp.where(place > 0, before[15:16], jnp.zeros_like(before[15:16]))
    last = jnp.where(place < 7, after[0:1], jnp.zeros_like(after[0:1]))
    padded = jnp.concatenate([first, rows_in, last], axis=0)
    unfolded = unfold_rows(padded, tokens_here, channels)
    letters = bases[0].reshape(tokens_here, BIN, 1)
    onehot = (
        (letters == jnp.arange(4, dtype=jnp.int32))
        .astype(BF16)
        .reshape(tokens_here, 4 * BIN)
    )
    pre_act = jnp.dot(unfolded, conv_full, preferred_element_type=F32) + jnp.dot(
        onehot, dna_full, preferred_element_type=F32
    )
    feature = jax.nn.gelu(pre_act).astype(BF16)
    feat_wide = feature.astype(F32)
    inverse = lax.rsqrt(jnp.mean(feat_wide * feat_wide, axis=1, keepdims=True) + epsilon)
    unit_rows = feat_wide * inverse
    normed = unit_rows.astype(BF16)
    normed_wide = spread(normed)
    projected = jnp.concatenate(
        [jnp.dot(normed_wide, qkv_full[i], preferred_element_type=F32).astype(BF16) for i in range(2)], axis=1
    )
    d_attend = right_dot(upstream, out_full).astype(BF16)
    mine = (
        jnp.concatenate([projected, d_attend], axis=1)
        .reshape(tokens_here, 4, H, 128)
        .transpose(2, 0, 1, 3)
        .reshape(H, tokens_here, 512)
    )
    back, back_kv = attention(mine)
    attend_all = back[:, :, :128].transpose(1, 0, 2).reshape(tokens_here, 512)
    d_queries = back[:, :, 128:256].transpose(1, 0, 2).reshape(tokens_here, 512)
    d_keys_values = (
        (back[:, :, 256:].astype(F32) + back_kv.astype(F32))
        .astype(BF16)
        .reshape(H, tokens_here, 2, 128)
        .transpose(1, 2, 0, 3)
        .reshape(tokens_here, 1024)
    )
    d_projected = jnp.concatenate([d_queries, d_keys_values], axis=1)
    d_normed = gathered_in(
        right_dot(d_projected[:, :768], qkv_full[0]) + right_dot(d_projected[:, 768:], qkv_full[1])
    )
    d_feature = upstream.astype(F32) + inverse * (
        d_normed - unit_rows * jnp.mean(d_normed * unit_rows, axis=1, keepdims=True)
    )
    d_pre = jax.vjp(jax.nn.gelu, pre_act)[1](d_feature)[0].astype(BF16)
    d_unfolded = right_dot(d_pre, conv_full)
    lower_taps = d_unfolded[:, : 2 * channels].reshape(2 * tokens_here, channels)
    upper_taps = d_unfolded[:, 2 * channels :].reshape(2 * tokens_here, channels)
    d_padded = jnp.pad(lower_taps, ((0, 2), (0, 0))) + jnp.pad(upper_taps, ((2, 0), (0, 0)))
    from_before, from_after = swap_rims(jnp.stack([d_padded[0], d_padded[-1]]))
    middle_rows = d_padded[1:-1]
    middle_rows = middle_rows.at[0].add(from_before[0]).at[-1].add(from_after[0])
    seq_grad = middle_rows.astype(BF16)[None]

    conv_p = row_dot(unfolded, d_pre).astype(BF16).reshape(4, 4, 2, 96, 768)
    dna_p = row_dot(onehot, d_pre).astype(BF16).reshape(4, 4, 2, 16, 768)
    out_p = row_dot(attend_all, upstream).astype(BF16).reshape(4, 4, 2, 16, 768)
    do_p = jnp.concatenate([dna_p, out_p], axis=3)
    qkv_p = jnp.stack(
        [row_dot(normed_wide, d_projected[:, 768 * i : 768 * i + 768]).astype(BF16) for i in range(2)]
    ).reshape(2, 4, 4, 2, 32, 768)
    conv_grad, dna_grad, out_grad, qkv_grad = reduce_gradients(conv_p, do_p, qkv_p)
    return (seq_grad, conv_grad, dna_grad, qkv_grad, out_grad)


def solution(mesh):
    in_specs = (
        P("dp", "seq", None),
        P("dp", "seq"),
        P("dp", None),
        P("dp", None),
        P("dp", None),
        P("dp", None),
        P("dp", "seq", None),
    )
    out_specs = (P("dp", "seq", None), P("dp", None), P("dp", None), P("dp", None), P("dp", None))
    return jax.shard_map(
        per_device, mesh=mesh, in_specs=in_specs, out_specs=out_specs, check_vma=False
    )
```

time: 710 us -> 210 us (0.30)
  waiting for transfers between devices: 483 us -> 0.01 us
  Pallas kernels: 0 us -> 157 us
  blocking collectives: 142 us -> 0 us
  matrix products: 39.3 us -> 17.1 us
  between operations: 14.5 us -> 1.25 us
  local copies, waits for them, and re-layouts: 6.3 us -> 18.4 us
    reduce_scatter x5 -> x0, waiting for transfers between devices: 396 us -> none  [the longest x4 353 us: data_shard(): lax.psum_scatter(row_product(left_rows, right_rows).astype(jnp.bfloat16),...]
    pallas_call x0 -> x3, Pallas kernels: none -> 157 us  [the longest x1 68.2 us: gather_weights(): pl.pallas_call(gather_kernel, name='gather_weights', out_shape=(jax.Shape...]
    all_gather x2 -> x0, blocking collectives: 99.5 us -> none  [the longest x1 54.1 us: per_device(): lax.all_gather(dna_weight, 'dp', axis=0, tiled=True)]
    all_gather x4 -> x0, waiting for transfers between devices: 84.3 us -> none  [the longest x1 49.9 us: per_device(): lax.all_gather(qkv_weight, 'dp', axis=0, tiled=True)]
    psum x1 -> x0, blocking collectives: 42.2 us -> none  [per_device(): totals = lax.psum(shards, 'seq')]
    dot_general x28 -> x13, matrix products: 39.3 us -> 17.1 us  [the longest x5 7.71 us: row_dot(): lax.dot_general(left, right, (((0,), (0,)), ((), ())), preferred_element_...]
  transfers between devices with their start and end apart: 13 -> 2, of which waited for: 9 -> 0; matrix products, arithmetic and copies ran while one was open for 6% -> 5% of each run, Pallas kernels for 0% -> 29%
where the time goes in v1:
time: 210 us; the launch traced here: 208 us
  Pallas kernels  157 us (75%)
  local copies, waits for them, and re-layouts  18.4 us (9%)
  matrix products  17.1 us (8%)
  starting transfers between devices  8.27 us (4%)
  other arithmetic  5.24 us (2%)
    pallas_call x1, Pallas kernels, gather_weights(): pl.pallas_call(gather_kernel, name='gather_weights', out_shape=(jax.Shape...  68.2 us
    pallas_call x1, Pallas kernels, reduce_gradients(): pl.pallas_call(reduce_kernel, name='reduce_gradients', out_shape=(jax.Sha...  59.2 us
    pallas_call x1, Pallas kernels, attention(): pl.pallas_call(attention_kernel, name='attention', out_shape=(jax.ShapeDt...  29.9 us
    dot_general x5, matrix products, row_dot(): lax.dot_general(left, right, (((0,), (0,)), ((), ())), preferred_element_...  7.71 us
    unnamed x45, local copies, waits for them, and re-layouts  6.63 us
    dot_general x4, matrix products, right_dot(): lax.dot_general(left, right, (((1,), (1,)), ((), ())), preferred_element_...  6.63 us
    ppermute x1, starting transfers between devices, swap_rims(): lax.ppermute(rim_rows[:1], 'seq', down)  6.03 us
  transfers between devices with their start and end apart: 2, of which 0 were waited for; matrix products, arithmetic and copies ran while one was open for 5% of the time, Pallas kernels for 29%

profile of v1, /device:TPU:32, one launch (start us, length us, event | category | flops | bytes accessed | tf_op | source)
XLA Modules:
  0.0 207.6 jit_solution(18294484212206870819)
XLA Ops:
  0.7 1.0 copy.14
  1.7 0.8 slice_bitcast_fusion.3
  2.5 1.4 pad_maximum_fusion.6.do_s
  3.9 0.6 fusion.24.qkv_s
  4.5 68.2 %gather_weights.1 = (bf16[4,4,2,96,768]{4,3,2,1,0:T(8,128)(2,1)}, bf16[4,4,2,32,768]{4,3,2,1,0:T(8,128)(2,1)}, bf16[2,4,4,2,32,768]{5,4,3,2,1,0:T(8,128)(2,1)}, bf16[16,768]{1,0:T(8,128)(2,1)}, bf16[16,768]{1,0:T(8,128)(2,1)}) custom-call(bf16[96,768]{1,0:T(8,128)(2,1)} %conv_s.1, bf16[32,768]{1,0:T(8,128)(2,1)} %pad_maximum_fusion.6.do_s, ...), custom_call_target="tpu_custom_call" | custom-call | tf_op jit(solution)/shard_map/gather_weights/pallas_call | solution.py:180
  72.7 0.7 broadcast_select_fusion
  74.0 0.9 copy-done.15
  75.4 2.1 %copy-done = bf16[4,4,2,96,768]{4,3,2,1,0:T(8,128)(2,1)S(1)} copy-done((bf16[4,4,2,96,768]{4,3,2,1,0:T(8,128)(2,1)S(1)}, bf16[4,4,2,96,768]{4,3,2,1,0:T(8,128)(2,1)}, u32[]{:S(2)}) %copy-start) | copy-done | bytes 4718616
  77.5 1.6 fusion.8
  79.4 2.1 %fusion.31 = (bf16[1,4,4,2,32,768]{5,4,3,2,1,0:T(8,128)(2,1)S(1)}, bf16[1,4,4,2,32,768]{5,4,3,2,1,0:T(8,128)(2,1)S(1)}) fusion(bf16[2,4,4,2,32,768]{5,4,3,2,1,0:T(8,128)(2,1)} %get-tuple-element.44), kind=kLoop, calls=%fused_computation.75 | loop fusion | bytes 6291456 | tf_op jit(solution)/shard_map/slice | solution.py:574
  84.0 29.9 %attention.1 = (bf16[4,128,512]{2,1,0:T(8,128)(2,1)S(1)}, bf16[4,128,256]{2,1,0:T(8,128)(2,1)S(1)}) custom-call(bf16[4,128,512]{2,1,0:T(8,128)(2,1)S(1)} %reshape.177.mine), custom_call_target="tpu_custom_call" | custom-call | tf_op jit(solution)/shard_map/attention/pallas_call | solution.py:266
  113.9 0.7 slice_bitcast_fusion
  114.7 0.8 reshape.179
  115.5 1.9 copy.19
  117.4 1.0 copy.18
  118.5 1.5 fusion.25
  120.0 0.6 convolution_add_fusion
  121.1 0.5 copy-done.9
  122.3 4.0 %fusion.35 = f32[128,3072]{1,0:T(8,128)S(1)} fusion(bf16[128,768]{1,0:T(8,128)(2,1)S(1)} %fusion.15, bf16[3072,768]{1,0:T(8,128)(2,1)} %bitcast.65), kind=kOutput, calls=%fused_computation.79 | convolution fusion | flops 603979776 | bytes 6488064 | tf_op jit(solution)/shard_map/dot_general | solution.py:202
  126.8 2.2 %collective-permute-start = (f32[1,768]{1,0:T(1,128)S(1)}, f32[1,768]{1,0:T(1,128)S(1)}, u32[]{:S(2)}, u32[]{:S(2)}) collective-permute-start(f32[1,768]{1,0:T(1,128)S(1)} %fusion.26), channel_id=1, source_target_pairs={{0,1},{1,2},{2,3},{3,4},{4,5},{5,6},{6,7},{8,9},{9,10},{10,11},{11... | collective-permute-start | bytes 9224 | tf_op jit(solution)/shard_map/ppermute | solution.py:518
  129.0 0.6 convolution_convert_fusion.2
  129.6 1.8 convolution_convert_fusion.1
  131.4 3.6 %convolution_convert_fusion = bf16[3072,768]{1,0:T(8,128)(2,1)} fusion(bf16[128,3072]{1,0:T(8,128)(2,1)S(1)} %copy-done.4, bf16[128,768]{1,0:T(8,128)(2,1)S(1)} %copy-done.11), kind=kOutput, calls=%fused_computation | convolution fusion | flops 606339072 | bytes 5701632 | tf_op jit(solution)/shard_map/dot_general | solution.py:206
  135.1 1.0 copy.23
  136.1 1.4 convolution_convert_fusion.3
  138.5 6.0 %collective-permute-start.1 = (f32[1,768]{1,0:T(1,128)S(1)}, f32[1,768]{1,0:T(1,128)S(1)}, u32[]{:S(2)}, u32[]{:S(2)}) collective-permute-start(f32[1,768]{1,0:T(1,128)S(1)} %get-tuple-element.55), channel_id=1, source_target_pairs={{1,0},{2,1},{3,2},{4,3},{5,4},{6,5},{7,6},{9,8},{10,9},{11,10},{12... | collective-permute-start | bytes 9224 | tf_op jit(solution)/shard_map/ppermute | solution.py:518
  144.7 59.2 %reduce_gradients.1 = (f32[96,768]{1,0:T(8,128)S(1)}, f32[16,768]{1,0:T(8,128)S(1)}, f32[16,768]{1,0:T(8,128)S(1)}, f32[24,1536]{1,0:T(8,128)S(1)}) custom-call(bf16[4,4,2,96,768]{4,3,2,1,0:T(8,128)(2,1)} %bitcast.64, bf16[4,4,2,32,768]{4,3,2,1,0:T(8,128)(2,1)S(1)} %pad_maximum_fusion.1.do_p, bf16[2,4,4,2,32,768]{5,4,3,2,1,0:T(8,128)(2,1)S(1)} %pad_maximum_fusion.qkv_p), custom_call_target="tpu_custom_call" | custom-call | tf_op jit(solution)/shard_map/reduce_gradients/pallas_call | solution.py:495
  204.2 0.8 convert_bitcast_fusion
  204.9 0.7 copy.34
  205.7 0.6 copy.35
  206.3 0.7 copy.36
  206.9 0.6 copy.37
  (80 shorter events, 6.5 us)
Async XLA Ops:
  0.6 72.8 %copy-start.17 = (bf16[1,256,768]{2,1,0:T(8,128)(2,1)S(1)}, bf16[1,256,768]{2,1,0:T(8,128)(2,1)}, u32[]{:S(2)}) copy-start(bf16[1,256,768]{2,1,0:T(8,128)(2,1)} %param.11) | copy-start | bytes 1179652
  1.6 72.2 %copy-start.18 = (s32[128,128]{0,1:T(8,128)}, s32[128,128]{0,1:T(8,128)S(1)}, u32[]{:S(2)}) copy-start(s32[128,128]{0,1:T(8,128)S(1)} %copy.14) | copy-start | bytes 196612
  73.5 1.4 copy-start.15
  74.9 2.6 %copy-start = (bf16[4,4,2,96,768]{4,3,2,1,0:T(8,128)(2,1)S(1)}, bf16[4,4,2,96,768]{4,3,2,1,0:T(8,128)(2,1)}, u32[]{:S(2)}) copy-start(bf16[4,4,2,96,768]{4,3,2,1,0:T(8,128)(2,1)} %get-tuple-element.42) | copy-start | bytes 14155780
  75.0 4.1 %copy-start.3 = (bf16[128,3072]{1,0:T(8,128)(2,1)}, bf16[128,3072]{1,0:T(8,128)(2,1)S(1)}, u32[]{:S(2)}) copy-start(bf16[128,3072]{1,0:T(8,128)(2,1)S(1)} %constant_dynamic-update-slice_fusion) | copy-start | bytes 2359300
  79.1 2.4 %copy-start.8 = (bf16[128,768]{1,0:T(8,128)(2,1)}, bf16[128,768]{1,0:T(8,128)(2,1)S(1)}, u32[]{:S(2)}) copy-start(bf16[128,768]{1,0:T(8,128)(2,1)S(1)} %get-tuple-element.52) | copy-start | bytes 589828
  81.5 1.2 copy-start.1
  81.6 1.2 copy-start.13
  115.5 4.5 %copy-start.2 = (bf16[1,4,4,2,32,768]{5,4,3,2,1,0:T(8,128)(2,1)S(1)}, bf16[1,4,4,2,32,768]{5,4,3,2,1,0:T(8,128)(2,1)}, u32[]{:S(2)}) copy-start(bf16[1,4,4,2,32,768]{5,4,3,2,1,0:T(8,128)(2,1)} %copy-done.1) | copy-start | bytes 4718596
  118.4 1.6 copy-start.6
  120.7 0.9 copy-start.9
  120.7 1.1 copy-start.14
  120.7 1.2 copy-start.16
  122.3 4.1 %copy-start.10 = (bf16[128,768]{1,0:T(8,128)(2,1)}, bf16[128,768]{1,0:T(8,128)(2,1)S(1)}, u32[]{:S(2)}) copy-start(bf16[128,768]{1,0:T(8,128)(2,1)S(1)} %fusion.15) | copy-start | bytes 589828
  126.7 2.3 %copy-start.7 = (bf16[4,128,2,128]{1,3,0,2:T(8,128)(2,1)S(1)}, bf16[4,128,2,128]{1,3,0,2:T(8,128)(2,1)}, u32[]{:S(2)}) copy-start(bf16[4,128,2,128]{1,3,0,2:T(8,128)(2,1)} %copy.19) | copy-start | bytes 786436
  126.8 4.6 %copy-start.4 = (bf16[128,3072]{1,0:T(8,128)(2,1)S(1)}, bf16[128,3072]{1,0:T(8,128)(2,1)}, u32[]{:S(2)}) copy-start(bf16[128,3072]{1,0:T(8,128)(2,1)} %copy-done.3) | copy-start | bytes 2359300
  126.8 4.6 %copy-start.11 = (bf16[128,768]{1,0:T(8,128)(2,1)S(1)}, bf16[128,768]{1,0:T(8,128)(2,1)}, u32[]{:S(2)}) copy-start(bf16[128,768]{1,0:T(8,128)(2,1)} %copy-done.10) | copy-start | bytes 589828
  126.8 11.7 %collective-permute-start = (f32[1,768]{1,0:T(1,128)S(1)}, f32[1,768]{1,0:T(1,128)S(1)}, u32[]{:S(2)}, u32[]{:S(2)}) collective-permute-start(f32[1,768]{1,0:T(1,128)S(1)} %fusion.26), channel_id=1, source_target_pairs={{0,1},{1,2},{2,3},{3,4},{4,5},{5,6},{6,7},{8,9},{9,10},{10,11},{11... | collective-permute-start | bytes 9224 | tf_op jit(solution)/shard_map/ppermute | solution.py:518
  131.4 6.1 %copy-start.19 = (s32[128,128]{0,1:T(8,128)S(1)}, s32[128,128]{0,1:T(8,128)}, u32[]{:S(2)}) copy-start(s32[128,128]{0,1:T(8,128)} %copy-done.18) | copy-start | bytes 196612
  135.0 2.6 %copy-start.12 = (bf16[128,768]{1,0:T(8,128)(2,1)S(1)}, bf16[128,768]{1,0:T(8,128)(2,1)}, u32[]{:S(2)}) copy-start(bf16[128,768]{1,0:T(8,128)(2,1)} %copy-done.10) | copy-start | bytes 589828
  136.1 1.9 copy-start.5
  138.5 65.5 %collective-permute-start.1 = (f32[1,768]{1,0:T(1,128)S(1)}, f32[1,768]{1,0:T(1,128)S(1)}, u32[]{:S(2)}, u32[]{:S(2)}) collective-permute-start(f32[1,768]{1,0:T(1,128)S(1)} %get-tuple-element.55), channel_id=1, source_target_pairs={{1,0},{2,1},{3,2},{4,3},{5,4},{6,5},{7,6},{9,8},{10,9},{11,10},{12... | collective-permute-start | bytes 9224 | tf_op jit(solution)/shard_map/ppermute | solution.py:518

commit v2 on v0

v2 whole, which is shorter than its diff:
```python
import math

import jax
import jax.numpy as jnp
from jax import lax
from jax.experimental import pallas as pl
from jax.experimental.pallas import tpu as pltpu
from jax.sharding import PartitionSpec as P

H = 4
BIN = 128
BF16 = jnp.bfloat16
F32 = jnp.float32
MESH = pl.DeviceIdType.MESH
epsilon = 1e-06

SIZES = {"zh": 4, "y": 4, "c": 2, "zl": 2, "x": 4}
PEERS = [(a, k) for a in ("zh", "y", "x") for k in (1, 2, 3)] + [("zl", 1), ("c", 1)]


def here():
    dp = lax.axis_index("dp")
    sq = lax.axis_index("seq")
    return {"zh": dp // 8, "y": lax.rem(dp // 2, 4), "c": lax.rem(dp, 2), "zl": sq // 4, "x": lax.rem(sq, 4)}


def moved(at, **steps):
    to = dict(at)
    for axis, step in steps.items():
        to[axis] = lax.rem(at[axis] + step, SIZES[axis])
    return to


def device(at):
    return (at["zh"] * 8 + at["y"] * 2 + at["c"], at["zl"] * 4 + at["x"])


def meet(devices):
    barrier = pltpu.get_barrier_semaphore()
    for one in devices:
        pl.semaphore_signal(barrier, inc=1, device_id=one, device_id_type=MESH)
    pl.semaphore_wait(barrier, len(devices))


class Sender:
    def __init__(self, send_sems, recv_sems):
        self.send_sems, self.recv_sems, self.used, self.copies = send_sems, recv_sems, 0, []

    def __call__(self, src, dst, to):
        copy = pltpu.make_async_remote_copy(
            src_ref=src,
            dst_ref=dst,
            send_sem=self.send_sems.at[self.used],
            recv_sem=self.recv_sems.at[self.used],
            device_id=to,
            device_id_type=MESH,
        )
        copy.start()
        self.used += 1
        self.copies.append(copy)
        return copy

    def finish(self):
        for copy in self.copies:
            copy.wait_send()


def arrive(copies):
    for copy in copies:
        copy.wait_recv()


def rows16(index, base=0):
    return pl.ds(pl.multiple_of(index * 16 + base, 16), 16)


def half_columns(index):
    return pl.ds(pl.multiple_of(index * 384, 128), 384)


def right_dot(left, right):
    return lax.dot_general(left, right, (((1,), (1,)), ((), ())), preferred_element_type=F32)


def row_dot(left, right):
    return lax.dot_general(left, right, (((0,), (0,)), ((), ())), preferred_element_type=F32)


def dot(left, right):
    return jnp.dot(left, right, preferred_element_type=F32)


def add(target, *terms):
    total = terms[0].astype(F32)
    for term in terms[1:]:
        total += term.astype(F32)
    return total.astype(target.dtype)


def loop(n, body):
    def step(i, carry):
        body(i)
        return carry

    lax.fori_loop(0, n, step, 0)


class Ring:
    def __init__(self, send, at, axis, region):
        self.send, self.me, self.region = send, at[axis], region
        self.right, self.left = device(moved(at, **{axis: 1})), device(moved(at, **{axis: 3}))

    def at(self, step):
        return lax.rem(self.me + step, 4)

    def go(self, index, part, to):
        return [self.send(ref, ref, to) for ref in self.region(index, part)]

    def start(self):
        self.from_left = self.go(self.me, None, self.right)
        self.from_right = self.go(self.me, None, self.left)

    def left_in(self):
        arrive(self.from_left)
        self.far_left = self.go(self.at(3), 0, self.right)
        return self.region(self.at(3), None)

    def right_in(self):
        arrive(self.from_right)
        self.far_right = self.go(self.at(1), 1, self.left)
        return self.region(self.at(1), None)

    def far_left_in(self):
        arrive(self.far_left)
        return self.region(self.at(2), 0)

    def far_right_in(self):
        arrive(self.far_right)
        return self.region(self.at(2), 1)


def layer_kernel(
    conv_s, do_s, qkv_s, pairs, letters, upstream,
    seq_o, conv_o, dna_o, out_o, qkv_o,
    conv_g, do_g, qkv_g, before, after,
    taps, taps_t, onehot, onehot_t, choose, wide, wide_t, unit, slope, inverse, d_proj, attended, shift,
    mine, got, got_kv, outgo, outgo_kv, back, back_kv, d_kv,
    conv_p, do_p, qkv_p, conv_r, do_r, qkv_r,
    ra1, ra2, ra3, ra4, sa1, sa2, sa3,
    rb1, rb2, rb3, rb4, sb1, sb2, sb3,
    rc1, rc2, rc3, rc4, sc1, sc2, sc3,
    final, rim_out, rim_before, rim_after,
    send_sems, recv_sems,
):
    at = here()
    zh, y, c, zl, x = (at[a] for a in ("zh", "y", "c", "zl", "x"))
    sq = lax.axis_index("seq")
    dp = lax.axis_index("dp")
    behind, ahead = (dp, lax.rem(sq + 7, 8)), (dp, lax.rem(sq + 1, 8))
    sibling = device(moved(at, c=1))
    near = device(moved(at, zl=1))
    partners = [moved(at, x=k) for k in (1, 2, 3)]
    across = [moved(at, x=k, zl=1) for k in range(4)]
    everyone = [device(moved(at, **{a: k})) for a, k in PEERS] + [behind, ahead]
    everyone += [device(p) for p in across[1:]]
    barrier = pltpu.get_barrier_semaphore()
    for one in everyone:
        pl.semaphore_signal(barrier, inc=1, device_id=one, device_id_type=MESH)

    row = lax.broadcasted_iota(jnp.int32, (128, 512), 0)
    column = lax.broadcasted_iota(jnp.int32, (128, 512), 1)
    repeat = (column // 4 == row).astype(F32).astype(BF16)
    repeated = dot(letters[...].astype(F32).astype(BF16), repeat)
    onehot[...] = (repeated == lax.rem(column, 4).astype(F32)).astype(F32).astype(BF16)
    onehot_t[...] = onehot[...].T
    row = lax.broadcasted_iota(jnp.int32, (768, 1024), 0)
    column = lax.broadcasted_iota(jnp.int32, (768, 1024), 1)
    inside = lax.rem(column, 32)
    choose[...] = ((column // 32 * 24 + inside == row) & (inside < 24)).astype(F32).astype(BF16)
    quarter = rows16(x)
    part, part_rows = x // 2, rows16(lax.rem(x, 2))
    half, other_half = half_columns(zl), half_columns(1 - zl)
    tail = pl.ds(64, 32)
    conv_g[zh, y, c, quarter] = conv_s[quarter]
    conv_g[zh, y, c, 64:96] = conv_s[64:96]
    do_g[zh, y, c] = do_s[...]
    qkv_g[part, zh, y, c, part_rows, half] = qkv_s[part, part_rows, half]
    pl.semaphore_wait(barrier, len(everyone))

    send = Sender(send_sems, recv_sems)
    a1, b1, c1, a2, c2 = ([] for _ in range(5))
    for k in (1, 2, 3):
        block = qkv_g.at[part, zh, y, c, part_rows, half]
        c1.append(send(block, block, device(moved(at, zh=k))))
    for k in (1, 2, 3):
        block = conv_g.at[zh, y, c, quarter]
        a1.append(send(block, block, device(moved(at, zh=k))))
    halo = [
        send(pairs.at[pl.ds(112, 16), pl.ds(768, 768)], before, ahead),
        send(pairs.at[pl.ds(0, 16), pl.ds(0, 768)], after, behind),
    ]
    for k in (1, 2, 3):
        to = device(moved(at, zh=k))
        for block in (conv_g.at[zh, y, c, tail], do_g.at[zh, y, c]):
            b1.append(send(block, block, to))
    arrive(c1)
    for k in (1, 2, 3):
        block = qkv_g.at[part, :, y, c, part_rows, half]
        c2.append(send(block, block, device(moved(at, y=k))))
    arrive(a1)
    for k in (1, 2, 3):
        block = conv_g.at[:, y, c, quarter]
        a2.append(send(block, block, device(moved(at, y=k))))
    arrive(b1)

    def cut(part):
        return pl.ds(0, 4) if part is None else pl.ds(2 * part, 2)

    def region_a(index, part):
        return [conv_g.at[cut(part), :, c, rows16(index)]]

    def region_b(index, part):
        return [conv_g.at[cut(part), index, c, tail], do_g.at[cut(part), index, c]]

    def region_c(index, part, columns=half):
        return [qkv_g.at[index // 2, cut(part), :, c, rows16(lax.rem(index, 2)), columns]]

    core, far = [], []

    def pass_on(refs):
        for ref in refs:
            core.append(send(ref, ref, sibling))

    def pass_far(refs):
        for ref in refs:
            far.append(send(ref, ref, near))

    ring_a = Ring(send, at, "x", region_a)
    ring_b = Ring(send, at, "y", region_b)
    ring_c = Ring(send, at, "x", region_c)
    ring_b.start()
    pass_on(region_b(y, None))
    arrive(c2)
    ring_c.start()
    pass_far(region_c(x, None))
    pass_on(region_c(x, None))
    arrive(a2)
    ring_a.start()
    pass_on(region_a(x, None))

    arrive(halo)
    taps[1] = pairs[:, 0:768]
    taps[2] = pairs[:, 768:1536]
    shift[8:136] = pairs[:, 768:1536].astype(F32)
    shift[0:8] = jnp.where(sq > 0, before[...].astype(F32)[8:16], 0.0)
    taps[0] = shift[7:135].astype(BF16)
    shift[0:128] = pairs[:, 0:768].astype(F32)
    shift[128:136] = jnp.where(sq < 7, after[...].astype(F32)[0:8], 0.0)
    taps[3] = shift[1:129].astype(BF16)

    refs = ring_c.left_in()
    pass_far(refs)
    pass_on(refs)
    refs = ring_c.right_in()
    pass_far(refs)
    pass_on(refs)
    pass_on(ring_b.left_in())
    pass_on(ring_b.right_in())
    refs = ring_c.far_left_in() + ring_c.far_right_in()
    pass_far(refs)
    pass_on(refs)
    pass_on(ring_a.left_in())
    pass_on(ring_a.right_in())
    pass_on(ring_b.far_left_in())
    pass_on(ring_b.far_right_in())
    for k in (0, 3, 1):
        arrive([far[(0, 3, 1).index(k)]])
        pass_on(region_c(lax.rem(x + k, 4), None, other_half))
    for k in (0, 1):
        arrive([far[3 + k]])
        pass_on(region_c(lax.rem(x + 2, 4), k, other_half))
    pass_on(ring_a.far_left_in())
    pass_on(ring_a.far_right_in())

    def transpose_tap(i):
        taps_t[i] = taps[i].T

    loop(4, transpose_tap)
    arrive(core)

    dna_full = do_g[:, :, :, 0:16].reshape(512, 768)
    out_full = do_g[:, :, :, 16:32].reshape(512, 768)
    d_attend = right_dot(upstream[...], out_full).astype(BF16)
    slope[...] = dot(onehot[...], dna_full)

    def one_tap(i):
        slope[...] += dot(taps[i], conv_g[i].reshape(768, 768))

    loop(4, one_tap)
    pre = slope[...]
    bend = jnp.tanh(math.sqrt(2.0 / math.pi) * (pre + 0.044715 * (pre * pre * pre)))
    share = 0.5 * (1.0 + bend)
    feature = (pre * share).astype(BF16).astype(F32)
    slope[...] = share + pre * (0.5 * (1.0 - bend * bend)) * (
        math.sqrt(2.0 / math.pi) * (1.0 + 3.0 * 0.044715 * (pre * pre))
    )
    scale = lax.rsqrt(jnp.mean(feature * feature, axis=1, keepdims=True) + epsilon)
    inverse[...] = scale
    unit[...] = feature * scale
    wide[...] = dot(unit[...].astype(BF16), choose[...]).astype(BF16)
    for i in range(2):
        projected = dot(wide[...], qkv_g[i].reshape(1024, 768)).astype(BF16)
        for piece in range(6):
            kind, head = divmod(6 * i + piece, 4)
            place = (2, 0, 1)[kind] * 128
            mine[head, :, place : place + 128] = projected[:, 128 * piece : 128 * piece + 128]
    for head in range(H):
        mine[head, :, 384:512] = d_attend[:, 128 * head : 128 * head + 128]

    kv, rest = pl.ds(0, 256), pl.ds(256, 256)
    kv_in, rest_in = [], {}
    for p in across:
        kv_in.append(send(mine.at[p["x"], :, kv], got_kv.at[x], device(p)))
    for p in partners:
        kv_in.append(send(mine.at[p["x"], :, kv], got.at[x, :, kv], device(p)))
    for k, p in zip((1, 2, 3), partners):
        rest_in[k] = send(mine.at[p["x"], :, rest], got.at[x, :, rest], device(p))
    got[x] = mine[x]
    wide_t[...] = wide[...].T
    d_kv[...] = jnp.zeros_like(d_kv)
    arrive(kv_in)
    keys = jnp.concatenate([got[:, :, 0:128].reshape(512, 128), got_kv[:, :, 0:128].reshape(512, 128)], axis=0)
    values = jnp.concatenate([got[:, :, 128:256].reshape(512, 128), got_kv[:, :, 128:256].reshape(512, 128)], axis=0)
    scaling = 1.0 / math.sqrt(128)
    home = []
    for k in (0, 1, 3, 2):
        if k:
            arrive([rest_in[k]])
        source = lax.rem(x + 4 - k, 4)
        queries = got[source, :, 256:384]
        upward = got[source, :, 384:512]
        scores = right_dot(queries, keys) * scaling
        powers = jnp.exp(scores - jnp.max(scores, axis=1, keepdims=True))
        probs = powers * (1.0 / jnp.sum(powers, axis=1, keepdims=True))
        probs_low = probs.astype(BF16)
        outgo[source, :, 0:128] = dot(probs_low, values).astype(BF16)
        d_probs = right_dot(upward, values)
        inner = jnp.sum(probs * d_probs, axis=1, keepdims=True)
        d_scores = (probs * (d_probs - inner) * scaling).astype(BF16)
        outgo[source, :, 128:256] = dot(d_scores, keys).astype(BF16)
        if k:
            block = pl.ds(0, 256)
            to = device(moved(at, x=4 - k))
            home.append(send(outgo.at[source, :, block], back.at[x, :, block], to))
        d_kv[:, 0:128] += row_dot(d_scores, queries)
        d_kv[:, 128:256] += row_dot(probs_low, upward)
    outgo_kv[...] = d_kv[512:1024].astype(BF16).reshape(4, 128, 256)
    for p in across:
        home.append(send(outgo_kv.at[p["x"]], back_kv.at[x], device(p)))
    outgo[:, :, 256:512] = d_kv[0:512].astype(BF16).reshape(4, 128, 256)
    for p in partners:
        block = pl.ds(256, 256)
        home.append(send(outgo.at[p["x"], :, block], back.at[x, :, block], device(p)))
    back[x] = outgo[x]
    arrive(home)
    for head in range(H):
        columns = slice(128 * head, 128 * head + 128)
        attended[:, columns] = back[head, :, 0:128]
        d_proj[:, columns] = back[head, :, 128:256]
        for kind in range(2):
            total = back[head, :, 256 + 128 * kind : 384 + 128 * kind].astype(F32) + back_kv[
                head, :, 128 * kind : 128 * kind + 128
            ].astype(F32)
            start = 512 * (kind + 1) + 128 * head
            d_proj[:, start : start + 128] = total.astype(BF16)

    for i in range(2):
        qkv_p[i] = dot(wide_t[...], d_proj[:, 768 * i : 768 * i + 768]).astype(BF16).reshape(4, 4, 2, 32, 768)
    core_c = {}
    for k, columns in ((1, other_half), (0, half)):
        core_c[k] = [send(qkv_p.at[:, :, :, 1 - c, :, columns], qkv_r.at[:, :, :, :, columns], sibling)]
    d_wide = right_dot(d_proj[:, 0:768], qkv_g[0].reshape(1024, 768)) + right_dot(
        d_proj[:, 768:1536], qkv_g[1].reshape(1024, 768)
    )

    def sum_c(columns):
        def one(i):
            for part in range(2):
                qkv_p[part, i, :, c, :, columns] = add(
                    qkv_p, qkv_p[part, i, :, c, :, columns], qkv_r[part, i, :, :, columns]
                )

        loop(4, one)

    arrive(core_c[1])
    sum_c(other_half)
    c1 = [send(qkv_p.at[:, :, :, c, :, other_half], rc1, near)]
    high = d_wide.astype(BF16)
    low = (d_wide - high.astype(F32)).astype(BF16)
    d_normed = right_dot(high, choose[...]) + right_dot(low, choose[...])
    d_feature = upstream[...].astype(F32) + inverse[...] * (
        d_normed - unit[...] * jnp.mean(d_normed * unit[...], axis=1, keepdims=True)
    )
    d_pre = (d_feature * slope[...]).astype(BF16)

    def one_conv(i):
        conv_p[i] = dot(taps_t[i], d_pre).astype(BF16).reshape(4, 2, 96, 768)

    loop(4, one_conv)
    do_p[:, :, :, 0:16] = dot(onehot_t[...], d_pre).astype(BF16).reshape(4, 4, 2, 16, 768)
    do_p[:, :, :, 16:32] = row_dot(attended[...], upstream[...]).astype(BF16).reshape(4, 4, 2, 16, 768)
    order = (1, 2, 3, 0)
    xs = {k: lax.rem(x + k, 4) for k in order}
    ys = {k: lax.rem(y + k, 4) for k in order}
    zs = {k: lax.rem(zh + k, 4) for k in order}
    core_a, core_b = {}, {}
    for k in order:
        core_a[k] = [send(conv_p.at[:, :, 1 - c, rows16(xs[k])], conv_r.at[:, :, rows16(xs[k])], sibling)]
        core_b[k] = [
            send(conv_p.at[:, ys[k], 1 - c, tail], conv_r.at[:, ys[k], tail], sibling),
            send(do_p.at[:, ys[k], 1 - c], do_r.at[:, ys[k]], sibling),
        ]
    arrive(core_c[0])
    sum_c(half)
    a1, b1 = {}, {}
    for k in order:
        arrive(core_a[k])
        rows = rows16(xs[k])

        def sum_a(i, rows=rows):
            conv_p[i, :, c, rows] = add(conv_p, conv_p[i, :, c, rows], conv_r[i, :, rows])

        loop(4, sum_a)
        if k:
            a1[k] = send(conv_p.at[:, :, c, rows], ra1.at[k - 1], device(moved(at, x=k)))
        arrive(core_b[k])
        ky = ys[k]

        def sum_b(i, ky=ky):
            conv_p[i, ky, c, 64:96] = add(conv_p, conv_p[i, ky, c, 64:96], conv_r[i, ky, 64:96])
            do_p[i, ky, c] = add(do_p, do_p[i, ky, c], do_r[i, ky])

        loop(4, sum_b)
        if k:
            to = device(moved(at, y=k))
            b1[k] = [
                send(conv_p.at[:, ky, c, tail], rb1.at[k - 1, :, pl.ds(0, 32)], to),
                send(do_p.at[:, ky, c], rb1.at[k - 1, :, pl.ds(32, 32)], to),
            ]

    arrive(c1)

    def first_c(i):
        for part in range(2):
            sc1[part, i] = add(sc1, qkv_p[part, i, :, c, :, half], rc1[part, i])

    loop(4, first_c)
    c2 = [
        send(sc1.at[xs[k] // 2, :, :, rows16(lax.rem(xs[k], 2))], rc2.at[k - 1], device(moved(at, x=k)))
        for k in (1, 2, 3)
    ]

    def tap_grad(i):
        return right_dot(d_pre, conv_g[i].reshape(768, 768))

    shift[8:136] = tap_grad(3)
    rim_out[0] = shift[128:136]
    rims = [send(rim_out.at[0], rim_before, ahead)]
    inner_rows = tap_grad(0)
    rim_out[1] = inner_rows[0:8]
    rims.append(send(rim_out.at[1], rim_after, behind))
    even = tap_grad(1)
    odd = tap_grad(2)
    arrive(rims)
    shift[0:8] = jnp.where(sq > 0, rim_before[...], 0.0)
    seq_o[:, 0:768] = (even + shift[7:135]).astype(BF16)
    shift[0:128] = inner_rows
    shift[128:136] = jnp.where(sq < 7, rim_after[...], 0.0)
    seq_o[:, 768:1536] = (odd + shift[1:129]).astype(BF16)

    arrive(a1.values())

    def first_a(i):
        sa1[i] = add(sa1, conv_p[i, :, c, rows16(x)], ra1[0, i], ra1[1, i], ra1[2, i])

    loop(4, first_a)
    a2 = [send(sa1.at[:, ys[k]], ra2.at[k - 1], device(moved(at, y=k))) for k in (1, 2, 3)]
    for k in (1, 2, 3):
        arrive(b1[k])

    def first_b(i):
        sb1[i, 0:32] = add(sb1, conv_p[i, y, c, 64:96], rb1[0, i, 0:32], rb1[1, i, 0:32], rb1[2, i, 0:32])
        sb1[i, 32:64] = add(sb1, do_p[i, y, c], rb1[0, i, 32:64], rb1[1, i, 32:64], rb1[2, i, 32:64])

    loop(4, first_b)
    b2 = [send(sb1.at[:, rows16(xs[k])], rb2.at[k - 1], device(moved(at, x=k))) for k in (1, 2, 3)]

    arrive(c2)

    def second_c(i):
        own = sc1[x // 2, i, :, rows16(lax.rem(x, 2))]
        sc2[i] = add(sc2, own, rc2[0, i], rc2[1, i], rc2[2, i])

    loop(4, second_c)
    c3 = [send(sc2.at[:, ys[k]], rc3.at[k - 1], device(moved(at, y=k))) for k in (1, 2, 3)]
    arrive(a2)

    def second_a(i):
        sa2[i] = add(sa2, sa1[i, y], ra2[0, i], ra2[1, i], ra2[2, i])

    loop(4, second_a)
    a3 = [send(sa2.at[zs[k]], ra3.at[k - 1], device(moved(at, zh=k))) for k in (1, 2, 3)]
    arrive(b2)

    def second_b(i):
        sb2[i] = add(sb2, sb1[i, rows16(x)], rb2[0, i], rb2[1, i], rb2[2, i])

    loop(4, second_b)
    b3 = [send(sb2.at[zs[k]], rb3.at[k - 1], device(moved(at, zh=k))) for k in (1, 2, 3)]

    arrive(c3)

    def third_c(i):
        sc3[i] = add(sc3, sc2[i, y], rc3[0, i], rc3[1, i], rc3[2, i])

    loop(4, third_c)
    c4 = [send(sc3.at[zs[k]], rc4.at[k - 1], device(moved(at, zh=k))) for k in (1, 2, 3)]
    arrive(a3)
    sa3[...] = add(sa3, sa2[zh], ra3[0], ra3[1], ra3[2])
    a4 = send(sa3, ra4, near)
    arrive(b3)
    sb3[...] = add(sb3, sb2[zh], rb3[0], rb3[1], rb3[2])
    b4 = send(sb3, rb4, near)

    arrive(c4)
    final[x, 2, :, half] = add(final, sc3[zh], rc4[0], rc4[1], rc4[2])
    block = final.at[x, 2, :, half]
    c5 = send(block, block, near)
    arrive([a4])
    final[x, 0] = add(final, sa3[...], ra4[...])
    arrive([b4])
    final[x, 1] = add(final, sb3[...], rb4[...])
    block = final.at[x, pl.ds(0, 2)]
    spread = [send(block, block, device(moved(at, x=k))) for k in (1, 2, 3)]
    arrive([c5])
    spread += [send(final.at[x, 2], final.at[x, 2], device(moved(at, x=k))) for k in (1, 2, 3)]
    arrive(spread)
    for q in range(4):
        conv_o[16 * q : 16 * q + 16] = final[q, 0].astype(F32)
    conv_o[64:80] = final[0, 1].astype(F32)
    conv_o[80:96] = final[1, 1].astype(F32)
    dna_o[...] = final[2, 1].astype(F32)
    out_o[...] = final[3, 1].astype(F32)
    qkv_o[0:16, 0:768] = final[0, 2].astype(F32)
    qkv_o[16:24, 0:768] = final[1, 2].astype(F32)[0:8]
    qkv_o[0:16, 768:1536] = final[2, 2].astype(F32)
    qkv_o[16:24, 768:1536] = final[3, 2].astype(F32)[0:8]
    send.finish()


def layer(conv_s, do_s, qkv_s, pairs, letters, upstream):
    vmem = pl.BlockSpec(memory_space=pltpu.VMEM)
    low = [
        (4, 4, 2, 96, 768), (4, 4, 2, 32, 768), (2, 4, 4, 2, 32, 768), (16, 768), (16, 768),
        (4, 128, 768), (4, 768, 128), (128, 512), (512, 128), (768, 1024), (128, 1024), (1024, 128),
    ]
    wide = [(128, 768), (128, 768), (128, 1)]
    low_2 = [(128, 1536), (128, 512)]
    wide_2 = [(136, 768)]
    low_3 = [(4, 128, 512), (4, 128, 512), (4, 128, 256), (4, 128, 512), (4, 128, 256), (4, 128, 512), (4, 128, 256)]
    wide_3 = [(1024, 256)]
    low_4 = [
        (4, 4, 2, 96, 768), (4, 4, 2, 32, 768), (2, 4, 4, 2, 32, 768), (4, 4, 96, 768), (4, 4, 32, 768), (2, 4, 4, 32, 768),
        (3, 4, 4, 16, 768), (3, 4, 16, 768), (3, 16, 768), (16, 768), (4, 4, 16, 768), (4, 16, 768), (16, 768),
        (3, 4, 64, 768), (3, 4, 16, 768), (3, 16, 768), (16, 768), (4, 64, 768), (4, 16, 768), (16, 768),
        (2, 4, 4, 32, 384), (3, 4, 4, 16, 384), (3, 4, 16, 384), (3, 16, 384),
        (2, 4, 4, 32, 384), (4, 4, 16, 384), (4, 16, 384),
        (4, 3, 16, 768),
    ]
    wide_4 = [(2, 8, 768), (8, 768), (8, 768)]
    scratch = []
    for shapes, kind in (
        (low, BF16), (wide, F32), (low_2, BF16), (wide_2, F32), (low_3, BF16), (wide_3, F32), (low_4, BF16), (wide_4, F32),
    ):
        scratch += [pltpu.VMEM(shape, kind) for shape in shapes]
    return pl.pallas_call(
        layer_kernel,
        name="layer",
        out_shape=(
            jax.ShapeDtypeStruct((128, 1536), BF16),
            jax.ShapeDtypeStruct((96, 768), F32),
            jax.ShapeDtypeStruct((16, 768), F32),
            jax.ShapeDtypeStruct((16, 768), F32),
            jax.ShapeDtypeStruct((24, 1536), F32),
        ),
        in_specs=[vmem] * 6,
        out_specs=(vmem,) * 5,
        scratch_shapes=scratch + [pltpu.SemaphoreType.DMA((160,)), pltpu.SemaphoreType.DMA((160,))],
        compiler_params=pltpu.CompilerParams(
            collective_id=1, has_side_effects=True, vmem_limit_bytes=60 * 2**20
        ),
    )(conv_s, do_s, qkv_s, pairs, letters, upstream)


def per_device(seq_in, bases, conv_weight, dna_weight, qkv_weight, out_weight, cotangent):
    qkv_parts = jnp.pad(
        jnp.stack([qkv_weight[:, :768], qkv_weight[:, 768:]]), ((0, 0), (0, 8), (0, 0))
    )
    seq_grad, conv_grad, dna_grad, out_grad, qkv_grad = layer(
        conv_weight,
        jnp.concatenate([dna_weight, out_weight], axis=0),
        qkv_parts,
        seq_in[0].reshape(128, 1536),
        bases[0].reshape(128, BIN),
        cotangent[0],
    )
    return (seq_grad.reshape(1, 256, 768), conv_grad, dna_grad, qkv_grad, out_grad)


def solution(mesh):
    in_specs = (
        P("dp", "seq", None),
        P("dp", "seq"),
        P("dp", None),
        P("dp", None),
        P("dp", None),
        P("dp", None),
        P("dp", "seq", None),
    )
    out_specs = (P("dp", "seq", None), P("dp", None), P("dp", None), P("dp", None), P("dp", None))
    return jax.shard_map(
        per_device, mesh=mesh, in_specs=in_specs, out_specs=out_specs, check_vma=False
    )
```

time: 710 us -> 148 us (0.21)
  waiting for transfers between devices: 483 us -> 0 us
  blocking collectives: 142 us -> 0 us
  Pallas kernels: 0 us -> 139 us
  matrix products: 39.3 us -> 0 us
  starting transfers between devices: 14.3 us -> 0 us
  between operations: 14.5 us -> 0.66 us
  other arithmetic: 9.5 us -> 2.07 us
    reduce_scatter x5 -> x0, waiting for transfers between devices: 396 us -> none  [the longest x4 353 us: data_shard(): lax.psum_scatter(row_product(left_rows, right_rows).astype(jnp.bfloat16),...]
    pallas_call x0 -> x1, Pallas kernels: none -> 139 us  [layer(): pl.pallas_call(layer_kernel, name='layer', out_shape=(jax.ShapeDtypeStruc...]
    all_gather x2 -> x0, blocking collectives: 99.5 us -> none  [the longest x1 54.1 us: per_device(): lax.all_gather(dna_weight, 'dp', axis=0, tiled=True)]
    all_gather x4 -> x0, waiting for transfers between devices: 84.3 us -> none  [the longest x1 49.9 us: per_device(): lax.all_gather(qkv_weight, 'dp', axis=0, tiled=True)]
    psum x1 -> x0, blocking collectives: 42.2 us -> none  [per_device(): totals = lax.psum(shards, 'seq')]
    dot_general x28 -> x0, matrix products: 39.3 us -> none  [the longest x11 12.7 us: right_product(): lax.dot_general(left_rows, right_rows, (((1,), (1,)), ((), ())), preferre...]
    ppermute x4 -> x0, starting transfers between devices: 13.7 us -> none  [the longest x2 9.61 us: with_halo(): after = lax.ppermute(first, axis, down)]
  transfers between devices with their start and end apart: 13 -> 0, of which waited for: 9 -> 0; matrix products, arithmetic and copies ran while one was open for 6% -> 0% of each run, Pallas kernels for 0% -> 0%
where the time goes in v2:
time: 148 us
  Pallas kernels  139 us (94%)
  local copies, waits for them, and re-layouts  6.43 us (4%)
  other arithmetic  2.07 us (1%)
    pallas_call x1, Pallas kernels, layer(): pl.pallas_call(layer_kernel, name='layer', out_shape=(jax.ShapeDtypeStruc...  139 us

profile of v2, /device:TPU:32, one launch (start us, length us, event | category | flops | bytes accessed | tf_op | source)
XLA Modules:
  0.0 148.2 jit_solution(7114767710722391099)
XLA Ops:
  0.6 0.0 copy-start
  0.6 1.4 pad_maximum_fusion.do_s
  2.1 0.8 slice_bitcast_fusion.1
  2.9 0.6 fusion.2.qkv_s
  3.5 0.0 copy-done
  3.5 0.9 reshape_squeeze.6.pairs
  4.4 139.0 %layer.1 = (bf16[128,1536]{1,0:T(8,128)(2,1)}, f32[96,768]{1,0:T(8,128)}, f32[16,768]{1,0:T(8,128)}, f32[16,768]{1,0:T(8,128)}, f32[24,1536]{1,0:T(8,128)}) custom-call(bf16[96,768]{1,0:T(8,128)(2,1)} %conv_s.1, bf16[32,768]{1,0:T(8,128)(2,1)} %pad_maximum_fusion.do_s, bf16[2,32,768]{2,1,0:T(8,128)(2,1)} %fusion.2.qkv_s, ...), custom_call_target="tpu_custom_call" | custom-call | tf_op jit(solution)/shard_map/layer/pallas_call | solution.py:586
  143.4 0.0 copy-start.1
  143.4 1.9 %reshape.13 = bf16[1,256,768]{2,1,0:T(8,128)(2,1)} reshape(bf16[128,1536]{1,0:T(8,128)(2,1)} %get-tuple-element.10) | data formatting | bytes 786432 | tf_op jit(solution)/shard_map/reshape | solution.py:617
  145.4 0.0 copy-done.1
  145.4 0.0 copy-start.4
  145.4 0.0 copy-start.2
  145.4 0.7 copy.16
  146.1 0.1 copy-done.4
  146.2 0.6 copy.17
  146.8 0.0 copy-done.2
  146.8 0.0 copy-start.3
  146.8 0.7 copy.18
  147.4 0.1 copy-done.3
  147.6 0.6 copy.19
Async XLA Ops:
  0.6 2.9 %copy-start = (bf16[1,256,768]{2,1,0:T(8,128)(2,1)S(1)}, bf16[1,256,768]{2,1,0:T(8,128)(2,1)}, u32[]{:S(2)}) copy-start(bf16[1,256,768]{2,1,0:T(8,128)(2,1)} %param.7) | copy-start | bytes 1179652
  143.4 1.9 %copy-start.1 = (f32[96,768]{1,0:T(8,128)S(1)}, f32[96,768]{1,0:T(8,128)}, u32[]{:S(2)}) copy-start(f32[96,768]{1,0:T(8,128)} %get-tuple-element.23) | copy-start | bytes 884740
  145.4 0.8 copy-start.4
  145.4 1.4 copy-start.2
  146.8 0.8 copy-start.3

commit v3 on v2

v3 whole, which is shorter than its diff:
```python
import math

import jax
import jax.numpy as jnp
from jax import lax
from jax.experimental import pallas as pl
from jax.experimental.pallas import tpu as pltpu
from jax.sharding import PartitionSpec as P

H = 4
BIN = 128
BF16 = jnp.bfloat16
F32 = jnp.float32
MESH = pl.DeviceIdType.MESH
epsilon = 1e-06

SIZES = {"zh": 4, "y": 4, "c": 2, "zl": 2, "x": 4}
PEERS = [(a, k) for a in ("zh", "y", "x") for k in (1, 2, 3)] + [("zl", 1), ("c", 1)]


def here():
    dp = lax.axis_index("dp")
    sq = lax.axis_index("seq")
    return {"zh": dp // 8, "y": lax.rem(dp // 2, 4), "c": lax.rem(dp, 2), "zl": sq // 4, "x": lax.rem(sq, 4)}


def moved(at, **steps):
    to = dict(at)
    for axis, step in steps.items():
        to[axis] = lax.rem(at[axis] + step, SIZES[axis])
    return to


def device(at):
    return (at["zh"] * 8 + at["y"] * 2 + at["c"], at["zl"] * 4 + at["x"])


class Sender:
    def __init__(self, send_sems, recv_sems):
        self.send_sems, self.recv_sems, self.used, self.copies = send_sems, recv_sems, 0, []

    def __call__(self, src, dst, to):
        copy = pltpu.make_async_remote_copy(
            src_ref=src,
            dst_ref=dst,
            send_sem=self.send_sems.at[self.used],
            recv_sem=self.recv_sems.at[self.used],
            device_id=to,
            device_id_type=MESH,
        )
        copy.start()
        self.used += 1
        self.copies.append(copy)
        return copy

    def finish(self):
        for copy in self.copies:
            copy.wait_send()


def arrive(copies):
    for copy in copies:
        copy.wait_recv()


def rows16(index, base=0):
    return pl.ds(pl.multiple_of(index * 16 + base, 16), 16)


def half_columns(index):
    return pl.ds(pl.multiple_of(index * 384, 128), 384)


def right_dot(left, right):
    return lax.dot_general(left, right, (((1,), (1,)), ((), ())), preferred_element_type=F32)


def row_dot(left, right):
    return lax.dot_general(left, right, (((0,), (0,)), ((), ())), preferred_element_type=F32)


def dot(left, right):
    return jnp.dot(left, right, preferred_element_type=F32)


def add(target, *terms):
    total = terms[0].astype(F32)
    for term in terms[1:]:
        total += term.astype(F32)
    return total.astype(target.dtype)


def loop(n, body):
    def step(i, carry):
        body(i)
        return carry

    lax.fori_loop(0, n, step, 0)


class Ring:
    def __init__(self, send, at, axis, region):
        self.send, self.me, self.region = send, at[axis], region
        self.right, self.left = device(moved(at, **{axis: 1})), device(moved(at, **{axis: 3}))

    def at(self, step):
        return lax.rem(self.me + step, 4)

    def go(self, index, part, to):
        return [self.send(ref, ref, to) for ref in self.region(index, part)]

    def start(self):
        self.from_left = self.go(self.me, None, self.right)
        self.from_right = self.go(self.me, None, self.left)

    def left_in(self):
        arrive(self.from_left)
        self.far_left = self.go(self.at(3), 0, self.right)

    def right_in(self):
        arrive(self.from_right)
        self.far_right = self.go(self.at(1), 1, self.left)

    def both_in(self):
        self.left_in()
        self.right_in()

    def far_in(self):
        arrive(self.far_left)
        arrive(self.far_right)


def layer_kernel(
    conv_s, dna_s, qkv_s, out_s, rows_in, letters, upstream,
    seq_o, final,
    conv_g, do_g, qkv_g, qkv_pad, before, after,
    taps, taps_t, onehot, onehot_t, choose, wide, wide_t, d_proj, attended,
    mine, got, got_kv, outgo, outgo_kv, back, back_kv,
    conv_p, do_p, qkv_p, conv_r, do_r, qkv_r,
    fa, na, sa1, ra2, sa2, ra3, sa3, ra4,
    fb, nb, sb1, rb2, sb2, rb3, sb3, rb4,
    fcx, ncx, scx1, rcx2, fcy, ncy, scy1, rcy2, sc2, rc3, sc3, rc4,
    slope, unit, inverse, rows_f, d_kv, rim_out, rim_before, rim_after,
    send_sems, recv_sems,
):
    at = here()
    zh, y, c, zl, x = (at[a] for a in ("zh", "y", "c", "zl", "x"))
    sq = lax.axis_index("seq")
    dp = lax.axis_index("dp")
    behind, ahead = (dp, lax.rem(sq + 7, 8)), (dp, lax.rem(sq + 1, 8))
    sibling = device(moved(at, c=1))
    near = device(moved(at, zl=1))
    partners = [moved(at, x=k) for k in (1, 2, 3)]
    across = [moved(at, x=k, zl=1) for k in range(4)]
    everyone = [device(moved(at, **{a: k})) for a, k in PEERS] + [behind, ahead]
    everyone += [device(p) for p in across[1:]]
    barrier = pltpu.get_barrier_semaphore()
    for one in everyone:
        pl.semaphore_signal(barrier, inc=1, device_id=one, device_id_type=MESH)
    xs = [lax.rem(x + k, 4) for k in range(4)]
    ys = [lax.rem(y + k, 4) for k in range(4)]
    zs = [lax.rem(zh + k, 4) for k in range(4)]

    quarter = rows16(x)
    part, part_rows = x // 2, rows16(lax.rem(x, 2))
    tail, first_half, second_half = pl.ds(64, 32), pl.ds(0, 384), pl.ds(384, 384)
    for i in range(2):
        block = qkv_s[:, 768 * i : 768 * i + 768].astype(F32)
        qkv_pad[i] = jnp.concatenate([block, jnp.zeros((8, 768), F32)], axis=0).astype(BF16)
    conv_g[zh, y, c, quarter] = conv_s[quarter]
    conv_g[zh, y, c, 64:96] = conv_s[64:96]
    do_g[zh, y, c, 0:16] = dna_s[...]
    do_g[zh, y, c, 16:32] = out_s[...]
    qkv_g[part, zh, y, c, part_rows, 0:384] = qkv_pad[part, part_rows, 0:384]
    for i in range(2):
        qkv_g[i, zh, y, c, :, 384:768] = qkv_pad[i, :, 384:768]
    row = lax.broadcasted_iota(jnp.int32, (128, 512), 0)
    column = lax.broadcasted_iota(jnp.int32, (128, 512), 1)
    repeat = (column // 4 == row).astype(F32).astype(BF16)
    repeated = dot(letters[...].astype(F32).astype(BF16), repeat)
    onehot[...] = (repeated == lax.rem(column, 4).astype(F32)).astype(F32).astype(BF16)
    pl.semaphore_wait(barrier, len(everyone))

    send = Sender(send_sems, recv_sems)

    def refs_a(height, step, index, part=None):
        rows = pl.ds(0, 4) if part is None else pl.ds(2 * part, 2)
        rows = rows if height is None else height
        return [
            conv_g.at[rows, step, c, rows16(index)],
            qkv_g.at[index // 2, rows, step, c, rows16(lax.rem(index, 2)), first_half],
        ]

    def refs_b(height, step, part=None):
        if part is None:
            return [
                conv_g.at[height, step, c, tail],
                do_g.at[height, step, c],
                qkv_g.at[:, height, step, c, :, second_half],
            ]
        return [
            conv_g.at[height, step, c, pl.ds(64 + 16 * part, 16)],
            do_g.at[height, step, c, pl.ds(16 * part, 16)],
            qkv_g.at[part, height, step, c, :, second_half],
        ]

    core = []

    def pass_on(refs):
        for ref in refs:
            core.append(send(ref, ref, sibling))

    def pass_a(step):
        pass_on([conv_g.at[:, step, c, pl.ds(0, 64)], qkv_g.at[:, :, step, c, :, first_half]])

    def pass_b(height):
        pass_on([conv_g.at[height, :, c, tail], do_g.at[height, :, c], qkv_g.at[:, height, :, c, :, second_half]])

    a1, a2 = [], []
    for k in (1, 3, 2):
        a1 += [send(ref, ref, device(moved(at, zh=k))) for ref in refs_a(zh, y, x)]
    halo = [
        send(rows_in.at[pl.ds(240, 16)], before, ahead),
        send(rows_in.at[pl.ds(0, 16)], after, behind),
    ]
    ring_z = Ring(send, at, "zh", lambda index, part: refs_b(index, y, part))
    rings_y = [Ring(send, at, "y", lambda index, part, v=zs[k]: refs_b(v, index, part)) for k in range(4)]
    rings_x = [Ring(send, at, "x", lambda index, part, v=ys[k]: refs_a(None, v, index, part)) for k in range(4)]
    ring_z.start()
    rings_y[0].start()
    arrive(a1)
    rings_x[0].start()
    for k in (1, 3, 2):
        a2.append([send(ref, ref, device(moved(at, y=k))) for ref in refs_a(None, y, x)])
    ring_z.left_in()
    rings_y[3].start()
    ring_z.right_in()
    rings_y[1].start()
    rings_y[0].both_in()
    rings_x[0].both_in()
    arrive(a2[0])
    rings_x[3].start()
    arrive(a2[1])
    rings_x[1].start()
    ring_z.far_in()
    rings_y[2].start()
    rings_y[3].both_in()
    rings_y[1].both_in()
    arrive(a2[2])
    rings_x[2].start()
    rings_y[0].far_in()
    pass_b(zs[0])
    rings_x[0].far_in()
    pass_a(ys[0])
    rings_x[3].both_in()
    rings_x[1].both_in()
    rings_y[2].both_in()
    rings_x[2].both_in()

    arrive(halo)
    for j in range(6):
        lanes = slice(128 * j, 128 * j + 128)
        rows_f[j, 8:264] = rows_in[:, lanes].astype(F32)
        rows_f[j, 0:8] = jnp.where(sq > 0, before[:, lanes].astype(F32)[8:16], 0.0)
        rows_f[j, 264:272] = jnp.where(sq < 7, after[:, lanes].astype(F32)[0:8], 0.0)
        for i in range(4):
            taps[i, :, lanes] = rows_f[j, pl.ds(7 + i, 128, stride=2)].astype(BF16)

    rings_y[3].far_in()
    pass_b(zs[3])
    rings_y[1].far_in()
    pass_b(zs[1])
    rings_x[3].far_in()
    pass_a(ys[3])
    rings_x[1].far_in()
    pass_a(ys[1])
    rings_y[2].far_in()
    pass_b(zs[2])
    rings_x[2].far_in()
    pass_a(ys[2])

    def transpose_tap(i):
        taps_t[i] = taps[i].T

    loop(4, transpose_tap)
    onehot_t[...] = onehot[...].T
    row = lax.broadcasted_iota(jnp.int32, (768, 1024), 0)
    column = lax.broadcasted_iota(jnp.int32, (768, 1024), 1)
    inside = lax.rem(column, 32)
    choose[...] = ((column // 32 * 24 + inside == row) & (inside < 24)).astype(F32).astype(BF16)
    arrive(core)

    dna_full = do_g[:, :, :, 0:16].reshape(512, 768)
    out_full = do_g[:, :, :, 16:32].reshape(512, 768)
    d_attend = right_dot(upstream[...], out_full).astype(BF16)
    slope[...] = dot(onehot[...], dna_full)

    def one_tap(i):
        slope[...] += dot(taps[i], conv_g[i].reshape(768, 768))

    loop(4, one_tap)
    pre = slope[...]
    bend = jnp.tanh(math.sqrt(2.0 / math.pi) * (pre + 0.044715 * (pre * pre * pre)))
    share = 0.5 * (1.0 + bend)
    feature = (pre * share).astype(BF16).astype(F32)
    slope[...] = share + pre * (0.5 * (1.0 - bend * bend)) * (
        math.sqrt(2.0 / math.pi) * (1.0 + 3.0 * 0.044715 * (pre * pre))
    )
    scale = lax.rsqrt(jnp.mean(feature * feature, axis=1, keepdims=True) + epsilon)
    inverse[...] = scale
    unit[...] = feature * scale
    wide[...] = dot(unit[...].astype(BF16), choose[...]).astype(BF16)
    for i in range(2):
        projected = dot(wide[...], qkv_g[i].reshape(1024, 768)).astype(BF16)
        for piece in range(6):
            kind, head = divmod(6 * i + piece, 4)
            place = (2, 0, 1)[kind] * 128
            mine[head, :, place : place + 128] = projected[:, 128 * piece : 128 * piece + 128]
    for head in range(H):
        mine[head, :, 384:512] = d_attend[:, 128 * head : 128 * head + 128]

    kv, rest = pl.ds(0, 256), pl.ds(256, 256)
    kv_in, rest_in = [], {}
    for p in across:
        kv_in.append(send(mine.at[p["x"], :, kv], got_kv.at[x], device(p)))
    for p in partners:
        kv_in.append(send(mine.at[p["x"], :, kv], got.at[x, :, kv], device(p)))
    for k, p in zip((1, 2, 3), partners):
        rest_in[k] = send(mine.at[p["x"], :, rest], got.at[x, :, rest], device(p))
    got[x] = mine[x]
    wide_t[...] = wide[...].T
    d_kv[...] = jnp.zeros_like(d_kv)
    arrive(kv_in)
    keys = jnp.concatenate([got[:, :, 0:128].reshape(512, 128), got_kv[:, :, 0:128].reshape(512, 128)], axis=0)
    values = jnp.concatenate([got[:, :, 128:256].reshape(512, 128), got_kv[:, :, 128:256].reshape(512, 128)], axis=0)
    scaling = 1.0 / math.sqrt(128)
    home = []
    for k in (0, 1, 3, 2):
        if k:
            arrive([rest_in[k]])
        source = lax.rem(x + 4 - k, 4)
        queries = got[source, :, 256:384]
        upward = got[source, :, 384:512]
        scores = right_dot(queries, keys) * scaling
        powers = jnp.exp(scores - jnp.max(scores, axis=1, keepdims=True))
        probs = powers * (1.0 / jnp.sum(powers, axis=1, keepdims=True))
        probs_low = probs.astype(BF16)
        outgo[source, :, 0:128] = dot(probs_low, values).astype(BF16)
        d_probs = right_dot(upward, values)
        inner = jnp.sum(probs * d_probs, axis=1, keepdims=True)
        d_scores = (probs * (d_probs - inner) * scaling).astype(BF16)
        outgo[source, :, 128:256] = dot(d_scores, keys).astype(BF16)
        if k:
            block = pl.ds(0, 256)
            to = device(moved(at, x=4 - k))
            home.append(send(outgo.at[source, :, block], back.at[x, :, block], to))
        d_kv[:, 0:128] += row_dot(d_scores, queries)
        d_kv[:, 128:256] += row_dot(probs_low, upward)
    outgo_kv[...] = d_kv[512:1024].astype(BF16).reshape(4, 128, 256)
    for p in across:
        home.append(send(outgo_kv.at[p["x"]], back_kv.at[x], device(p)))
    outgo[:, :, 256:512] = d_kv[0:512].astype(BF16).reshape(4, 128, 256)
    for p in partners:
        block = pl.ds(256, 256)
        home.append(send(outgo.at[p["x"], :, block], back.at[x, :, block], device(p)))
    back[x] = outgo[x]
    arrive(home)
    for head in range(H):
        columns = slice(128 * head, 128 * head + 128)
        attended[:, columns] = back[head, :, 0:128]
        d_proj[:, columns] = back[head, :, 128:256]
        for kind in range(2):
            total = back[head, :, 256 + 128 * kind : 384 + 128 * kind].astype(F32) + back_kv[
                head, :, 128 * kind : 128 * kind + 128
            ].astype(F32)
            start = 512 * (kind + 1) + 128 * head
            d_proj[:, start : start + 128] = total.astype(BF16)

    for i in range(2):
        qkv_p[i] = dot(wide_t[...], d_proj[:, 768 * i : 768 * i + 768]).astype(BF16).reshape(4, 4, 2, 32, 768)

    def rows_of(index):
        return index // 2, rows16(lax.rem(index, 2))

    def chunk_cx(index, parity, target):
        part, rows = rows_of(index)
        if parity is None:
            return [target.at[part, :, :, rows, first_half]]
        return [target.at[part, :, :, parity, rows, first_half]]

    def chunk_cy(index, parity, target):
        if parity is None:
            return [target.at[:, :, index, :, second_half]]
        return [target.at[:, :, index, parity, :, second_half]]

    order = (2, 1, 3, 0)
    core_cx, core_cy, core_a, core_b = {}, {}, {}, {}
    for k in order:
        for got_core, chunk, index in ((core_cx, chunk_cx, xs[k]), (core_cy, chunk_cy, ys[k])):
            got_core[k] = [
                send(src, dst, sibling)
                for src, dst in zip(chunk(index, 1 - c, qkv_p), chunk(index, None, qkv_r))
            ]
    d_wide = right_dot(d_proj[:, 0:768], qkv_g[0].reshape(1024, 768)) + right_dot(
        d_proj[:, 768:1536], qkv_g[1].reshape(1024, 768)
    )

    def sum_cx(k):
        arrive(core_cx[k])
        part, rows = rows_of(xs[k])

        def one(i):
            qkv_p[part, i, :, c, rows, 0:384] = add(
                qkv_p, qkv_p[part, i, :, c, rows, 0:384], qkv_r[part, i, :, rows, 0:384]
            )

        loop(4, one)

    def sum_cy(k):
        arrive(core_cy[k])
        index = ys[k]

        def one(i):
            for part in range(2):
                qkv_p[part, i, index, c, :, 384:768] = add(
                    qkv_p, qkv_p[part, i, index, c, :, 384:768], qkv_r[part, i, index, :, 384:768]
                )

        loop(4, one)

    right_x, left_x = device(moved(at, x=1)), device(moved(at, x=3))
    right_y, left_y = device(moved(at, y=1)), device(moved(at, y=3))
    low, high = pl.ds(0, 2), pl.ds(2, 2)
    sum_cx(2)
    far_part, far_rows = rows_of(xs[2])
    far_cx = [
        send(qkv_p.at[far_part, low, :, c, far_rows, first_half], fcx.at[0], right_x),
        send(qkv_p.at[far_part, high, :, c, far_rows, first_half], fcx.at[1], left_x),
    ]
    sum_cy(2)
    far_cy = [
        send(qkv_p.at[0, :, ys[2], c, :, second_half], fcy.at[0], right_y),
        send(qkv_p.at[1, :, ys[2], c, :, second_half], fcy.at[1], left_y),
    ]
    d_high = d_wide.astype(BF16)
    d_low = (d_wide - d_high.astype(F32)).astype(BF16)
    d_normed = right_dot(d_high, choose[...]) + right_dot(d_low, choose[...])
    d_feature = upstream[...].astype(F32) + inverse[...] * (
        d_normed - unit[...] * jnp.mean(d_normed * unit[...], axis=1, keepdims=True)
    )
    d_pre = (d_feature * slope[...]).astype(BF16)

    near_cx, near_cy = [], []
    for side, k in ((0, 1), (1, 3)):
        sum_cx(k)
        arrive([far_cx[side]])
        near_part, near_rows = rows_of(xs[k])

        def join_cx(i, side=side, near_part=near_part, near_rows=near_rows):
            block = qkv_p[near_part, 2 * side + i, :, c, near_rows, 0:384]
            qkv_p[near_part, 2 * side + i, :, c, near_rows, 0:384] = add(qkv_p, block, fcx[side, i])

        loop(2, join_cx)
        to = (right_x, left_x)[side]
        near_cx.append(send(qkv_p.at[near_part, :, :, c, near_rows, first_half], ncx.at[side], to))
        sum_cy(k)
        arrive([far_cy[side]])

        def join_cy(i, side=side, index=ys[k]):
            block = qkv_p[side, i, index, c, :, 384:768]
            qkv_p[side, i, index, c, :, 384:768] = add(qkv_p, block, fcy[side, i])

        loop(4, join_cy)
        to = (right_y, left_y)[side]
        near_cy.append(send(qkv_p.at[:, :, ys[k], c, :, second_half], ncy.at[side], to))

    def one_conv(i):
        conv_p[i] = dot(taps_t[i], d_pre).astype(BF16).reshape(4, 2, 96, 768)

    loop(4, one_conv)
    do_p[:, :, :, 0:16] = dot(onehot_t[...], d_pre).astype(BF16).reshape(4, 4, 2, 16, 768)
    do_p[:, :, :, 16:32] = row_dot(attended[...], upstream[...]).astype(BF16).reshape(4, 4, 2, 16, 768)
    for k in order:
        core_a[k] = [send(conv_p.at[:, :, 1 - c, rows16(xs[k])], conv_r.at[:, :, rows16(xs[k])], sibling)]
        core_b[k] = [
            send(conv_p.at[:, ys[k], 1 - c, tail], conv_r.at[:, ys[k], tail], sibling),
            send(do_p.at[:, ys[k], 1 - c], do_r.at[:, ys[k]], sibling),
        ]

    def sum_a(k):
        arrive(core_a[k])
        rows = rows16(xs[k])

        def one(i):
            conv_p[i, :, c, rows] = add(conv_p, conv_p[i, :, c, rows], conv_r[i, :, rows])

        loop(4, one)

    def sum_b(k):
        arrive(core_b[k])
        index = ys[k]

        def one(i):
            conv_p[i, index, c, 64:96] = add(conv_p, conv_p[i, index, c, 64:96], conv_r[i, index, 64:96])
            do_p[i, index, c] = add(do_p, do_p[i, index, c], do_r[i, index])

        loop(4, one)

    sum_a(2)
    far_a = [
        send(conv_p.at[low, :, c, rows16(xs[2])], fa.at[0], right_x),
        send(conv_p.at[high, :, c, rows16(xs[2])], fa.at[1], left_x),
    ]
    sum_b(2)
    far_b = []
    for side, heights in ((0, low), (1, high)):
        to = (right_y, left_y)[side]
        far_b.append(
            [
                send(conv_p.at[heights, ys[2], c, tail], fb.at[side, :, pl.ds(0, 32)], to),
                send(do_p.at[heights, ys[2], c], fb.at[side, :, pl.ds(32, 32)], to),
            ]
        )
    near_a, near_b = [], []
    for side, k in ((0, 1), (1, 3)):
        sum_a(k)
        sum_b(k)
        arrive([far_a[side]])

        def join_a(i, side=side, rows=rows16(xs[k])):
            block = conv_p[2 * side + i, :, c, rows]
            conv_p[2 * side + i, :, c, rows] = add(conv_p, block, fa[side, i])

        loop(2, join_a)
        to = (right_x, left_x)[side]
        near_a.append(send(conv_p.at[:, :, c, rows16(xs[k])], na.at[side], to))
        arrive(far_b[side])

        def join_b(i, side=side, index=ys[k]):
            i = 2 * side + i
            conv_p[i, index, c, 64:96] = add(conv_p, conv_p[i, index, c, 64:96], fb[side, i - 2 * side, 0:32])
            do_p[i, index, c] = add(do_p, do_p[i, index, c], fb[side, i - 2 * side, 32:64])

        loop(2, join_b)
        to = (right_y, left_y)[side]
        near_b += [
            send(conv_p.at[:, ys[k], c, tail], nb.at[side, :, pl.ds(0, 32)], to),
            send(do_p.at[:, ys[k], c], nb.at[side, :, pl.ds(32, 32)], to),
        ]

    sum_cx(0)
    arrive(near_cx)

    def first_cx(i):
        scx1[i] = add(scx1, qkv_p[part, i, :, c, part_rows, 0:384], ncx[0, i], ncx[1, i])

    loop(4, first_cx)
    cx2 = [send(scx1.at[:, ys[k]], rcx2.at[k - 1], device(moved(at, y=k))) for k in (1, 2, 3)]
    sum_cy(0)
    arrive(near_cy)

    def first_cy(i):
        for part in range(2):
            scy1[part, i] = add(scy1, qkv_p[part, i, y, c, :, 384:768], ncy[0, part, i], ncy[1, part, i])

    loop(4, first_cy)
    cy2 = []
    for k in (1, 2, 3):
        to_part, to_rows = rows_of(xs[k])
        cy2.append(send(scy1.at[to_part, :, to_rows], rcy2.at[k - 1], device(moved(at, x=k))))
    sum_a(0)
    sum_b(0)

    def tap_grad(i):
        return right_dot(d_pre, conv_g[i].reshape(768, 768))

    rows_f[:, 256:272] = jnp.zeros((6, 16, 128), F32)
    for i in range(4):
        terms = tap_grad(i)
        for j in range(6):
            target = pl.ds(7 + i, 128, stride=2)
            block = terms[:, 128 * j : 128 * j + 128]
            rows_f[j, target] = block if i < 2 else rows_f[j, target] + block
    rim_out[0] = rows_f[:, 264:272]
    rim_out[1] = rows_f[:, 0:8]
    rims = [send(rim_out.at[0], rim_before, ahead), send(rim_out.at[1], rim_after, behind)]

    arrive(cx2)
    arrive(cy2)

    def second_c(i):
        sc2[i, :, 0:384] = add(sc2, scx1[i, y], rcx2[0, i], rcx2[1, i], rcx2[2, i])
        sc2[i, :, 384:768] = add(sc2, scy1[part, i, part_rows], rcy2[0, i], rcy2[1, i], rcy2[2, i])

    loop(4, second_c)
    c3 = [send(sc2.at[zs[k]], rc3.at[k - 1], device(moved(at, zh=k))) for k in (1, 2, 3)]

    arrive(near_a)

    def first_a(i):
        sa1[i] = add(sa1, conv_p[i, :, c, rows16(x)], na[0, i], na[1, i])

    loop(4, first_a)
    a2 = [send(sa1.at[:, ys[k]], ra2.at[k - 1], device(moved(at, y=k))) for k in (1, 2, 3)]
    arrive(near_b)

    def first_b(i):
        sb1[i, 0:32] = add(sb1, conv_p[i, y, c, 64:96], nb[0, i, 0:32], nb[1, i, 0:32])
        sb1[i, 32:64] = add(sb1, do_p[i, y, c], nb[0, i, 32:64], nb[1, i, 32:64])

    loop(4, first_b)
    b2 = [send(sb1.at[:, rows16(xs[k])], rb2.at[k - 1], device(moved(at, x=k))) for k in (1, 2, 3)]
    arrive(rims)
    rows_f[:, 8:9] += jnp.where(sq > 0, rim_before[:, 0:1], 0.0)
    rows_f[:, 263:264] += jnp.where(sq < 7, rim_after[:, 7:8], 0.0)
    for j in range(6):
        seq_o[:, 128 * j : 128 * j + 128] = rows_f[j, 8:264].astype(BF16)
    arrive(c3)
    sc3[...] = add(sc3, sc2[zh], rc3[0], rc3[1], rc3[2])
    c4 = send(sc3, rc4, near)
    arrive(a2)

    def second_a(i):
        sa2[i] = add(sa2, sa1[i, y], ra2[0, i], ra2[1, i], ra2[2, i])

    loop(4, second_a)
    a3 = [send(sa2.at[zs[k]], ra3.at[k - 1], device(moved(at, zh=k))) for k in (1, 2, 3)]
    arrive(b2)

    def second_b(i):
        sb2[i] = add(sb2, sb1[i, rows16(x)], rb2[0, i], rb2[1, i], rb2[2, i])

    loop(4, second_b)
    b3 = [send(sb2.at[zs[k]], rb3.at[k - 1], device(moved(at, zh=k))) for k in (1, 2, 3)]
    arrive([c4])
    final[x, 2] = add(final, sc3[...], rc4[...])
    spread = [send(final.at[x, 2], final.at[x, 2], device(moved(at, x=k))) for k in (1, 2, 3)]

    arrive(a3)
    sa3[...] = add(sa3, sa2[zh], ra3[0], ra3[1], ra3[2])
    a4 = send(sa3, ra4, near)
    arrive(b3)
    sb3[...] = add(sb3, sb2[zh], rb3[0], rb3[1], rb3[2])
    b4 = send(sb3, rb4, near)
    arrive([a4])
    final[x, 0] = add(final, sa3[...], ra4[...])
    arrive([b4])
    final[x, 1] = add(final, sb3[...], rb4[...])
    block = final.at[x, pl.ds(0, 2)]
    spread += [send(block, block, device(moved(at, x=k))) for k in (1, 2, 3)]
    arrive(spread)
    send.finish()


def finish_kernel(seq_i, final, seq_o, conv_o, dna_o, qkv_o, out_o):
    seq_o[0] = seq_i[...]
    for q in range(4):
        conv_o[16 * q : 16 * q + 16] = final[q, 0].astype(F32)
    conv_o[64:80] = final[0, 1].astype(F32)
    conv_o[80:96] = final[1, 1].astype(F32)
    dna_o[...] = final[2, 1].astype(F32)
    out_o[...] = final[3, 1].astype(F32)
    qkv_o[0:16, 0:768] = final[0, 2].astype(F32)
    qkv_o[16:24, 0:768] = final[1, 2].astype(F32)[0:8]
    qkv_o[0:16, 768:1536] = final[2, 2].astype(F32)
    qkv_o[16:24, 768:1536] = final[3, 2].astype(F32)[0:8]


def layer(*operands):
    vmem = pl.BlockSpec(memory_space=pltpu.VMEM)
    low = [
        (4, 4, 2, 96, 768), (4, 4, 2, 32, 768), (2, 4, 4, 2, 32, 768), (2, 32, 768), (16, 768), (16, 768),
        (4, 128, 768), (4, 768, 128), (128, 512), (512, 128), (768, 1024), (128, 1024), (1024, 128), (128, 1536), (128, 512),
        (4, 128, 512), (4, 128, 512), (4, 128, 256), (4, 128, 512), (4, 128, 256), (4, 128, 512), (4, 128, 256),
        (4, 4, 2, 96, 768), (4, 4, 2, 32, 768), (2, 4, 4, 2, 32, 768), (4, 4, 96, 768), (4, 4, 32, 768), (2, 4, 4, 32, 768),
        (2, 2, 4, 16, 768), (2, 4, 4, 16, 768), (4, 4, 16, 768), (3, 4, 16, 768), (4, 16, 768), (3, 16, 768), (16, 768), (16, 768),
        (2, 2, 64, 768), (2, 4, 64, 768), (4, 64, 768), (3, 4, 16, 768), (4, 16, 768), (3, 16, 768), (16, 768), (16, 768),
        (2, 2, 4, 16, 384), (2, 4, 4, 16, 384), (4, 4, 16, 384), (3, 4, 16, 384),
        (2, 4, 32, 384), (2, 2, 4, 32, 384), (2, 4, 32, 384), (3, 4, 16, 384),
        (4, 16, 768), (3, 16, 768), (16, 768), (16, 768),
    ]
    wide = [(128, 768), (128, 768), (128, 1), (6, 272, 128), (1024, 256), (2, 6, 8, 128), (6, 8, 128), (6, 8, 128)]
    seq_i, final = pl.pallas_call(
        layer_kernel,
        name="layer",
        out_shape=(jax.ShapeDtypeStruct((256, 768), BF16), jax.ShapeDtypeStruct((4, 3, 16, 768), BF16)),
        in_specs=[vmem] * 7,
        out_specs=(vmem,) * 2,
        scratch_shapes=[pltpu.VMEM(shape, BF16) for shape in low]
        + [pltpu.VMEM(shape, F32) for shape in wide]
        + [pltpu.SemaphoreType.DMA((240,)), pltpu.SemaphoreType.DMA((240,))],
        compiler_params=pltpu.CompilerParams(
            collective_id=1, has_side_effects=True, vmem_limit_bytes=60 * 2**20
        ),
    )(*operands)
    return pl.pallas_call(
        finish_kernel,
        name="finish",
        out_shape=(
            jax.ShapeDtypeStruct((1, 256, 768), BF16),
            jax.ShapeDtypeStruct((96, 768), F32),
            jax.ShapeDtypeStruct((16, 768), F32),
            jax.ShapeDtypeStruct((24, 1536), F32),
            jax.ShapeDtypeStruct((16, 768), F32),
        ),
        in_specs=[vmem] * 2,
        out_specs=(vmem,) * 5,
    )(seq_i, final)


def per_device(seq_in, bases, conv_weight, dna_weight, qkv_weight, out_weight, cotangent):
    return layer(
        conv_weight, dna_weight, qkv_weight, out_weight, seq_in[0], bases[0].reshape(128, BIN), cotangent[0]
    )


def solution(mesh):
    in_specs = (
        P("dp", "seq", None),
        P("dp", "seq"),
        P("dp", None),
        P("dp", None),
        P("dp", None),
        P("dp", None),
        P("dp", "seq", None),
    )
    out_specs = (P("dp", "seq", None), P("dp", None), P("dp", None), P("dp", None), P("dp", None))
    return jax.shard_map(
        per_device, mesh=mesh, in_specs=in_specs, out_specs=out_specs, check_vma=False
    )
```

time: 148 us -> 133 us (0.90)
  local copies, waits for them, and re-layouts: 6.43 us -> 0 us
  Pallas kernels: 139 us -> 133 us
  other arithmetic: 2.07 us -> 0 us
    pallas_call x1, Pallas kernels: 139 us -> 131 us  [layer(): pl.pallas_call(layer_kernel, name='layer', out_shape=(jax.ShapeDtypeStruc...]
    unnamed x14 -> x0, local copies, waits for them, and re-layouts: 2.84 us -> none
    pallas_call x0 -> x1, Pallas kernels: none -> 2.02 us  [layer(): pl.pallas_call(finish_kernel, name='finish', out_shape=(jax.ShapeDtypeStr...]
    reshape x1 -> x0, local copies, waits for them, and re-layouts: 1.92 us -> none  [per_device(): seq_grad.reshape(1, 256, 768)]
    another operation x2 -> x0, local copies, waits for them, and re-layouts: 1.67 us -> none  [the longest x1 0.88 us: per_device(): seq_in[0].reshape(128, 1536)]
where the time goes in v3:
time: 133 us
  Pallas kernels  133 us (100%)
    pallas_call x1, Pallas kernels, layer(): pl.pallas_call(layer_kernel, name='layer', out_shape=(jax.ShapeDtypeStruc...  131 us

profile of v3, /device:TPU:32, one launch (start us, length us, event | category | flops | bytes accessed | tf_op | source)
XLA Modules:
  0.0 133.2 jit_solution(6012757957677951138)
XLA Ops:
  0.6 130.5 %layer.1 = (bf16[256,768]{1,0:T(8,128)(2,1)}, bf16[4,3,16,768]{3,2,1,0:T(8,128)(2,1)}) custom-call(bf16[96,768]{1,0:T(8,128)(2,1)} %conv_s.1, bf16[16,768]{1,0:T(8,128)(2,1)} %dna_s.1, bf16[24,1536]{1,0:T(8,128)(2,1)} %qkv_s.1, bf16[16,768]{1,0:T(8,128)(2,1)} %out_s.1, bf16[256,768]{1,0:T(8,128)(2,1)} %bitcast.3, s32[128,128]{1,0:T(8,128)} %bitcast.5, ...), custom_call_target="tpu_custom_call" | custom-call | tf_op jit(solution)/shard_map/layer/pallas_call | solution.py:683
  131.1 2.0 %finish.1 = (bf16[1,256,768]{2,1,0:T(8,128)(2,1)}, f32[96,768]{1,0:T(8,128)}, f32[16,768]{1,0:T(8,128)}, f32[24,1536]{1,0:T(8,128)}, f32[16,768]{1,0:T(8,128)}) custom-call(bf16[256,768]{1,0:T(8,128)(2,1)} %get-tuple-element.7.seq_i, bf16[4,3,16,768]{3,2,1,0:T(8,128)(2,1)} %get-tuple-element.8.final), custom_call_target="tpu_custom_call" | custom-call | tf_op jit(solution)/shard_map/finish/pallas_call | solution.py:696

commit v4 on v3

--- a/solution.py
+++ b/solution.py
@@ -68,7 +68,7 @@
 
 
 def half_columns(index):
-    return pl.ds(pl.multiple_of(index * 384, 128), 384)
+    return pl.ds(pl.multiple_of(index * 384, 128) if not isinstance(index, int) else index * 384, 384)
 
 
 def right_dot(left, right):
@@ -132,14 +132,15 @@
 
 def layer_kernel(
     conv_s, dna_s, qkv_s, out_s, rows_in, letters, upstream,
-    seq_o, final,
-    conv_g, do_g, qkv_g, qkv_pad, before, after,
-    taps, taps_t, onehot, onehot_t, choose, wide, wide_t, d_proj, attended,
+    seq_o, final, final_x, final_y,
+    conv_g, do_g, qx_g, qy_g, before, after,
+    taps, taps_t, onehot, onehot_t, choose_x, choose_y, wide_x, wide_y, wide_xt, wide_yt, d_proj, attended,
     mine, got, got_kv, outgo, outgo_kv, back, back_kv,
-    conv_p, do_p, qkv_p, conv_r, do_r, qkv_r,
+    conv_p, do_p, qx_p, qy_p, conv_r, do_r, qx_r, qy_r,
     fa, na, sa1, ra2, sa2, ra3, sa3, ra4,
     fb, nb, sb1, rb2, sb2, rb3, sb3, rb4,
-    fcx, ncx, scx1, rcx2, fcy, ncy, scy1, rcy2, sc2, rc3, sc3, rc4,
+    fcx, ncx, scx1, rcx2, scx2, rcx3, scx3, rcx4,
+    fcy, ncy, scy1, rcy2, scy2, rcy3, scy3, rcy4,
     slope, unit, inverse, rows_f, d_kv, rim_out, rim_before, rim_after,
     send_sems, recv_sems,
 ):
@@ -162,18 +163,19 @@
     zs = [lax.rem(zh + k, 4) for k in range(4)]
 
     quarter = rows16(x)
-    part, part_rows = x // 2, rows16(lax.rem(x, 2))
-    tail, first_half, second_half = pl.ds(64, 32), pl.ds(0, 384), pl.ds(384, 384)
-    for i in range(2):
-        block = qkv_s[:, 768 * i : 768 * i + 768].astype(F32)
-        qkv_pad[i] = jnp.concatenate([block, jnp.zeros((8, 768), F32)], axis=0).astype(BF16)
+    tail = pl.ds(64, 32)
+
+    def corner(index):
+        return index // 2, half_columns(lax.rem(index, 2))
+
+    part, part_columns = corner(x)
     conv_g[zh, y, c, quarter] = conv_s[quarter]
     conv_g[zh, y, c, 64:96] = conv_s[64:96]
     do_g[zh, y, c, 0:16] = dna_s[...]
     do_g[zh, y, c, 16:32] = out_s[...]
-    qkv_g[part, zh, y, c, part_rows, 0:384] = qkv_pad[part, part_rows, 0:384]
-    for i in range(2):
-        qkv_g[i, zh, y, c, :, 384:768] = qkv_pad[i, :, 384:768]
+    qx_g[part, zh, y, c, :, part_columns] = qkv_s[0:16, half_columns(x)]
+    last_rows = [qkv_s[:, 768 * i : 768 * i + 768].astype(F32)[16:24] for i in range(2)]
+    qy_g[zh, y, c] = jnp.concatenate(last_rows, axis=0).astype(BF16)
     row = lax.broadcasted_iota(jnp.int32, (128, 512), 0)
     column = lax.broadcasted_iota(jnp.int32, (128, 512), 1)
     repeat = (column // 4 == row).astype(F32).astype(BF16)
@@ -188,7 +190,7 @@
         rows = rows if height is None else height
         return [
             conv_g.at[rows, step, c, rows16(index)],
-            qkv_g.at[index // 2, rows, step, c, rows16(lax.rem(index, 2)), first_half],
+            qx_g.at[corner(index)[0], rows, step, c, :, corner(index)[1]],
         ]
 
     def refs_b(height, step, part=None):
@@ -196,12 +198,12 @@
             return [
                 conv_g.at[height, step, c, tail],
                 do_g.at[height, step, c],
-                qkv_g.at[:, height, step, c, :, second_half],
+                qy_g.at[height, step, c],
             ]
         return [
             conv_g.at[height, step, c, pl.ds(64 + 16 * part, 16)],
             do_g.at[height, step, c, pl.ds(16 * part, 16)],
-            qkv_g.at[part, height, step, c, :, second_half],
+            qy_g.at[height, step, c, :, half_columns(part)],
         ]
 
     core = []
@@ -211,12 +213,12 @@
             core.append(send(ref, ref, sibling))
 
     def pass_a(step):
-        pass_on([conv_g.at[:, step, c, pl.ds(0, 64)], qkv_g.at[:, :, step, c, :, first_half]])
+        pass_on([conv_g.at[:, step, c, pl.ds(0, 64)], qx_g.at[:, :, step, c]])
 
     def pass_b(height):
-        pass_on([conv_g.at[height, :, c, tail], do_g.at[height, :, c], qkv_g.at[:, height, :, c, :, second_half]])
-
-    a1, a2 = [], []
+        pass_on([conv_g.at[height, :, c, tail], do_g.at[height, :, c], qy_g.at[height, :, c]])
+
+    a1 = []
     for k in (1, 3, 2):
         a1 += [send(ref, ref, device(moved(at, zh=k))) for ref in refs_a(zh, y, x)]
     halo = [
@@ -226,27 +228,27 @@
     ring_z = Ring(send, at, "zh", lambda index, part: refs_b(index, y, part))
     rings_y = [Ring(send, at, "y", lambda index, part, v=zs[k]: refs_b(v, index, part)) for k in range(4)]
     rings_x = [Ring(send, at, "x", lambda index, part, v=ys[k]: refs_a(None, v, index, part)) for k in range(4)]
+    ring_a = Ring(send, at, "y", lambda index, part: refs_a(None, index, x, part))
     ring_z.start()
     rings_y[0].start()
     arrive(a1)
     rings_x[0].start()
-    for k in (1, 3, 2):
-        a2.append([send(ref, ref, device(moved(at, y=k))) for ref in refs_a(None, y, x)])
+    ring_a.start()
     ring_z.left_in()
     rings_y[3].start()
     ring_z.right_in()
     rings_y[1].start()
     rings_y[0].both_in()
+    ring_a.left_in()
+    rings_x[3].start()
+    ring_a.right_in()
+    rings_x[1].start()
     rings_x[0].both_in()
-    arrive(a2[0])
-    rings_x[3].start()
-    arrive(a2[1])
-    rings_x[1].start()
     ring_z.far_in()
     rings_y[2].start()
     rings_y[3].both_in()
     rings_y[1].both_in()
-    arrive(a2[2])
+    ring_a.far_in()
     rings_x[2].start()
     rings_y[0].far_in()
     pass_b(zs[0])
@@ -284,16 +286,18 @@
 
     loop(4, transpose_tap)
     onehot_t[...] = onehot[...].T
-    row = lax.broadcasted_iota(jnp.int32, (768, 1024), 0)
-    column = lax.broadcasted_iota(jnp.int32, (768, 1024), 1)
-    inside = lax.rem(column, 32)
-    choose[...] = ((column // 32 * 24 + inside == row) & (inside < 24)).astype(F32).astype(BF16)
-    arrive(core)
+    row = lax.broadcasted_iota(jnp.int32, (768, 512), 0)
+    column = lax.broadcasted_iota(jnp.int32, (768, 512), 1)
+    first_row = column // 16 * 24
+    choose_x[...] = (first_row + lax.rem(column, 16) == row).astype(F32).astype(BF16)
+    choose_y[...] = (first_row + 16 + lax.rem(column, 8) == row).astype(F32).astype(BF16)
+    arrive(core[:-2])
 
     dna_full = do_g[:, :, :, 0:16].reshape(512, 768)
     out_full = do_g[:, :, :, 16:32].reshape(512, 768)
     d_attend = right_dot(upstream[...], out_full).astype(BF16)
     slope[...] = dot(onehot[...], dna_full)
+    arrive(core[-2:])
 
     def one_tap(i):
         slope[...] += dot(taps[i], conv_g[i].reshape(768, 768))
@@ -309,9 +313,13 @@
     scale = lax.rsqrt(jnp.mean(feature * feature, axis=1, keepdims=True) + epsilon)
     inverse[...] = scale
     unit[...] = feature * scale
-    wide[...] = dot(unit[...].astype(BF16), choose[...]).astype(BF16)
+    normed = unit[...].astype(BF16)
+    wide_x[...] = dot(normed, choose_x[...]).astype(BF16)
+    wide_y[...] = dot(normed, choose_y[...]).astype(BF16)
+    side_of = lax.rem(lax.broadcasted_iota(jnp.int32, (128, 512), 1), 16) // 8
     for i in range(2):
-        projected = dot(wide[...], qkv_g[i].reshape(1024, 768)).astype(BF16)
+        own_y = jnp.where(side_of == i, wide_y[...].astype(F32), 0.0).astype(BF16)
+        projected = (dot(wide_x[...], qx_g[i].reshape(512, 768)) + dot(own_y, qy_g[...].reshape(512, 768))).astype(BF16)
         for piece in range(6):
             kind, head = divmod(6 * i + piece, 4)
             place = (2, 0, 1)[kind] * 128
@@ -328,7 +336,8 @@
     for k, p in zip((1, 2, 3), partners):
         rest_in[k] = send(mine.at[p["x"], :, rest], got.at[x, :, rest], device(p))
     got[x] = mine[x]
-    wide_t[...] = wide[...].T
+    wide_xt[...] = wide_x[...].T
+    wide_yt[...] = wide_y[...].T
     d_kv[...] = jnp.zeros_like(d_kv)
     arrive(kv_in)
     keys = jnp.concatenate([got[:, :, 0:128].reshape(512, 128), got_kv[:, :, 0:128].reshape(512, 128)], axis=0)
@@ -376,103 +385,63 @@
             start = 512 * (kind + 1) + 128 * head
             d_proj[:, start : start + 128] = total.astype(BF16)
 
+    d_halves = [d_proj[:, 0:768], d_proj[:, 768:1536]]
     for i in range(2):
-        qkv_p[i] = dot(wide_t[...], d_proj[:, 768 * i : 768 * i + 768]).astype(BF16).reshape(4, 4, 2, 32, 768)
-
-    def rows_of(index):
-        return index // 2, rows16(lax.rem(index, 2))
-
-    def chunk_cx(index, parity, target):
-        part, rows = rows_of(index)
-        if parity is None:
-            return [target.at[part, :, :, rows, first_half]]
-        return [target.at[part, :, :, parity, rows, first_half]]
-
-    def chunk_cy(index, parity, target):
-        if parity is None:
-            return [target.at[:, :, index, :, second_half]]
-        return [target.at[:, :, index, parity, :, second_half]]
+        qx_p[i] = dot(wide_xt[...], d_halves[i]).astype(BF16).reshape(4, 4, 2, 16, 768)
+    row_side = lax.rem(lax.broadcasted_iota(jnp.int32, (512, 768), 0), 16)
+    both = [dot(wide_yt[...], d_half) for d_half in d_halves]
+    qy_p[...] = jnp.where(row_side < 8, both[0], both[1]).astype(BF16).reshape(4, 4, 2, 16, 768)
 
     order = (2, 1, 3, 0)
     core_cx, core_cy, core_a, core_b = {}, {}, {}, {}
     for k in order:
-        for got_core, chunk, index in ((core_cx, chunk_cx, xs[k]), (core_cy, chunk_cy, ys[k])):
-            got_core[k] = [
-                send(src, dst, sibling)
-                for src, dst in zip(chunk(index, 1 - c, qkv_p), chunk(index, None, qkv_r))
-            ]
-    d_wide = right_dot(d_proj[:, 0:768], qkv_g[0].reshape(1024, 768)) + right_dot(
-        d_proj[:, 768:1536], qkv_g[1].reshape(1024, 768)
-    )
+        to_part, to_columns = corner(xs[k])
+        core_cx[k] = send(
+            qx_p.at[to_part, :, :, 1 - c, :, to_columns], qx_r.at[to_part, :, :, :, to_columns], sibling
+        )
+        core_cy[k] = send(qy_p.at[:, ys[k], 1 - c], qy_r.at[:, ys[k]], sibling)
+    d_x = sum(right_dot(d_halves[i], qx_g[i].reshape(512, 768)) for i in range(2))
+    both = [right_dot(d_half, qy_g[...].reshape(512, 768)) for d_half in d_halves]
+    d_y = jnp.where(side_of == 0, both[0], both[1])
 
     def sum_cx(k):
-        arrive(core_cx[k])
-        part, rows = rows_of(xs[k])
+        arrive([core_cx[k]])
+        own_part, own_columns = corner(xs[k])
 
         def one(i):
-            qkv_p[part, i, :, c, rows, 0:384] = add(
-                qkv_p, qkv_p[part, i, :, c, rows, 0:384], qkv_r[part, i, :, rows, 0:384]
+            qx_p[own_part, i, :, c, :, own_columns] = add(
+                qx_p, qx_p[own_part, i, :, c, :, own_columns], qx_r[own_part, i, :, :, own_columns]
             )
 
         loop(4, one)
 
     def sum_cy(k):
-        arrive(core_cy[k])
-        index = ys[k]
-
-        def one(i):
-            for part in range(2):
-                qkv_p[part, i, index, c, :, 384:768] = add(
-                    qkv_p, qkv_p[part, i, index, c, :, 384:768], qkv_r[part, i, index, :, 384:768]
-                )
-
-        loop(4, one)
+        arrive([core_cy[k]])
+        qy_p[:, ys[k], c] = add(qy_p, qy_p[:, ys[k], c], qy_r[:, ys[k]])
 
     right_x, left_x = device(moved(at, x=1)), device(moved(at, x=3))
     right_y, left_y = device(moved(at, y=1)), device(moved(at, y=3))
     low, high = pl.ds(0, 2), pl.ds(2, 2)
     sum_cx(2)
-    far_part, far_rows = rows_of(xs[2])
+    far_part, far_columns = corner(xs[2])
     far_cx = [
-        send(qkv_p.at[far_part, low, :, c, far_rows, first_half], fcx.at[0], right_x),
-        send(qkv_p.at[far_part, high, :, c, far_rows, first_half], fcx.at[1], left_x),
+        send(qx_p.at[far_part, low, :, c, :, far_columns], fcx.at[0], right_x),
+        send(qx_p.at[far_part, high, :, c, :, far_columns], fcx.at[1], left_x),
     ]
     sum_cy(2)
     far_cy = [
-        send(qkv_p.at[0, :, ys[2], c, :, second_half], fcy.at[0], right_y),
-        send(qkv_p.at[1, :, ys[2], c, :, second_half], fcy.at[1], left_y),
+        send(qy_p.at[low, ys[2], c], fcy.at[0], right_y),
+        send(qy_p.at[high, ys[2], c], fcy.at[1], left_y),
     ]
-    d_high = d_wide.astype(BF16)
-    d_low = (d_wide - d_high.astype(F32)).astype(BF16)
-    d_normed = right_dot(d_high, choose[...]) + right_dot(d_low, choose[...])
+    d_normed = 0.0
+    for terms, choose in ((d_x, choose_x), (d_y, choose_y)):
+        d_high = terms.astype(BF16)
+        d_low = (terms - d_high.astype(F32)).astype(BF16)
+        d_normed += right_dot(d_high, choose[...]) + right_dot(d_low, choose[...])
     d_feature = upstream[...].astype(F32) + inverse[...] * (
         d_normed - unit[...] * jnp.mean(d_normed * unit[...], axis=1, keepdims=True)
     )
     d_pre = (d_feature * slope[...]).astype(BF16)
-
-    near_cx, near_cy = [], []
-    for side, k in ((0, 1), (1, 3)):
-        sum_cx(k)
-        arrive([far_cx[side]])
-        near_part, near_rows = rows_of(xs[k])
-
-        def join_cx(i, side=side, near_part=near_part, near_rows=near_rows):
-            block = qkv_p[near_part, 2 * side + i, :, c, near_rows, 0:384]
-            qkv_p[near_part, 2 * side + i, :, c, near_rows, 0:384] = add(qkv_p, block, fcx[side, i])
-
-        loop(2, join_cx)
-        to = (right_x, left_x)[side]
-        near_cx.append(send(qkv_p.at[near_part, :, :, c, near_rows, first_half], ncx.at[side], to))
-        sum_cy(k)
-        arrive([far_cy[side]])
-
-        def join_cy(i, side=side, index=ys[k]):
-            block = qkv_p[side, i, index, c, :, 384:768]
-            qkv_p[side, i, index, c, :, 384:768] = add(qkv_p, block, fcy[side, i])
-
-        loop(4, join_cy)
-        to = (right_y, left_y)[side]
-        near_cy.append(send(qkv_p.at[:, :, ys[k], c, :, second_half], ncy.at[side], to))
 
     def one_conv(i):
         conv_p[i] = dot(taps_t[i], d_pre).astype(BF16).reshape(4, 2, 96, 768)
@@ -505,6 +474,26 @@
             do_p[i, index, c] = add(do_p, do_p[i, index, c], do_r[i, index])
 
         loop(4, one)
+
+    near_cx, near_cy = [], []
+    for side, k in ((0, 1), (1, 3)):
+        sum_cx(k)
+        arrive([far_cx[side]])
+        near_part, near_columns = corner(xs[k])
+
+        def join_cx(i, side=side, near_part=near_part, near_columns=near_columns):
+            block = qx_p[near_part, 2 * side + i, :, c, :, near_columns]
+            qx_p[near_part, 2 * side + i, :, c, :, near_columns] = add(qx_p, block, fcx[side, i])
+
+        loop(2, join_cx)
+        to = (right_x, left_x)[side]
+        near_cx.append(send(qx_p.at[near_part, :, :, c, :, near_columns], ncx.at[side], to))
+        sum_cy(k)
+        arrive([far_cy[side]])
+        half = slice(2 * side, 2 * side + 2)
+        qy_p[half, ys[k], c] = add(qy_p, qy_p[half, ys[k], c], fcy[side])
+        to = (right_y, left_y)[side]
+        near_cy.append(send(qy_p.at[:, ys[k], c], ncy.at[side], to))
 
     sum_a(2)
     far_a = [
@@ -552,22 +541,14 @@
     arrive(near_cx)
 
     def first_cx(i):
-        scx1[i] = add(scx1, qkv_p[part, i, :, c, part_rows, 0:384], ncx[0, i], ncx[1, i])
+        scx1[i] = add(scx1, qx_p[part, i, :, c, :, part_columns], ncx[0, i], ncx[1, i])
 
     loop(4, first_cx)
     cx2 = [send(scx1.at[:, ys[k]], rcx2.at[k - 1], device(moved(at, y=k))) for k in (1, 2, 3)]
     sum_cy(0)
     arrive(near_cy)
-
-    def first_cy(i):
-        for part in range(2):
-            scy1[part, i] = add(scy1, qkv_p[part, i, y, c, :, 384:768], ncy[0, part, i], ncy[1, part, i])
-
-    loop(4, first_cy)
-    cy2 = []
-    for k in (1, 2, 3):
-        to_part, to_rows = rows_of(xs[k])
-        cy2.append(send(scy1.at[to_part, :, to_rows], rcy2.at[k - 1], device(moved(at, x=k))))
+    scy1[...] = add(scy1, qy_p[:, y, c], ncy[0], ncy[1])
+    cy2 = [send(scy1.at[zs[k]], rcy2.at[k - 1], device(moved(at, zh=k))) for k in (1, 2, 3)]
     sum_a(0)
     sum_b(0)
 
@@ -586,14 +567,15 @@
     rims = [send(rim_out.at[0], rim_before, ahead), send(rim_out.at[1], rim_after, behind)]
 
     arrive(cx2)
+
+    def second_cx(i):
+        scx2[i] = add(scx2, scx1[i, y], rcx2[0, i], rcx2[1, i], rcx2[2, i])
+
+    loop(4, second_cx)
+    cx3 = [send(scx2.at[zs[k]], rcx3.at[k - 1], device(moved(at, zh=k))) for k in (1, 2, 3)]
     arrive(cy2)
-
-    def second_c(i):
-        sc2[i, :, 0:384] = add(sc2, scx1[i, y], rcx2[0, i], rcx2[1, i], rcx2[2, i])
-        sc2[i, :, 384:768] = add(sc2, scy1[part, i, part_rows], rcy2[0, i], rcy2[1, i], rcy2[2, i])
-
-    loop(4, second_c)
-    c3 = [send(sc2.at[zs[k]], rc3.at[k - 1], device(moved(at, zh=k))) for k in (1, 2, 3)]
+    scy2[...] = add(scy2, scy1[zh], rcy2[0], rcy2[1], rcy2[2])
+    cy3 = send(scy2, rcy3, near)
 
     arrive(near_a)
 
@@ -615,9 +597,12 @@
     rows_f[:, 263:264] += jnp.where(sq < 7, rim_after[:, 7:8], 0.0)
     for j in range(6):
         seq_o[:, 128 * j : 128 * j + 128] = rows_f[j, 8:264].astype(BF16)
-    arrive(c3)
-    sc3[...] = add(sc3, sc2[zh], rc3[0], rc3[1], rc3[2])
-    c4 = send(sc3, rc4, near)
+    arrive(cx3)
+    scx3[...] = add(scx3, scx2[zh], rcx3[0], rcx3[1], rcx3[2])
+    cx4 = send(scx3, rcx4, near)
+    arrive([cy3])
+    scy3[...] = add(scy3, scy2[...], rcy3[...])
+    cy4 = [send(scy3, rcy4.at[k - 1], device(moved(at, x=k))) for k in (1, 2, 3)]
     arrive(a2)
 
     def second_a(i):
@@ -632,9 +617,11 @@
 
     loop(4, second_b)
     b3 = [send(sb2.at[zs[k]], rb3.at[k - 1], device(moved(at, zh=k))) for k in (1, 2, 3)]
-    arrive([c4])
-    final[x, 2] = add(final, sc3[...], rc4[...])
-    spread = [send(final.at[x, 2], final.at[x, 2], device(moved(at, x=k))) for k in (1, 2, 3)]
+    arrive([cx4])
+    final_x[x] = add(final_x, scx3[...], rcx4[...])
+    spread = [send(final_x.at[x], final_x.at[x], device(moved(at, x=k))) for k in (1, 2, 3)]
+    arrive(cy4)
+    final_y[...] = add(final_y, scy3[...], rcy4[0], rcy4[1], rcy4[2])
 
     arrive(a3)
     sa3[...] = add(sa3, sa2[zh], ra3[0], ra3[1], ra3[2])
@@ -646,13 +633,12 @@
     final[x, 0] = add(final, sa3[...], ra4[...])
     arrive([b4])
     final[x, 1] = add(final, sb3[...], rb4[...])
-    block = final.at[x, pl.ds(0, 2)]
-    spread += [send(block, block, device(moved(at, x=k))) for k in (1, 2, 3)]
+    spread += [send(final.at[x], final.at[x], device(moved(at, x=k))) for k in (1, 2, 3)]
     arrive(spread)
     send.finish()
 
 
-def finish_kernel(seq_i, final, seq_o, conv_o, dna_o, qkv_o, out_o):
+def finish_kernel(seq_i, final, final_x, final_y, seq_o, conv_o, dna_o, qkv_o, out_o):
     seq_o[0] = seq_i[...]
     for q in range(4):
         conv_o[16 * q : 16 * q + 16] = final[q, 0].astype(F32)
@@ -660,35 +646,40 @@
     conv_o[80:96] = final[1, 1].astype(F32)
     dna_o[...] = final[2, 1].astype(F32)
     out_o[...] = final[3, 1].astype(F32)
-    qkv_o[0:16, 0:768] = final[0, 2].astype(F32)
-    qkv_o[16:24, 0:768] = final[1, 2].astype(F32)[0:8]
-    qkv_o[0:16, 768:1536] = final[2, 2].astype(F32)
-    qkv_o[16:24, 768:1536] = final[3, 2].astype(F32)[0:8]
+    for q in range(4):
+        qkv_o[0:16, 384 * q : 384 * q + 384] = final_x[q].astype(F32)
+    last_rows = final_y[...].astype(F32)
+    qkv_o[16:24, 0:768] = last_rows[0:8]
+    qkv_o[16:24, 768:1536] = last_rows[8:16]
 
 
 def layer(*operands):
     vmem = pl.BlockSpec(memory_space=pltpu.VMEM)
     low = [
-        (4, 4, 2, 96, 768), (4, 4, 2, 32, 768), (2, 4, 4, 2, 32, 768), (2, 32, 768), (16, 768), (16, 768),
-        (4, 128, 768), (4, 768, 128), (128, 512), (512, 128), (768, 1024), (128, 1024), (1024, 128), (128, 1536), (128, 512),
+        (4, 4, 2, 96, 768), (4, 4, 2, 32, 768), (2, 4, 4, 2, 16, 768), (4, 4, 2, 16, 768), (16, 768), (16, 768),
+        (4, 128, 768), (4, 768, 128), (128, 512), (512, 128), (768, 512), (768, 512),
+        (128, 512), (128, 512), (512, 128), (512, 128), (128, 1536), (128, 512),
         (4, 128, 512), (4, 128, 512), (4, 128, 256), (4, 128, 512), (4, 128, 256), (4, 128, 512), (4, 128, 256),
-        (4, 4, 2, 96, 768), (4, 4, 2, 32, 768), (2, 4, 4, 2, 32, 768), (4, 4, 96, 768), (4, 4, 32, 768), (2, 4, 4, 32, 768),
+        (4, 4, 2, 96, 768), (4, 4, 2, 32, 768), (2, 4, 4, 2, 16, 768), (4, 4, 2, 16, 768),
+        (4, 4, 96, 768), (4, 4, 32, 768), (2, 4, 4, 16, 768), (4, 4, 16, 768),
         (2, 2, 4, 16, 768), (2, 4, 4, 16, 768), (4, 4, 16, 768), (3, 4, 16, 768), (4, 16, 768), (3, 16, 768), (16, 768), (16, 768),
         (2, 2, 64, 768), (2, 4, 64, 768), (4, 64, 768), (3, 4, 16, 768), (4, 16, 768), (3, 16, 768), (16, 768), (16, 768),
-        (2, 2, 4, 16, 384), (2, 4, 4, 16, 384), (4, 4, 16, 384), (3, 4, 16, 384),
-        (2, 4, 32, 384), (2, 2, 4, 32, 384), (2, 4, 32, 384), (3, 4, 16, 384),
-        (4, 16, 768), (3, 16, 768), (16, 768), (16, 768),
+        (2, 2, 4, 16, 384), (2, 4, 4, 16, 384), (4, 4, 16, 384), (3, 4, 16, 384), (4, 16, 384), (3, 16, 384), (16, 384), (16, 384),
+        (2, 2, 16, 768), (2, 4, 16, 768), (4, 16, 768), (3, 16, 768), (16, 768), (16, 768), (16, 768), (3, 16, 768),
     ]
     wide = [(128, 768), (128, 768), (128, 1), (6, 272, 128), (1024, 256), (2, 6, 8, 128), (6, 8, 128), (6, 8, 128)]
-    seq_i, final = pl.pallas_call(
+    results = pl.pallas_call(
         layer_kernel,
         name="layer",
-        out_shape=(jax.ShapeDtypeStruct((256, 768), BF16), jax.ShapeDtypeStruct((4, 3, 16, 768), BF16)),
+        out_shape=tuple(
+            jax.ShapeDtypeStruct(shape, BF16)
+            for shape in ((256, 768), (4, 2, 16, 768), (4, 16, 384), (16, 768))
+        ),
         in_specs=[vmem] * 7,
-        out_specs=(vmem,) * 2,
+        out_specs=(vmem,) * 4,
         scratch_shapes=[pltpu.VMEM(shape, BF16) for shape in low]
         + [pltpu.VMEM(shape, F32) for shape in wide]
-        + [pltpu.SemaphoreType.DMA((240,)), pltpu.SemaphoreType.DMA((240,))],
+        + [pltpu.SemaphoreType.DMA((250,)), pltpu.SemaphoreType.DMA((250,))],
         compiler_params=pltpu.CompilerParams(
             collective_id=1, has_side_effects=True, vmem_limit_bytes=60 * 2**20
         ),
@@ -703,9 +694,9 @@
             jax.ShapeDtypeStruct((24, 1536), F32),
             jax.ShapeDtypeStruct((16, 768), F32),
         ),
-        in_specs=[vmem] * 2,
+        in_specs=[vmem] * 4,
         out_specs=(vmem,) * 5,
-    )(seq_i, final)
+    )(*results)
 
 
 def per_device(seq_in, bases, conv_weight, dna_weight, qkv_weight, out_weight, cotangent):

time: 133 us -> 130 us (0.977)
  Pallas kernels: 133 us -> 129 us
    pallas_call x1, Pallas kernels: 131 us -> 127 us  [layer(): pl.pallas_call(layer_kernel, name='layer', out_shape=tuple((jax.ShapeDtyp...]
where the time goes in v4:
time: 130 us
  Pallas kernels  129 us (99%)
    pallas_call x1, Pallas kernels, layer(): pl.pallas_call(layer_kernel, name='layer', out_shape=tuple((jax.ShapeDtyp...  127 us

profile of v4, /device:TPU:32, one launch (start us, length us, event | category | flops | bytes accessed | tf_op | source)
XLA Modules:
  0.0 130.1 jit_solution(639250030249651832)
XLA Ops:
  0.6 127.5 %layer.1 = (bf16[256,768]{1,0:T(8,128)(2,1)}, bf16[4,2,16,768]{3,2,1,0:T(8,128)(2,1)}, bf16[4,16,384]{2,1,0:T(8,128)(2,1)}, bf16[16,768]{1,0:T(8,128)(2,1)}) custom-call(bf16[96,768]{1,0:T(8,128)(2,1)} %conv_s.1, bf16[16,768]{1,0:T(8,128)(2,1)} %dna_s.1, bf16[24,1536]{1,0:T(8,128)(2,1)} %qkv_s.1, bf16[16,768]{1,0:T(8,128)(2,1)} %out_s.1, ...), custom_call_target="tpu_custom_call" | custom-call | tf_op jit(solution)/shard_map/layer/pallas_call | solution.py:671
  128.1 2.0 %finish.1 = (bf16[1,256,768]{2,1,0:T(8,128)(2,1)}, f32[96,768]{1,0:T(8,128)}, f32[16,768]{1,0:T(8,128)}, f32[24,1536]{1,0:T(8,128)}, f32[16,768]{1,0:T(8,128)}) custom-call(bf16[256,768]{1,0:T(8,128)(2,1)} %get-tuple-element.9.seq_i, bf16[4,2,16,768]{3,2,1,0:T(8,128)(2,1)} %get-tuple-element.10.final, bf16[4,16,384]{2,1,0:T(8,128)(2,1)} %get-tuple-element.11.final_x, ...), custom_call_target="tpu_custom_call" | custom-call | tf_op jit(solution)/shard_map/finish/pallas_call | solution.py:687

commit v5 on v4

v5 whole, which is shorter than its diff:
```python
import math

import jax
import jax.numpy as jnp
from jax import lax
from jax.experimental import pallas as pl
from jax.experimental.pallas import tpu as pltpu
from jax.sharding import PartitionSpec as P

H = 4
BIN = 128
BF16 = jnp.bfloat16
F32 = jnp.float32
MESH = pl.DeviceIdType.MESH
epsilon = 1e-06

SIZES = {"zh": 4, "y": 4, "c": 2, "zl": 2, "x": 4}
PEERS = [(a, k) for a in ("zh", "y", "x") for k in (1, 2, 3)] + [("zl", 1), ("c", 1)]


def here():
    dp = lax.axis_index("dp")
    sq = lax.axis_index("seq")
    return {"zh": dp // 8, "y": lax.rem(dp // 2, 4), "c": lax.rem(dp, 2), "zl": sq // 4, "x": lax.rem(sq, 4)}


def moved(at, **steps):
    to = dict(at)
    for axis, step in steps.items():
        to[axis] = lax.rem(at[axis] + step, SIZES[axis])
    return to


def device(at):
    return (at["zh"] * 8 + at["y"] * 2 + at["c"], at["zl"] * 4 + at["x"])


class Sender:
    def __init__(self, send_sems, recv_sems):
        self.send_sems, self.recv_sems, self.sent, self.due, self.copies = send_sems, recv_sems, 0, 0, []

    def copy(self, src, dst, to, recv):
        copy = pltpu.make_async_remote_copy(
            src_ref=src,
            dst_ref=dst,
            send_sem=self.send_sems.at[self.sent],
            recv_sem=self.recv_sems.at[recv],
            device_id=to,
            device_id_type=MESH,
        )
        copy.start()
        self.sent += 1
        self.copies.append(copy)
        return copy

    def __call__(self, src, dst, to):
        self.due += 1
        return self.copy(src, dst, to, self.due - 1)

    def group(self, whole, copies):
        self.due += 1
        for src, dst, to in copies:
            self.copy(src, dst, to, self.due - 1)
        return pltpu.make_async_remote_copy(
            src_ref=whole,
            dst_ref=whole,
            send_sem=self.send_sems.at[0],
            recv_sem=self.recv_sems.at[self.due - 1],
            device_id=copies[0][2],
            device_id_type=MESH,
        )

    def finish(self):
        for copy in self.copies:
            copy.wait_send()
        self.sent, self.copies = 0, []


def arrive(copies):
    for copy in copies:
        copy.wait_recv()


def rows16(index, base=0):
    return pl.ds(pl.multiple_of(index * 16 + base, 16), 16)


def half_columns(index):
    return pl.ds(pl.multiple_of(index * 384, 128) if not isinstance(index, int) else index * 384, 384)


def right_dot(left, right):
    return lax.dot_general(left, right, (((1,), (1,)), ((), ())), preferred_element_type=F32)


def row_dot(left, right):
    return lax.dot_general(left, right, (((0,), (0,)), ((), ())), preferred_element_type=F32)


def dot(left, right):
    return jnp.dot(left, right, preferred_element_type=F32)


def add(target, *terms):
    total = terms[0].astype(F32)
    for term in terms[1:]:
        total += term.astype(F32)
    return total.astype(target.dtype)


def loop(n, body):
    def step(i, carry):
        body(i)
        return carry

    lax.fori_loop(0, n, step, 0)


class Ring:
    def __init__(self, send, at, axis, region):
        self.send, self.me, self.region = send, at[axis], region
        self.right, self.left = device(moved(at, **{axis: 1})), device(moved(at, **{axis: 3}))

    def at(self, step):
        return lax.rem(self.me + step, 4)

    def go(self, index, part, to):
        ref = self.region(index, part)
        return [self.send(ref, ref, to)]

    def start(self):
        self.from_left = self.go(self.me, None, self.right)
        self.from_right = self.go(self.me, None, self.left)

    def left_in(self):
        arrive(self.from_left)
        self.far_left = self.go(self.at(3), 0, self.right)

    def right_in(self):
        arrive(self.from_right)
        self.far_right = self.go(self.at(1), 1, self.left)

    def both_in(self):
        self.left_in()
        self.right_in()

    def far_in(self):
        arrive(self.far_left)
        arrive(self.far_right)


def layer_kernel(
    conv_s, dna_s, qkv_s, out_s, rows_in, letters, upstream,
    seq_o, final, final_x, final_y,
    ga, gb, before, after,
    taps, taps_t, onehot, onehot_t, choose_x, choose_y, wide_x, wide_y, wide_xt, wide_yt, d_proj, attended, attended_t,
    mine, got, got_kv, outgo, outgo_kv, back, back_kv, probs_s, scores_s,
    pa_s, pb_s, px_s, py_s, pa, pb, px, py, pa_r, pb_r, px_r, py_r,
    fa, na, sa1, ra2, sa2, ra3, sa3, ra4,
    fb, nb, sb1, rb2, sb2, rb3, sb3, rb4,
    fcx, ncx, scx1, rcx2, scx2, rcx3, scx3, rcx4,
    fcy, ncy, scy1, rcy2, scy2, rcy3, scy3, rcy4,
    slope, unit, inverse, rows_f, rim_out, rim_before, rim_after,
    send_sems, recv_sems,
):
    at = here()
    zh, y, c, zl, x = (at[a] for a in ("zh", "y", "c", "zl", "x"))
    sq = lax.axis_index("seq")
    dp = lax.axis_index("dp")
    behind, ahead = (dp, lax.rem(sq + 7, 8)), (dp, lax.rem(sq + 1, 8))
    sibling = device(moved(at, c=1))
    near = device(moved(at, zl=1))
    partners = [moved(at, x=k) for k in (1, 2, 3)]
    across = [moved(at, x=k, zl=1) for k in range(4)]
    everyone = [device(moved(at, **{a: k})) for a, k in PEERS] + [behind, ahead]
    everyone += [device(p) for p in across[1:]]
    barrier = pltpu.get_barrier_semaphore()
    for one in everyone:
        pl.semaphore_signal(barrier, inc=1, device_id=one, device_id_type=MESH)
    xs = [lax.rem(x + k, 4) for k in range(4)]
    ys = [lax.rem(y + k, 4) for k in range(4)]
    zs = [lax.rem(zh + k, 4) for k in range(4)]

    quarter = rows16(x)
    ga[zh, y, c, x, :, 0:768] = conv_s[quarter]
    ga[zh, y, c, x, :, 768:1152] = qkv_s[0:16, half_columns(x)]
    gb[zh, y, c, 0:32] = conv_s[64:96]
    gb[zh, y, c, 32:48] = dna_s[...]
    gb[zh, y, c, 48:64] = out_s[...]
    last_rows = [qkv_s[:, 768 * i : 768 * i + 768].astype(F32)[16:24] for i in range(2)]
    gb[zh, y, c, 64:80] = jnp.concatenate(last_rows, axis=0).astype(BF16)
    row = lax.broadcasted_iota(jnp.int32, (128, 512), 0)
    column = lax.broadcasted_iota(jnp.int32, (128, 512), 1)
    repeat = (column // 4 == row).astype(F32).astype(BF16)
    repeated = dot(letters[...].astype(F32).astype(BF16), repeat)
    onehot[...] = (repeated == lax.rem(column, 4).astype(F32)).astype(F32).astype(BF16)
    pl.semaphore_wait(barrier, len(everyone))

    send = Sender(send_sems, recv_sems)

    def ref_a(height, step, index, part=None):
        rows = pl.ds(0, 4) if part is None else pl.ds(2 * part, 2)
        return ga.at[rows if height is None else height, step, c, index]

    def ref_b(height, step, part=None):
        return gb.at[height, step, c] if part is None else gb.at[height, step, c, :, half_columns(part)]

    core = []

    def pass_on(ref):
        core.append(send(ref, ref, sibling))

    def pass_a(step):
        pass_on(ga.at[:, step, c])

    def pass_b(height):
        pass_on(gb.at[height, :, c])

    a1 = []
    for k in (1, 3, 2):
        a1.append(send(ref_a(zh, y, x), ref_a(zh, y, x), device(moved(at, zh=k))))
    halo = [
        send(rows_in.at[pl.ds(240, 16)], before, ahead),
        send(rows_in.at[pl.ds(0, 16)], after, behind),
    ]
    ring_z = Ring(send, at, "zh", lambda index, part: ref_b(index, y, part))
    rings_y = [Ring(send, at, "y", lambda index, part, v=zs[k]: ref_b(v, index, part)) for k in range(4)]
    rings_x = [Ring(send, at, "x", lambda index, part, v=ys[k]: ref_a(None, v, index, part)) for k in range(4)]
    ring_a = Ring(send, at, "y", lambda index, part: ref_a(None, index, x, part))
    ring_z.start()
    rings_y[0].start()
    arrive(a1)
    rings_x[0].start()
    ring_a.start()
    ring_z.left_in()
    rings_y[3].start()
    ring_z.right_in()
    rings_y[1].start()
    rings_y[0].both_in()
    ring_a.left_in()
    rings_x[3].start()
    ring_a.right_in()
    rings_x[1].start()
    rings_x[0].both_in()
    ring_z.far_in()
    rings_y[2].start()
    rings_y[3].both_in()
    rings_y[1].both_in()
    ring_a.far_in()
    rings_x[2].start()
    rings_y[0].far_in()
    pass_b(zs[0])
    rings_x[0].far_in()
    pass_a(ys[0])
    rings_x[3].both_in()
    rings_x[1].both_in()
    rings_y[2].both_in()
    rings_x[2].both_in()

    arrive(halo)
    for j in range(6):
        lanes = slice(128 * j, 128 * j + 128)
        rows_f[j, 8:264] = rows_in[:, lanes].astype(F32)
        rows_f[j, 0:8] = jnp.where(sq > 0, before[:, lanes].astype(F32)[8:16], 0.0)
        rows_f[j, 264:272] = jnp.where(sq < 7, after[:, lanes].astype(F32)[0:8], 0.0)
        for i in range(4):
            taps[i, :, lanes] = rows_f[j, pl.ds(7 + i, 128, stride=2)].astype(BF16)

    rings_y[3].far_in()
    pass_b(zs[3])
    rings_y[1].far_in()
    pass_b(zs[1])
    rings_x[3].far_in()
    pass_a(ys[3])
    rings_x[1].far_in()
    pass_a(ys[1])
    rings_y[2].far_in()
    pass_b(zs[2])
    rings_x[2].far_in()
    pass_a(ys[2])

    def transpose_tap(i):
        taps_t[i] = taps[i].T.reshape(4, 2, 96, 128)

    loop(4, transpose_tap)
    onehot_t[...] = onehot[...].T.reshape(4, 4, 2, 16, 128)
    row = lax.broadcasted_iota(jnp.int32, (768, 512), 0)
    column = lax.broadcasted_iota(jnp.int32, (768, 512), 1)
    first_row = column // 16 * 24
    choose_x[...] = (first_row + lax.rem(column, 16) == row).astype(F32).astype(BF16)
    choose_y[...] = (first_row + 16 + lax.rem(column, 8) == row).astype(F32).astype(BF16)
    arrive(core[:-1])

    def conv_full(i):
        first = ga[i, :, :, :, :, 0:768].reshape(4, 2, 64, 768)
        return jnp.concatenate([first, gb[i, :, :, 0:32]], axis=2).reshape(768, 768)

    def qx_full(i):
        return jnp.concatenate(
            [ga[:, :, :, 2 * i + j, :, 768:1152].reshape(512, 384) for j in range(2)], axis=1
        )

    def qy_full():
        return gb[:, :, :, 64:80].reshape(512, 768)

    dna_full = gb[:, :, :, 32:48].reshape(512, 768)
    out_full = gb[:, :, :, 48:64].reshape(512, 768)
    d_attend = right_dot(upstream[...], out_full).astype(BF16)
    slope[...] = dot(onehot[...], dna_full)
    arrive(core[-1:])

    def one_tap(i):
        slope[...] += dot(taps[i], conv_full(i))

    loop(4, one_tap)
    pre = slope[...]
    bend = jnp.tanh(math.sqrt(2.0 / math.pi) * (pre + 0.044715 * (pre * pre * pre)))
    share = 0.5 * (1.0 + bend)
    feature = (pre * share).astype(BF16).astype(F32)
    slope[...] = share + pre * (0.5 * (1.0 - bend * bend)) * (
        math.sqrt(2.0 / math.pi) * (1.0 + 3.0 * 0.044715 * (pre * pre))
    )
    scale = lax.rsqrt(jnp.mean(feature * feature, axis=1, keepdims=True) + epsilon)
    inverse[...] = scale
    unit[...] = feature * scale
    normed = unit[...].astype(BF16)
    wide_x[...] = dot(normed, choose_x[...]).astype(BF16)
    wide_y[...] = dot(normed, choose_y[...]).astype(BF16)
    side_of = lax.rem(lax.broadcasted_iota(jnp.int32, (128, 512), 1), 16) // 8
    for i in range(2):
        own_y = jnp.where(side_of == i, wide_y[...].astype(F32), 0.0).astype(BF16)
        projected = (dot(wide_x[...], qx_full(i)) + dot(own_y, qy_full())).astype(BF16)
        for piece in range(6):
            kind, head = divmod(6 * i + piece, 4)
            place = (2, 0, 1)[kind] * 128
            mine[head, :, place : place + 128] = projected[:, 128 * piece : 128 * piece + 128]
    for head in range(H):
        mine[head, :, 384:512] = d_attend[:, 128 * head : 128 * head + 128]

    kv, rest = pl.ds(0, 256), pl.ds(256, 256)
    kv_in, rest_in = {}, {}
    to_near = [(mine.at[x, :, kv], got_kv.at[x], near)]
    for k, p in zip((1, 2, 3), partners):
        kv_in[k] = send(mine.at[p["x"], :, kv], got.at[x, :, kv], device(p))
    for k, p in zip((1, 2, 3), partners):
        rest_in[k] = send(mine.at[p["x"], :, rest], got.at[x, :, rest], device(p))
    to_near += [(got.at[xs[3], :, kv], got_kv.at[xs[3]], near), (got.at[xs[1], :, kv], got_kv.at[xs[1]], near)]
    to_near += [(got.at[xs[2], :, kv], got_kv.at[xs[2]], near)]
    from_near = send.group(got_kv, to_near[:1])
    for k, copy in zip((1, 3, 2), to_near[1:]):
        arrive([kv_in[k]])
        send.copy(*copy, send.due - 1)
    got[x] = mine[x]
    wide_xt[...] = wide_x[...].T.reshape(4, 4, 2, 16, 128)
    wide_yt[...] = wide_y[...].T.reshape(4, 4, 2, 16, 128)
    arrive([from_near])
    keys = jnp.concatenate([got[:, :, 0:128].reshape(512, 128), got_kv[:, :, 0:128].reshape(512, 128)], axis=0)
    values = jnp.concatenate([got[:, :, 128:256].reshape(512, 128), got_kv[:, :, 128:256].reshape(512, 128)], axis=0)
    scaling = 1.0 / math.sqrt(128)
    home = []
    for k in (0, 1, 3, 2):
        if k:
            arrive([rest_in[k]])
        source = lax.rem(x + 4 - k, 4)
        queries = got[source, :, 256:384]
        upward = got[source, :, 384:512]
        scores = right_dot(queries, keys) * scaling
        powers = jnp.exp(scores - jnp.max(scores, axis=1, keepdims=True))
        probs = powers * (1.0 / jnp.sum(powers, axis=1, keepdims=True))
        probs_low = probs.astype(BF16)
        outgo[source, :, 0:128] = dot(probs_low, values).astype(BF16)
        d_probs = right_dot(upward, values)
        inner = jnp.sum(probs * d_probs, axis=1, keepdims=True)
        d_scores = (probs * (d_probs - inner) * scaling).astype(BF16)
        outgo[source, :, 128:256] = dot(d_scores, keys).astype(BF16)
        if k:
            block = pl.ds(0, 256)
            to = device(moved(at, x=4 - k))
            home.append(send(outgo.at[source, :, block], back.at[x, :, block], to))
        scores_s[source] = d_scores
        probs_s[source] = probs_low
    all_queries = got[:, :, 256:384].reshape(512, 128)
    all_upward = got[:, :, 384:512].reshape(512, 128)

    def d_pair(columns):
        d_keys = row_dot(all_queries, scores_s[:, :, columns].reshape(512, 512)).T
        d_values = row_dot(all_upward, probs_s[:, :, columns].reshape(512, 512)).T
        return jnp.concatenate([d_keys, d_values], axis=1).astype(BF16).reshape(4, 128, 256)

    outgo_kv[...] = d_pair(slice(512, 1024))
    from_across = send.group(back_kv, [(outgo_kv.at[p["x"]], back_kv.at[x], device(p)) for p in across])
    outgo[:, :, 256:512] = d_pair(slice(0, 512))
    for p in partners:
        block = pl.ds(256, 256)
        home.append(send(outgo.at[p["x"], :, block], back.at[x, :, block], device(p)))
    back[x] = outgo[x]
    arrive(home)
    arrive([from_across])
    send.finish()
    for head in range(H):
        columns = slice(128 * head, 128 * head + 128)
        attended[:, columns] = back[head, :, 0:128]
        d_proj[:, columns] = back[head, :, 128:256]
        for kind in range(2):
            total = back[head, :, 256 + 128 * kind : 384 + 128 * kind].astype(F32) + back_kv[
                head, :, 128 * kind : 128 * kind + 128
            ].astype(F32)
            start = 512 * (kind + 1) + 128 * head
            d_proj[:, start : start + 128] = total.astype(BF16)

    attended_t[...] = attended[...].T.reshape(4, 4, 2, 16, 128)
    d_halves = [d_proj[:, 0:768], d_proj[:, 768:1536]]
    row_side = lax.rem(lax.broadcasted_iota(jnp.int32, (256, 768), 0), 16)

    def qkv_grads(parity, to_x, to_y):
        left = wide_xt[:, :, parity].reshape(256, 128)
        for i in range(2):
            block = dot(left, d_halves[i]).astype(BF16)
            for j in range(2):
                to_x[2 * i + j] = block[:, 384 * j : 384 * j + 384].reshape(4, 4, 16, 384)
        left = wide_yt[:, :, parity].reshape(256, 128)
        both = [dot(left, d_half) for d_half in d_halves]
        to_y[...] = jnp.where(row_side < 8, both[0], both[1]).astype(BF16).reshape(4, 4, 16, 768)

    order = (2, 1, 3, 0)
    core_cx, core_cy, core_a, core_b = {}, {}, {}, {}
    qkv_grads(1 - c, px_s, py_s)
    for k in order:
        core_cx[k] = send(px_s.at[xs[k]], px_r.at[xs[k]], sibling)
        core_cy[k] = send(py_s.at[:, ys[k]], py_r.at[:, ys[k]], sibling)
    qkv_grads(c, px, py)
    d_x = sum(right_dot(d_halves[i], qx_full(i)) for i in range(2))
    both = [right_dot(d_half, qy_full()) for d_half in d_halves]
    d_y = jnp.where(side_of == 0, both[0], both[1])

    def sum_cx(k):
        arrive([core_cx[k]])
        px[xs[k]] = add(px, px[xs[k]], px_r[xs[k]])

    def sum_cy(k):
        arrive([core_cy[k]])
        py[:, ys[k]] = add(py, py[:, ys[k]], py_r[:, ys[k]])

    right_x, left_x = device(moved(at, x=1)), device(moved(at, x=3))
    right_y, left_y = device(moved(at, y=1)), device(moved(at, y=3))
    low, high = pl.ds(0, 2), pl.ds(2, 2)
    sides = ((0, 1, right_x, right_y), (1, 3, left_x, left_y))
    sum_cx(2)
    far_cx = [
        send(px.at[xs[2], heights], fcx.at[side], to) for side, heights, to in ((0, low, right_x), (1, high, left_x))
    ]
    sum_cy(2)
    far_cy = [
        send(py.at[heights, ys[2]], fcy.at[side], to) for side, heights, to in ((0, low, right_y), (1, high, left_y))
    ]
    d_normed = 0.0
    for terms, choose in ((d_x, choose_x), (d_y, choose_y)):
        d_high = terms.astype(BF16)
        d_low = (terms - d_high.astype(F32)).astype(BF16)
        d_normed += right_dot(d_high, choose[...]) + right_dot(d_low, choose[...])
    d_feature = upstream[...].astype(F32) + inverse[...] * (
        d_normed - unit[...] * jnp.mean(d_normed * unit[...], axis=1, keepdims=True)
    )
    d_pre = (d_feature * slope[...]).astype(BF16)

    def conv_grads(parity, to_a, to_b):
        def one(i):
            block = dot(taps_t[i, :, parity].reshape(384, 128), d_pre).astype(BF16).reshape(4, 96, 768)
            to_a[i] = block[:, 0:64]
            to_b[i, :, 0:32] = block[:, 64:96]

        loop(4, one)
        left = onehot_t[:, :, parity].reshape(256, 128)
        to_b[:, :, 32:48] = dot(left, d_pre).astype(BF16).reshape(4, 4, 16, 768)
        left = attended_t[:, :, parity].reshape(256, 128)
        to_b[:, :, 48:64] = dot(left, upstream[...]).astype(BF16).reshape(4, 4, 16, 768)

    conv_grads(1 - c, pa_s, pb_s)
    for k in order:
        core_a[k] = send(pa_s.at[:, :, rows16(xs[k])], pa_r.at[:, :, rows16(xs[k])], sibling)
        core_b[k] = send(pb_s.at[:, ys[k]], pb_r.at[:, ys[k]], sibling)
    conv_grads(c, pa, pb)

    def sum_a(k):
        arrive([core_a[k]])
        rows = rows16(xs[k])

        def one(i):
            pa[i, :, rows] = add(pa, pa[i, :, rows], pa_r[i, :, rows])

        loop(4, one)

    def sum_b(k):
        arrive([core_b[k]])

        def one(i):
            pb[i, ys[k]] = add(pb, pb[i, ys[k]], pb_r[i, ys[k]])

        loop(4, one)

    halves = [(h, pl.ds(384 * h, 384), slice(384 * h, 384 * h + 384)) for h in range(2)]
    far_a, far_b = {}, {}
    sum_a(2)
    sum_b(2)
    for h, columns, _ in halves:
        for side, heights, to_x, to_y in ((0, low, right_x, right_y), (1, high, left_x, left_y)):
            far_a[h, side] = send(pa.at[heights, :, rows16(xs[2]), columns], fa.at[h, side], to_x)
            far_b[h, side] = send(pb.at[heights, ys[2], :, columns], fb.at[h, side], to_y)
    near_cx, near_cy = [], []
    for side, k, to_x, to_y in sides:
        sum_cx(k)
        arrive([far_cx[side]])
        part = slice(2 * side, 2 * side + 2)
        px[xs[k], part] = add(px, px[xs[k], part], fcx[side])
        near_cx.append(send(px.at[xs[k]], ncx.at[side], to_x))
        sum_cy(k)
        arrive([far_cy[side]])
        py[part, ys[k]] = add(py, py[part, ys[k]], fcy[side])
        near_cy.append(send(py.at[:, ys[k]], ncy.at[side], to_y))
    for side, k, to_x, to_y in sides:
        sum_a(k)
        sum_b(k)
    near_a, near_b = {}, {}
    for h, columns, cols in halves:
        for side, k, to_x, to_y in sides:
            rows = rows16(xs[k])
            arrive([far_a[h, side]])

            def join_a(i, h=h, side=side, rows=rows, cols=cols):
                pa[2 * side + i, :, rows, cols] = add(pa, pa[2 * side + i, :, rows, cols], fa[h, side, i])

            loop(2, join_a)
            near_a[h, side] = send(pa.at[:, :, rows, columns], na.at[h, side], to_x)
            arrive([far_b[h, side]])

            def join_b(i, h=h, side=side, index=ys[k], cols=cols):
                pb[2 * side + i, index, :, cols] = add(pb, pb[2 * side + i, index, :, cols], fb[h, side, i])

            loop(2, join_b)
            near_b[h, side] = send(pb.at[:, ys[k], :, columns], nb.at[h, side], to_y)

    def three(axis, whole, source):
        return send.group(
            whole, [(source(k), whole.at[k - 1], device(moved(at, **{axis: k}))) for k in (1, 3, 2)]
        )

    sum_cx(0)
    arrive(near_cx)
    scx1[...] = add(scx1, px[x], ncx[0], ncx[1])
    cx2 = three("y", rcx2, lambda k: scx1.at[:, ys[k]])
    sum_cy(0)
    arrive(near_cy)
    scy1[...] = add(scy1, py[:, y], ncy[0], ncy[1])
    cy2 = three("zh", rcy2, lambda k: scy1.at[zs[k]])
    sum_a(0)
    sum_b(0)

    rows_f[:, 256:272] = jnp.zeros((6, 16, 128), F32)
    for i in range(4):
        terms = right_dot(d_pre, conv_full(i))
        for j in range(6):
            target = pl.ds(7 + i, 128, stride=2)
            block = terms[:, 128 * j : 128 * j + 128]
            rows_f[j, target] = block if i < 2 else rows_f[j, target] + block
    rim_out[0] = rows_f[:, 264:272]
    rim_out[1] = rows_f[:, 0:8]
    rims = [send(rim_out.at[0], rim_before, ahead), send(rim_out.at[1], rim_after, behind)]

    a2, b2, a3, b3, a4, b4 = {}, {}, {}, {}, {}, {}
    for h, columns, cols in halves:
        arrive([near_a[h, 0], near_a[h, 1]])

        def first_a(i, h=h, cols=cols):
            sa1[h, i] = add(sa1, pa[i, :, rows16(x), cols], na[h, 0, i], na[h, 1, i])

        loop(4, first_a)
        a2[h] = three("y", ra2.at[h], lambda k, h=h: sa1.at[h, :, ys[k]])
        arrive([near_b[h, 0], near_b[h, 1]])

        def first_b(i, h=h, cols=cols):
            sb1[h, i] = add(sb1, pb[i, y, :, cols], nb[h, 0, i], nb[h, 1, i])

        loop(4, first_b)
        b2[h] = three("x", rb2.at[h], lambda k, h=h: sb1.at[h, :, rows16(xs[k])])
        if h == 0:
            arrive([cx2])
            scx2[...] = add(scx2, scx1[:, y], rcx2[0], rcx2[1], rcx2[2])
            cx3 = three("zh", rcx3, lambda k: scx2.at[zs[k]])
            arrive([cy2])
            scy2[...] = add(scy2, scy1[zh], rcy2[0], rcy2[1], rcy2[2])
            cy3 = send(scy2, rcy3, near)
    arrive(rims)
    rows_f[:, 8:9] += jnp.where(sq > 0, rim_before[:, 0:1], 0.0)
    rows_f[:, 263:264] += jnp.where(sq < 7, rim_after[:, 7:8], 0.0)
    for j in range(6):
        seq_o[:, 128 * j : 128 * j + 128] = rows_f[j, 8:264].astype(BF16)
    for h in range(2):
        arrive([a2[h]])
        sa2[h] = add(sa2, sa1[h, :, y], ra2[h, 0], ra2[h, 1], ra2[h, 2])
        a3[h] = three("zh", ra3.at[h], lambda k, h=h: sa2.at[h, zs[k]])
        arrive([b2[h]])
        sb2[h] = add(sb2, sb1[h, :, rows16(x)], rb2[h, 0], rb2[h, 1], rb2[h, 2])
        b3[h] = three("zh", rb3.at[h], lambda k, h=h: sb2.at[h, zs[k]])
        if h == 0:
            arrive([cx3])
            scx3[...] = add(scx3, scx2[zh], rcx3[0], rcx3[1], rcx3[2])
            cx4 = send(scx3, rcx4, near)
            arrive([cy3])
            scy3[...] = add(scy3, scy2[...], rcy3[...])
            cy4 = three("x", rcy4, lambda k: scy3)

    for h in range(2):
        arrive([a3[h]])
        sa3[h] = add(sa3, sa2[h, zh], ra3[h, 0], ra3[h, 1], ra3[h, 2])
        a4[h] = send(sa3.at[h], ra4.at[h], near)
        arrive([b3[h]])
        sb3[h] = add(sb3, sb2[h, zh], rb3[h, 0], rb3[h, 1], rb3[h, 2])
        b4[h] = send(sb3.at[h], rb4.at[h], near)
        if h == 0:
            arrive([cx4])
            final_x[x] = add(final_x, scx3[...], rcx4[...])
            spread = [send(final_x.at[x], final_x.at[x], device(moved(at, x=k))) for k in (1, 2, 3)]
            arrive([cy4])
            final_y[...] = add(final_y, scy3[...], rcy4[0], rcy4[1], rcy4[2])
    for h in range(2):
        arrive([a4[h]])
        final[x, 0, h] = add(final, sa3[h], ra4[h])
        arrive([b4[h]])
        final[x, 1, h] = add(final, sb3[h], rb4[h])
    spread += [send(final.at[x], final.at[x], device(moved(at, x=k))) for k in (1, 2, 3)]
    arrive(spread)
    send.finish()


def finish_kernel(seq_i, final, final_x, final_y, seq_o, conv_o, dna_o, qkv_o, out_o):
    seq_o[0] = seq_i[...]
    for h in range(2):
        columns = slice(384 * h, 384 * h + 384)
        for q in range(4):
            conv_o[16 * q : 16 * q + 16, columns] = final[q, 0, h].astype(F32)
        conv_o[64:80, columns] = final[0, 1, h].astype(F32)
        conv_o[80:96, columns] = final[1, 1, h].astype(F32)
        dna_o[:, columns] = final[2, 1, h].astype(F32)
        out_o[:, columns] = final[3, 1, h].astype(F32)
    for q in range(4):
        qkv_o[0:16, 384 * q : 384 * q + 384] = final_x[q].astype(F32)
    last_rows = final_y[...].astype(F32)
    qkv_o[16:24, 0:768] = last_rows[0:8]
    qkv_o[16:24, 768:1536] = last_rows[8:16]


def layer(*operands):
    vmem = pl.BlockSpec(memory_space=pltpu.VMEM)
    low = [
        (4, 4, 2, 4, 16, 1152), (4, 4, 2, 80, 768), (16, 768), (16, 768),
        (4, 128, 768), (4, 4, 2, 96, 128), (128, 512), (4, 4, 2, 16, 128), (768, 512), (768, 512),
        (128, 512), (128, 512), (4, 4, 2, 16, 128), (4, 4, 2, 16, 128), (128, 1536), (128, 512), (4, 4, 2, 16, 128),
        (4, 128, 512), (4, 128, 512), (4, 128, 256), (4, 128, 512), (4, 128, 256), (4, 128, 512), (4, 128, 256),
        (4, 128, 1024), (4, 128, 1024),
    ] + 3 * [(4, 4, 64, 768), (4, 4, 64, 768), (4, 4, 4, 16, 384), (4, 4, 16, 768)] + [
        (2, 2, 2, 4, 16, 384), (2, 2, 4, 4, 16, 384), (2, 4, 4, 16, 384), (2, 3, 4, 16, 384),
        (2, 4, 16, 384), (2, 3, 16, 384), (2, 16, 384), (2, 16, 384),
        (2, 2, 2, 64, 384), (2, 2, 4, 64, 384), (2, 4, 64, 384), (2, 3, 4, 16, 384),
        (2, 4, 16, 384), (2, 3, 16, 384), (2, 16, 384), (2, 16, 384),
        (2, 2, 4, 16, 384), (2, 4, 4, 16, 384), (4, 4, 16, 384), (3, 4, 16, 384), (4, 16, 384), (3, 16, 384), (16, 384), (16, 384),
        (2, 2, 16, 768), (2, 4, 16, 768), (4, 16, 768), (3, 16, 768), (16, 768), (16, 768), (16, 768), (3, 16, 768),
    ]
    wide = [(128, 768), (128, 768), (128, 1), (6, 272, 128), (2, 6, 8, 128), (6, 8, 128), (6, 8, 128)]
    results = pl.pallas_call(
        layer_kernel,
        name="layer",
        out_shape=tuple(
            jax.ShapeDtypeStruct(shape, BF16)
            for shape in ((256, 768), (4, 2, 2, 16, 384), (4, 16, 384), (16, 768))
        ),
        in_specs=[vmem] * 7,
        out_specs=(vmem,) * 4,
        scratch_shapes=[pltpu.VMEM(shape, BF16) for shape in low]
        + [pltpu.VMEM(shape, F32) for shape in wide]
        + [pltpu.SemaphoreType.DMA((90,)), pltpu.SemaphoreType.DMA((133,))],
        compiler_params=pltpu.CompilerParams(
            collective_id=1, has_side_effects=True, vmem_limit_bytes=60 * 2**20
        ),
    )(*operands)
    return pl.pallas_call(
        finish_kernel,
        name="finish",
        out_shape=(
            jax.ShapeDtypeStruct((1, 256, 768), BF16),
            jax.ShapeDtypeStruct((96, 768), F32),
            jax.ShapeDtypeStruct((16, 768), F32),
            jax.ShapeDtypeStruct((24, 1536), F32),
            jax.ShapeDtypeStruct((16, 768), F32),
        ),
        in_specs=[vmem] * 4,
        out_specs=(vmem,) * 5,
    )(*results)


def per_device(seq_in, bases, conv_weight, dna_weight, qkv_weight, out_weight, cotangent):
    return layer(
        conv_weight, dna_weight, qkv_weight, out_weight, seq_in[0], bases[0].reshape(128, BIN), cotangent[0]
    )


def solution(mesh):
    in_specs = (
        P("dp", "seq", None),
        P("dp", "seq"),
        P("dp", None),
        P("dp", None),
        P("dp", None),
        P("dp", None),
        P("dp", "seq", None),
    )
    out_specs = (P("dp", "seq", None), P("dp", None), P("dp", None), P("dp", None), P("dp", None))
    return jax.shard_map(
        per_device, mesh=mesh, in_specs=in_specs, out_specs=out_specs, check_vma=False
    )
```

time: 130 us -> 123 us (0.946)
  Pallas kernels: 129 us -> 122 us
    pallas_call x1, Pallas kernels: 127 us -> 120 us  [layer(): pl.pallas_call(layer_kernel, name='layer', out_shape=tuple((jax.ShapeDtyp...]
where the time goes in v5:
time: 123 us
  Pallas kernels  122 us (99%)
    pallas_call x1, Pallas kernels, layer(): pl.pallas_call(layer_kernel, name='layer', out_shape=tuple((jax.ShapeDtyp...  120 us

profile of v5, /device:TPU:32, one launch (start us, length us, event | category | flops | bytes accessed | tf_op | source)
XLA Modules:
  0.0 122.6 jit_solution(7639102971554497726)
XLA Ops:
  0.6 119.9 %layer.1 = (bf16[256,768]{1,0:T(8,128)(2,1)}, bf16[4,2,2,16,384]{4,3,2,1,0:T(8,128)(2,1)}, bf16[4,16,384]{2,1,0:T(8,128)(2,1)}, bf16[16,768]{1,0:T(8,128)(2,1)}) custom-call(bf16[96,768]{1,0:T(8,128)(2,1)} %conv_s.1, bf16[16,768]{1,0:T(8,128)(2,1)} %dna_s.1, bf16[24,1536]{1,0:T(8,128)(2,1)} %qkv_s.1, bf16[16,768]{1,0:T(8,128)(2,1)} %out_s.1, ...), custom_call_target="tpu_custom_call" | custom-call | tf_op jit(solution)/shard_map/layer/pallas_call | solution.py:669
  120.5 2.0 %finish.1 = (bf16[1,256,768]{2,1,0:T(8,128)(2,1)}, f32[96,768]{1,0:T(8,128)}, f32[16,768]{1,0:T(8,128)}, f32[24,1536]{1,0:T(8,128)}, f32[16,768]{1,0:T(8,128)}) custom-call(bf16[256,768]{1,0:T(8,128)(2,1)} %get-tuple-element.9.seq_i, bf16[4,2,2,16,384]{4,3,2,1,0:T(8,128)(2,1)} %get-tuple-element.10.final, bf16[4,16,384]{2,1,0:T(8,128)(2,1)} %get-tuple-element.11.final_x, ...), custom_call_target="tpu_custom_call" | custom-call | tf_op jit(solution)/shard_map/finish/pallas_call | solution.py:685

commit v6 on v5

--- a/solution.py
+++ b/solution.py
@@ -154,13 +154,13 @@
     seq_o, final, final_x, final_y,
     ga, gb, before, after,
     taps, taps_t, onehot, onehot_t, choose_x, choose_y, wide_x, wide_y, wide_xt, wide_yt, d_proj, attended, attended_t,
-    mine, got, got_kv, outgo, outgo_kv, back, back_kv, probs_s, scores_s,
+    mine, got, got_k, got_v, outgo, outgo_k, outgo_v, back, back_k, back_v, probs_s, scores_s,
     pa_s, pb_s, px_s, py_s, pa, pb, px, py, pa_r, pb_r, px_r, py_r,
     fa, na, sa1, ra2, sa2, ra3, sa3, ra4,
     fb, nb, sb1, rb2, sb2, rb3, sb3, rb4,
     fcx, ncx, scx1, rcx2, scx2, rcx3, scx3, rcx4,
     fcy, ncy, scy1, rcy2, scy2, rcy3, scy3, rcy4,
-    slope, unit, inverse, rows_f, rim_out, rim_before, rim_after,
+    slope, unit, inverse, rows_f, probs_f, rim_out, rim_before, rim_after,
     send_sems, recv_sems,
 ):
     at = here()
@@ -170,7 +170,6 @@
     behind, ahead = (dp, lax.rem(sq + 7, 8)), (dp, lax.rem(sq + 1, 8))
     sibling = device(moved(at, c=1))
     near = device(moved(at, zl=1))
-    partners = [moved(at, x=k) for k in (1, 2, 3)]
     across = [moved(at, x=k, zl=1) for k in range(4)]
     everyone = [device(moved(at, **{a: k})) for a, k in PEERS] + [behind, ahead]
     everyone += [device(p) for p in across[1:]]
@@ -189,11 +188,6 @@
     gb[zh, y, c, 48:64] = out_s[...]
     last_rows = [qkv_s[:, 768 * i : 768 * i + 768].astype(F32)[16:24] for i in range(2)]
     gb[zh, y, c, 64:80] = jnp.concatenate(last_rows, axis=0).astype(BF16)
-    row = lax.broadcasted_iota(jnp.int32, (128, 512), 0)
-    column = lax.broadcasted_iota(jnp.int32, (128, 512), 1)
-    repeat = (column // 4 == row).astype(F32).astype(BF16)
-    repeated = dot(letters[...].astype(F32).astype(BF16), repeat)
-    onehot[...] = (repeated == lax.rem(column, 4).astype(F32)).astype(F32).astype(BF16)
     pl.semaphore_wait(barrier, len(everyone))
 
     send = Sender(send_sems, recv_sems)
@@ -229,33 +223,38 @@
     ring_a = Ring(send, at, "y", lambda index, part: ref_a(None, index, x, part))
     ring_z.start()
     rings_y[0].start()
+    row = lax.broadcasted_iota(jnp.int32, (128, 512), 0)
+    column = lax.broadcasted_iota(jnp.int32, (128, 512), 1)
+    repeat = (column // 4 == row).astype(F32).astype(BF16)
+    repeated = dot(letters[...].astype(F32).astype(BF16), repeat)
+    onehot[...] = (repeated == lax.rem(column, 4).astype(F32)).astype(F32).astype(BF16)
     arrive(a1)
+    ring_a.start()
     rings_x[0].start()
-    ring_a.start()
     ring_z.left_in()
     rings_y[3].start()
     ring_z.right_in()
-    rings_y[1].start()
     rings_y[0].both_in()
     ring_a.left_in()
     rings_x[3].start()
     ring_a.right_in()
     rings_x[1].start()
+    rings_y[1].start()
     rings_x[0].both_in()
+    ring_a.far_in()
+    rings_x[2].start()
     ring_z.far_in()
     rings_y[2].start()
     rings_y[3].both_in()
+    rings_x[3].both_in()
+    rings_x[1].both_in()
     rings_y[1].both_in()
-    ring_a.far_in()
-    rings_x[2].start()
     rings_y[0].far_in()
     pass_b(zs[0])
     rings_x[0].far_in()
     pass_a(ys[0])
-    rings_x[3].both_in()
-    rings_x[1].both_in()
+    rings_x[2].both_in()
     rings_y[2].both_in()
-    rings_x[2].both_in()
 
     arrive(halo)
     for j in range(6):
@@ -332,80 +331,95 @@
         projected = (dot(wide_x[...], qx_full(i)) + dot(own_y, qy_full())).astype(BF16)
         for piece in range(6):
             kind, head = divmod(6 * i + piece, 4)
-            place = (2, 0, 1)[kind] * 128
+            place = (1, 0, 2)[kind] * 128
             mine[head, :, place : place + 128] = projected[:, 128 * piece : 128 * piece + 128]
     for head in range(H):
         mine[head, :, 384:512] = d_attend[:, 128 * head : 128 * head + 128]
 
-    kv, rest = pl.ds(0, 256), pl.ds(256, 256)
-    kv_in, rest_in = {}, {}
-    to_near = [(mine.at[x, :, kv], got_kv.at[x], near)]
-    for k, p in zip((1, 2, 3), partners):
-        kv_in[k] = send(mine.at[p["x"], :, kv], got.at[x, :, kv], device(p))
-    for k, p in zip((1, 2, 3), partners):
-        rest_in[k] = send(mine.at[p["x"], :, rest], got.at[x, :, rest], device(p))
-    to_near += [(got.at[xs[3], :, kv], got_kv.at[xs[3]], near), (got.at[xs[1], :, kv], got_kv.at[xs[1]], near)]
-    to_near += [(got.at[xs[2], :, kv], got_kv.at[xs[2]], near)]
-    from_near = send.group(got_kv, to_near[:1])
-    for k, copy in zip((1, 3, 2), to_near[1:]):
-        arrive([kv_in[k]])
-        send.copy(*copy, send.due - 1)
+    col_k, col_v, col_kq, col_vd = pl.ds(0, 128), pl.ds(256, 128), pl.ds(0, 256), pl.ds(256, 256)
+    kq_in, vd_in = {}, {}
+    from_near_k = send.group(got_k, [(mine.at[x, :, col_k], got_k.at[x], near)])
+    near_k = send.due - 1
+    for k in (1, 3, 2):
+        kq_in[k] = send(mine.at[xs[k], :, col_kq], got.at[x, :, col_kq], device(moved(at, x=k)))
+    for k in (1, 3, 2):
+        vd_in[k] = send(mine.at[xs[k], :, col_vd], got.at[x, :, col_vd], device(moved(at, x=k)))
+    sources = {k: lax.rem(x + 4 - k, 4) for k in (0, 1, 3, 2)}
     got[x] = mine[x]
+    for k in (1, 3, 2):
+        arrive([kq_in[k]])
+        send.copy(got.at[sources[k], :, col_k], got_k.at[sources[k]], near, near_k)
+    from_near_v = send.group(got_v, [(mine.at[x, :, col_v], got_v.at[x], near)])
+    near_v = send.due - 1
     wide_xt[...] = wide_x[...].T.reshape(4, 4, 2, 16, 128)
     wide_yt[...] = wide_y[...].T.reshape(4, 4, 2, 16, 128)
-    arrive([from_near])
-    keys = jnp.concatenate([got[:, :, 0:128].reshape(512, 128), got_kv[:, :, 0:128].reshape(512, 128)], axis=0)
-    values = jnp.concatenate([got[:, :, 128:256].reshape(512, 128), got_kv[:, :, 128:256].reshape(512, 128)], axis=0)
+    arrive([from_near_k])
+    keys = jnp.concatenate([got[:, :, 0:128].reshape(512, 128), got_k[...].reshape(512, 128)], axis=0)
     scaling = 1.0 / math.sqrt(128)
-    home = []
-    for k in (0, 1, 3, 2):
-        if k:
-            arrive([rest_in[k]])
-        source = lax.rem(x + 4 - k, 4)
-        queries = got[source, :, 256:384]
-        upward = got[source, :, 384:512]
-        scores = right_dot(queries, keys) * scaling
+
+    def soft(source):
+        scores = right_dot(got[source, :, 128:256], keys) * scaling
         powers = jnp.exp(scores - jnp.max(scores, axis=1, keepdims=True))
         probs = powers * (1.0 / jnp.sum(powers, axis=1, keepdims=True))
-        probs_low = probs.astype(BF16)
-        outgo[source, :, 0:128] = dot(probs_low, values).astype(BF16)
-        d_probs = right_dot(upward, values)
+        probs_f[source] = probs
+        probs_s[source] = probs.astype(BF16)
+
+    def pass_v(k):
+        arrive([vd_in[k]])
+        send.copy(got.at[sources[k], :, col_v], got_v.at[sources[k]], near, near_v)
+
+    soft(sources[0])
+    pass_v(1)
+    pass_v(3)
+    soft(sources[1])
+    soft(sources[3])
+    pass_v(2)
+    soft(sources[2])
+    home = []
+    all_queries = got[:, :, 128:256].reshape(512, 128)
+    all_upward = got[:, :, 384:512].reshape(512, 128)
+    all_probs = probs_s[...].reshape(512, 1024)
+    d_values = row_dot(all_upward, all_probs).T.astype(BF16).reshape(8, 128, 128)
+    outgo_v[...] = d_values[4:8]
+    home.append(send.group(back_v, [(outgo_v.at[p["x"]], back_v.at[x], device(p)) for p in across]))
+    outgo[:, :, 384:512] = d_values[0:4]
+    arrive([from_near_v])
+    values = jnp.concatenate([got[:, :, 256:384].reshape(512, 128), got_v[...].reshape(512, 128)], axis=0)
+    outgo[:, :, 0:128] = dot(all_probs, values).astype(BF16).reshape(4, 128, 128)
+    for k in (1, 3, 2):
+        block = pl.ds(0, 128)
+        home.append(send(outgo.at[xs[k], :, block], back.at[x, :, block], device(moved(at, x=k))))
+
+    def step(i, carry):
+        probs = probs_f[i]
+        d_probs = right_dot(got[i, :, 384:512], values)
         inner = jnp.sum(probs * d_probs, axis=1, keepdims=True)
-        d_scores = (probs * (d_probs - inner) * scaling).astype(BF16)
-        outgo[source, :, 128:256] = dot(d_scores, keys).astype(BF16)
-        if k:
-            block = pl.ds(0, 256)
-            to = device(moved(at, x=4 - k))
-            home.append(send(outgo.at[source, :, block], back.at[x, :, block], to))
-        scores_s[source] = d_scores
-        probs_s[source] = probs_low
-    all_queries = got[:, :, 256:384].reshape(512, 128)
-    all_upward = got[:, :, 384:512].reshape(512, 128)
-
-    def d_pair(columns):
+        scores_s[i] = (probs * (d_probs - inner) * scaling).astype(BF16)
+        return carry
+
+    lax.fori_loop(0, 4, step, 0)
+
+    def key_grads(columns):
         d_keys = row_dot(all_queries, scores_s[:, :, columns].reshape(512, 512)).T
-        d_values = row_dot(all_upward, probs_s[:, :, columns].reshape(512, 512)).T
-        return jnp.concatenate([d_keys, d_values], axis=1).astype(BF16).reshape(4, 128, 256)
-
-    outgo_kv[...] = d_pair(slice(512, 1024))
-    from_across = send.group(back_kv, [(outgo_kv.at[p["x"]], back_kv.at[x], device(p)) for p in across])
-    outgo[:, :, 256:512] = d_pair(slice(0, 512))
-    for p in partners:
-        block = pl.ds(256, 256)
-        home.append(send(outgo.at[p["x"], :, block], back.at[x, :, block], device(p)))
+        return d_keys.astype(BF16).reshape(4, 128, 128)
+
+    outgo_k[...] = key_grads(slice(512, 1024))
+    home.append(send.group(back_k, [(outgo_k.at[p["x"]], back_k.at[x], device(p)) for p in across]))
+    outgo[:, :, 256:384] = key_grads(slice(0, 512))
+    outgo[:, :, 128:256] = dot(scores_s[...].reshape(512, 1024), keys).astype(BF16).reshape(4, 128, 128)
+    for k in (1, 3, 2):
+        block = pl.ds(128, 384)
+        home.append(send(outgo.at[xs[k], :, block], back.at[x, :, block], device(moved(at, x=k))))
     back[x] = outgo[x]
     arrive(home)
-    arrive([from_across])
     send.finish()
     for head in range(H):
         columns = slice(128 * head, 128 * head + 128)
         attended[:, columns] = back[head, :, 0:128]
         d_proj[:, columns] = back[head, :, 128:256]
-        for kind in range(2):
-            total = back[head, :, 256 + 128 * kind : 384 + 128 * kind].astype(F32) + back_kv[
-                head, :, 128 * kind : 128 * kind + 128
-            ].astype(F32)
-            start = 512 * (kind + 1) + 128 * head
+        for kind, other in ((1, back_k), (2, back_v)):
+            total = back[head, :, 128 + 128 * kind : 256 + 128 * kind].astype(F32) + other[head].astype(F32)
+            start = 512 * kind + 128 * head
             d_proj[:, start : start + 128] = total.astype(BF16)
 
     attended_t[...] = attended[...].T.reshape(4, 4, 2, 16, 128)
@@ -426,7 +440,7 @@
     core_cx, core_cy, core_a, core_b = {}, {}, {}, {}
     qkv_grads(1 - c, px_s, py_s)
     for k in order:
-        core_cx[k] = send(px_s.at[xs[k]], px_r.at[xs[k]], sibling)
+        core_cx[k] = send(px_s.at[:, zs[k]], px_r.at[:, zs[k]], sibling)
         core_cy[k] = send(py_s.at[:, ys[k]], py_r.at[:, ys[k]], sibling)
     qkv_grads(c, px, py)
     d_x = sum(right_dot(d_halves[i], qx_full(i)) for i in range(2))
@@ -435,7 +449,7 @@
 
     def sum_cx(k):
         arrive([core_cx[k]])
-        px[xs[k]] = add(px, px[xs[k]], px_r[xs[k]])
+        px[:, zs[k]] = add(px, px[:, zs[k]], px_r[:, zs[k]])
 
     def sum_cy(k):
         arrive([core_cy[k]])
@@ -443,11 +457,12 @@
 
     right_x, left_x = device(moved(at, x=1)), device(moved(at, x=3))
     right_y, left_y = device(moved(at, y=1)), device(moved(at, y=3))
+    right_z, left_z = device(moved(at, zh=1)), device(moved(at, zh=3))
     low, high = pl.ds(0, 2), pl.ds(2, 2)
     sides = ((0, 1, right_x, right_y), (1, 3, left_x, left_y))
     sum_cx(2)
     far_cx = [
-        send(px.at[xs[2], heights], fcx.at[side], to) for side, heights, to in ((0, low, right_x), (1, high, left_x))
+        send(px.at[quarters, zs[2]], fcx.at[side], to) for side, quarters, to in ((0, low, right_z), (1, high, left_z))
     ]
     sum_cy(2)
     far_cy = [
@@ -511,8 +526,8 @@
         sum_cx(k)
         arrive([far_cx[side]])
         part = slice(2 * side, 2 * side + 2)
-        px[xs[k], part] = add(px, px[xs[k], part], fcx[side])
-        near_cx.append(send(px.at[xs[k]], ncx.at[side], to_x))
+        px[part, zs[k]] = add(px, px[part, zs[k]], fcx[side])
+        near_cx.append(send(px.at[:, zs[k]], ncx.at[side], (right_z, left_z)[side]))
         sum_cy(k)
         arrive([far_cy[side]])
         py[part, ys[k]] = add(py, py[part, ys[k]], fcy[side])
@@ -546,8 +561,8 @@
 
     sum_cx(0)
     arrive(near_cx)
-    scx1[...] = add(scx1, px[x], ncx[0], ncx[1])
-    cx2 = three("y", rcx2, lambda k: scx1.at[:, ys[k]])
+    scx1[...] = add(scx1, px[:, zh], ncx[0], ncx[1])
+    cx2 = three("x", rcx2, lambda k: scx1.at[xs[k]])
     sum_cy(0)
     arrive(near_cy)
     scy1[...] = add(scy1, py[:, y], ncy[0], ncy[1])
@@ -584,8 +599,8 @@
         b2[h] = three("x", rb2.at[h], lambda k, h=h: sb1.at[h, :, rows16(xs[k])])
         if h == 0:
             arrive([cx2])
-            scx2[...] = add(scx2, scx1[:, y], rcx2[0], rcx2[1], rcx2[2])
-            cx3 = three("zh", rcx3, lambda k: scx2.at[zs[k]])
+            scx2[...] = add(scx2, scx1[x], rcx2[0], rcx2[1], rcx2[2])
+            cx3 = three("y", rcx3, lambda k: scx2.at[ys[k]])
             arrive([cy2])
             scy2[...] = add(scy2, scy1[zh], rcy2[0], rcy2[1], rcy2[2])
             cy3 = send(scy2, rcy3, near)
@@ -603,7 +618,7 @@
         b3[h] = three("zh", rb3.at[h], lambda k, h=h: sb2.at[h, zs[k]])
         if h == 0:
             arrive([cx3])
-            scx3[...] = add(scx3, scx2[zh], rcx3[0], rcx3[1], rcx3[2])
+            scx3[...] = add(scx3, scx2[y], rcx3[0], rcx3[1], rcx3[2])
             cx4 = send(scx3, rcx4, near)
             arrive([cy3])
             scy3[...] = add(scy3, scy2[...], rcy3[...])
@@ -655,7 +670,9 @@
         (4, 4, 2, 4, 16, 1152), (4, 4, 2, 80, 768), (16, 768), (16, 768),
         (4, 128, 768), (4, 4, 2, 96, 128), (128, 512), (4, 4, 2, 16, 128), (768, 512), (768, 512),
         (128, 512), (128, 512), (4, 4, 2, 16, 128), (4, 4, 2, 16, 128), (128, 1536), (128, 512), (4, 4, 2, 16, 128),
-        (4, 128, 512), (4, 128, 512), (4, 128, 256), (4, 128, 512), (4, 128, 256), (4, 128, 512), (4, 128, 256),
+        (4, 128, 512),
+        (4, 128, 512), (4, 128, 128), (4, 128, 128), (4, 128, 512), (4, 128, 128), (4, 128, 128),
+        (4, 128, 512), (4, 128, 128), (4, 128, 128),
         (4, 128, 1024), (4, 128, 1024),
     ] + 3 * [(4, 4, 64, 768), (4, 4, 64, 768), (4, 4, 4, 16, 384), (4, 4, 16, 768)] + [
         (2, 2, 2, 4, 16, 384), (2, 2, 4, 4, 16, 384), (2, 4, 4, 16, 384), (2, 3, 4, 16, 384),
@@ -665,7 +682,7 @@
         (2, 2, 4, 16, 384), (2, 4, 4, 16, 384), (4, 4, 16, 384), (3, 4, 16, 384), (4, 16, 384), (3, 16, 384), (16, 384), (16, 384),
         (2, 2, 16, 768), (2, 4, 16, 768), (4, 16, 768), (3, 16, 768), (16, 768), (16, 768), (16, 768), (3, 16, 768),
     ]
-    wide = [(128, 768), (128, 768), (128, 1), (6, 272, 128), (2, 6, 8, 128), (6, 8, 128), (6, 8, 128)]
+    wide = [(128, 768), (128, 768), (128, 1), (6, 272, 128), (4, 128, 1024), (2, 6, 8, 128), (6, 8, 128), (6, 8, 128)]
     results = pl.pallas_call(
         layer_kernel,
         name="layer",
@@ -677,7 +694,7 @@
         out_specs=(vmem,) * 4,
         scratch_shapes=[pltpu.VMEM(shape, BF16) for shape in low]
         + [pltpu.VMEM(shape, F32) for shape in wide]
-        + [pltpu.SemaphoreType.DMA((90,)), pltpu.SemaphoreType.DMA((133,))],
+        + [pltpu.SemaphoreType.DMA((90,)), pltpu.SemaphoreType.DMA((135,))],
         compiler_params=pltpu.CompilerParams(
             collective_id=1, has_side_effects=True, vmem_limit_bytes=60 * 2**20
         ),

time: 123 us -> 119 us (0.967)
  Pallas kernels: 122 us -> 119 us
    pallas_call x1, Pallas kernels: 120 us -> 117 us  [layer(): pl.pallas_call(layer_kernel, name='layer', out_shape=tuple((jax.ShapeDtyp...]
where the time goes in v6:
time: 119 us
  Pallas kernels  119 us (100%)
    pallas_call x1, Pallas kernels, layer(): pl.pallas_call(layer_kernel, name='layer', out_shape=tuple((jax.ShapeDtyp...  117 us

profile of v6, /device:TPU:32, one launch (start us, length us, event | category | flops | bytes accessed | tf_op | source)
XLA Modules:
  0.0 119.4 jit_solution(9974945546679470468)
XLA Ops:
  0.6 116.7 %layer.1 = (bf16[256,768]{1,0:T(8,128)(2,1)}, bf16[4,2,2,16,384]{4,3,2,1,0:T(8,128)(2,1)}, bf16[4,16,384]{2,1,0:T(8,128)(2,1)}, bf16[16,768]{1,0:T(8,128)(2,1)}) custom-call(bf16[96,768]{1,0:T(8,128)(2,1)} %conv_s.1, bf16[16,768]{1,0:T(8,128)(2,1)} %dna_s.1, bf16[24,1536]{1,0:T(8,128)(2,1)} %qkv_s.1, bf16[16,768]{1,0:T(8,128)(2,1)} %out_s.1, ...), custom_call_target="tpu_custom_call" | custom-call | tf_op jit(solution)/shard_map/layer/pallas_call | solution.py:686
  117.3 2.0 %finish.1 = (bf16[1,256,768]{2,1,0:T(8,128)(2,1)}, f32[96,768]{1,0:T(8,128)}, f32[16,768]{1,0:T(8,128)}, f32[24,1536]{1,0:T(8,128)}, f32[16,768]{1,0:T(8,128)}) custom-call(bf16[256,768]{1,0:T(8,128)(2,1)} %get-tuple-element.9.seq_i, bf16[4,2,2,16,384]{4,3,2,1,0:T(8,128)(2,1)} %get-tuple-element.10.final, bf16[4,16,384]{2,1,0:T(8,128)(2,1)} %get-tuple-element.11.final_x, ...), custom_call_target="tpu_custom_call" | custom-call | tf_op jit(solution)/shard_map/finish/pallas_call | solution.py:702

commit v7 on v6

--- a/solution.py
+++ b/solution.py
@@ -211,7 +211,7 @@
         pass_on(gb.at[height, :, c])
 
     a1 = []
-    for k in (1, 3, 2):
+    for k in (2, 1, 3):
         a1.append(send(ref_a(zh, y, x), ref_a(zh, y, x), device(moved(at, zh=k))))
     halo = [
         send(rows_in.at[pl.ds(240, 16)], before, ahead),
@@ -331,34 +331,33 @@
         projected = (dot(wide_x[...], qx_full(i)) + dot(own_y, qy_full())).astype(BF16)
         for piece in range(6):
             kind, head = divmod(6 * i + piece, 4)
-            place = (1, 0, 2)[kind] * 128
-            mine[head, :, place : place + 128] = projected[:, 128 * piece : 128 * piece + 128]
+            mine[head, (1, 0, 2)[kind]] = projected[:, 128 * piece : 128 * piece + 128]
     for head in range(H):
-        mine[head, :, 384:512] = d_attend[:, 128 * head : 128 * head + 128]
-
-    col_k, col_v, col_kq, col_vd = pl.ds(0, 128), pl.ds(256, 128), pl.ds(0, 256), pl.ds(256, 256)
+        mine[head, 3] = d_attend[:, 128 * head : 128 * head + 128]
+
+    kq, vd = pl.ds(0, 2), pl.ds(2, 2)
     kq_in, vd_in = {}, {}
-    from_near_k = send.group(got_k, [(mine.at[x, :, col_k], got_k.at[x], near)])
+    from_near_k = send.group(got_k, [(mine.at[x, 0], got_k.at[x], near)])
     near_k = send.due - 1
+    from_near_v = send.group(got_v, [(mine.at[x, 2], got_v.at[x], near)])
+    near_v = send.due - 1
     for k in (1, 3, 2):
-        kq_in[k] = send(mine.at[xs[k], :, col_kq], got.at[x, :, col_kq], device(moved(at, x=k)))
+        kq_in[k] = send(mine.at[xs[k], kq], got.at[x, kq], device(moved(at, x=k)))
     for k in (1, 3, 2):
-        vd_in[k] = send(mine.at[xs[k], :, col_vd], got.at[x, :, col_vd], device(moved(at, x=k)))
+        vd_in[k] = send(mine.at[xs[k], vd], got.at[x, vd], device(moved(at, x=k)))
     sources = {k: lax.rem(x + 4 - k, 4) for k in (0, 1, 3, 2)}
     got[x] = mine[x]
     for k in (1, 3, 2):
         arrive([kq_in[k]])
-        send.copy(got.at[sources[k], :, col_k], got_k.at[sources[k]], near, near_k)
-    from_near_v = send.group(got_v, [(mine.at[x, :, col_v], got_v.at[x], near)])
-    near_v = send.due - 1
+        send.copy(got.at[sources[k], 0], got_k.at[sources[k]], near, near_k)
     wide_xt[...] = wide_x[...].T.reshape(4, 4, 2, 16, 128)
     wide_yt[...] = wide_y[...].T.reshape(4, 4, 2, 16, 128)
     arrive([from_near_k])
-    keys = jnp.concatenate([got[:, :, 0:128].reshape(512, 128), got_k[...].reshape(512, 128)], axis=0)
+    keys = jnp.concatenate([got[:, 0].reshape(512, 128), got_k[...].reshape(512, 128)], axis=0)
     scaling = 1.0 / math.sqrt(128)
 
     def soft(source):
-        scores = right_dot(got[source, :, 128:256], keys) * scaling
+        scores = right_dot(got[source, 1], keys) * scaling
         powers = jnp.exp(scores - jnp.max(scores, axis=1, keepdims=True))
         probs = powers * (1.0 / jnp.sum(powers, axis=1, keepdims=True))
         probs_f[source] = probs
@@ -366,7 +365,7 @@
 
     def pass_v(k):
         arrive([vd_in[k]])
-        send.copy(got.at[sources[k], :, col_v], got_v.at[sources[k]], near, near_v)
+        send.copy(got.at[sources[k], 2], got_v.at[sources[k]], near, near_v)
 
     soft(sources[0])
     pass_v(1)
@@ -376,28 +375,29 @@
     pass_v(2)
     soft(sources[2])
     home = []
-    all_queries = got[:, :, 128:256].reshape(512, 128)
-    all_upward = got[:, :, 384:512].reshape(512, 128)
+    all_queries = got[:, 1].reshape(512, 128)
+    all_upward = got[:, 3].reshape(512, 128)
     all_probs = probs_s[...].reshape(512, 1024)
     d_values = row_dot(all_upward, all_probs).T.astype(BF16).reshape(8, 128, 128)
     outgo_v[...] = d_values[4:8]
     home.append(send.group(back_v, [(outgo_v.at[p["x"]], back_v.at[x], device(p)) for p in across]))
-    outgo[:, :, 384:512] = d_values[0:4]
+    outgo[:, 1] = d_values[0:4]
     arrive([from_near_v])
-    values = jnp.concatenate([got[:, :, 256:384].reshape(512, 128), got_v[...].reshape(512, 128)], axis=0)
-    outgo[:, :, 0:128] = dot(all_probs, values).astype(BF16).reshape(4, 128, 128)
+    values = jnp.concatenate([got[:, 2].reshape(512, 128), got_v[...].reshape(512, 128)], axis=0)
+    outgo[:, 0] = dot(all_probs, values).astype(BF16).reshape(4, 128, 128)
     for k in (1, 3, 2):
-        block = pl.ds(0, 128)
-        home.append(send(outgo.at[xs[k], :, block], back.at[x, :, block], device(moved(at, x=k))))
-
-    def step(i, carry):
+        block = pl.ds(0, 2)
+        home.append(send(outgo.at[xs[k], block], back.at[x, block], device(moved(at, x=k))))
+    for k in (1, 3, 2, 0):
+        i = xs[k]
         probs = probs_f[i]
-        d_probs = right_dot(got[i, :, 384:512], values)
+        d_probs = right_dot(got[i, 3], values)
         inner = jnp.sum(probs * d_probs, axis=1, keepdims=True)
-        scores_s[i] = (probs * (d_probs - inner) * scaling).astype(BF16)
-        return carry
-
-    lax.fori_loop(0, 4, step, 0)
+        d_scores = (probs * (d_probs - inner) * scaling).astype(BF16)
+        scores_s[i] = d_scores
+        outgo[i, 2] = dot(d_scores, keys).astype(BF16)
+        if k:
+            home.append(send(outgo.at[i, 2], back.at[x, 2], device(moved(at, x=k))))
 
     def key_grads(columns):
         d_keys = row_dot(all_queries, scores_s[:, :, columns].reshape(512, 512)).T
@@ -405,22 +405,19 @@
 
     outgo_k[...] = key_grads(slice(512, 1024))
     home.append(send.group(back_k, [(outgo_k.at[p["x"]], back_k.at[x], device(p)) for p in across]))
-    outgo[:, :, 256:384] = key_grads(slice(0, 512))
-    outgo[:, :, 128:256] = dot(scores_s[...].reshape(512, 1024), keys).astype(BF16).reshape(4, 128, 128)
+    outgo[:, 3] = key_grads(slice(0, 512))
     for k in (1, 3, 2):
-        block = pl.ds(128, 384)
-        home.append(send(outgo.at[xs[k], :, block], back.at[x, :, block], device(moved(at, x=k))))
+        home.append(send(outgo.at[xs[k], 3], back.at[x, 3], device(moved(at, x=k))))
     back[x] = outgo[x]
     arrive(home)
     send.finish()
     for head in range(H):
         columns = slice(128 * head, 128 * head + 128)
-        attended[:, columns] = back[head, :, 0:128]
-        d_proj[:, columns] = back[head, :, 128:256]
-        for kind, other in ((1, back_k), (2, back_v)):
-            total = back[head, :, 128 + 128 * kind : 256 + 128 * kind].astype(F32) + other[head].astype(F32)
-            start = 512 * kind + 128 * head
-            d_proj[:, start : start + 128] = total.astype(BF16)
+        attended[:, columns] = back[head, 0]
+        d_proj[:, columns] = back[head, 2]
+        for start, place, other in ((512, 3, back_k), (1024, 1, back_v)):
+            total = back[head, place].astype(F32) + other[head].astype(F32)
+            d_proj[:, start + 128 * head : start + 128 * head + 128] = total.astype(BF16)
 
     attended_t[...] = attended[...].T.reshape(4, 4, 2, 16, 128)
     d_halves = [d_proj[:, 0:768], d_proj[:, 768:1536]]
@@ -460,14 +457,6 @@
     right_z, left_z = device(moved(at, zh=1)), device(moved(at, zh=3))
     low, high = pl.ds(0, 2), pl.ds(2, 2)
     sides = ((0, 1, right_x, right_y), (1, 3, left_x, left_y))
-    sum_cx(2)
-    far_cx = [
-        send(px.at[quarters, zs[2]], fcx.at[side], to) for side, quarters, to in ((0, low, right_z), (1, high, left_z))
-    ]
-    sum_cy(2)
-    far_cy = [
-        send(py.at[heights, ys[2]], fcy.at[side], to) for side, heights, to in ((0, low, right_y), (1, high, left_y))
-    ]
     d_normed = 0.0
     for terms, choose in ((d_x, choose_x), (d_y, choose_y)):
         d_high = terms.astype(BF16)
@@ -478,6 +467,14 @@
     )
     d_pre = (d_feature * slope[...]).astype(BF16)
 
+    sum_cx(2)
+    far_cx = [
+        send(px.at[quarters, zs[2]], fcx.at[side], to) for side, quarters, to in ((0, low, right_z), (1, high, left_z))
+    ]
+    sum_cy(2)
+    far_cy = [
+        send(py.at[heights, ys[2]], fcy.at[side], to) for side, heights, to in ((0, low, right_y), (1, high, left_y))
+    ]
     def conv_grads(parity, to_a, to_b):
         def one(i):
             block = dot(taps_t[i, :, parity].reshape(384, 128), d_pre).astype(BF16).reshape(4, 96, 768)
@@ -670,9 +667,8 @@
         (4, 4, 2, 4, 16, 1152), (4, 4, 2, 80, 768), (16, 768), (16, 768),
         (4, 128, 768), (4, 4, 2, 96, 128), (128, 512), (4, 4, 2, 16, 128), (768, 512), (768, 512),
         (128, 512), (128, 512), (4, 4, 2, 16, 128), (4, 4, 2, 16, 128), (128, 1536), (128, 512), (4, 4, 2, 16, 128),
-        (4, 128, 512),
-        (4, 128, 512), (4, 128, 128), (4, 128, 128), (4, 128, 512), (4, 128, 128), (4, 128, 128),
-        (4, 128, 512), (4, 128, 128), (4, 128, 128),
+        (4, 4, 128, 128), (4, 4, 128, 128), (4, 128, 128), (4, 128, 128), (4, 4, 128, 128), (4, 128, 128), (4, 128, 128),
+        (4, 4, 128, 128), (4, 128, 128), (4, 128, 128),
         (4, 128, 1024), (4, 128, 1024),
     ] + 3 * [(4, 4, 64, 768), (4, 4, 64, 768), (4, 4, 4, 16, 384), (4, 4, 16, 768)] + [
         (2, 2, 2, 4, 16, 384), (2, 2, 4, 4, 16, 384), (2, 4, 4, 16, 384), (2, 3, 4, 16, 384),
@@ -694,7 +690,7 @@
         out_specs=(vmem,) * 4,
         scratch_shapes=[pltpu.VMEM(shape, BF16) for shape in low]
         + [pltpu.VMEM(shape, F32) for shape in wide]
-        + [pltpu.SemaphoreType.DMA((90,)), pltpu.SemaphoreType.DMA((135,))],
+        + [pltpu.SemaphoreType.DMA((90,)), pltpu.SemaphoreType.DMA((138,))],
         compiler_params=pltpu.CompilerParams(
             collective_id=1, has_side_effects=True, vmem_limit_bytes=60 * 2**20
         ),

time: 119 us -> 118 us (level)
  Pallas kernels: 119 us -> 117 us
    pallas_call x1, Pallas kernels: 117 us -> 115 us  [layer(): pl.pallas_call(layer_kernel, name='layer', out_shape=tuple((jax.ShapeDtyp...]
where the time goes in v7:
time: 118 us
  Pallas kernels  117 us (99%)
    pallas_call x1, Pallas kernels, layer(): pl.pallas_call(layer_kernel, name='layer', out_shape=tuple((jax.ShapeDtyp...  115 us

profile of v7, /device:TPU:32, one launch (start us, length us, event | category | flops | bytes accessed | tf_op | source)
XLA Modules:
  0.0 117.8 jit_solution(16941471720970196439)
XLA Ops:
  0.6 115.1 %layer.1 = (bf16[256,768]{1,0:T(8,128)(2,1)}, bf16[4,2,2,16,384]{4,3,2,1,0:T(8,128)(2,1)}, bf16[4,16,384]{2,1,0:T(8,128)(2,1)}, bf16[16,768]{1,0:T(8,128)(2,1)}) custom-call(bf16[96,768]{1,0:T(8,128)(2,1)} %conv_s.1, bf16[16,768]{1,0:T(8,128)(2,1)} %dna_s.1, bf16[24,1536]{1,0:T(8,128)(2,1)} %qkv_s.1, bf16[16,768]{1,0:T(8,128)(2,1)} %out_s.1, ...), custom_call_target="tpu_custom_call" | custom-call | tf_op jit(solution)/shard_map/layer/pallas_call | solution.py:682
  115.8 2.0 %finish.1 = (bf16[1,256,768]{2,1,0:T(8,128)(2,1)}, f32[96,768]{1,0:T(8,128)}, f32[16,768]{1,0:T(8,128)}, f32[24,1536]{1,0:T(8,128)}, f32[16,768]{1,0:T(8,128)}) custom-call(bf16[256,768]{1,0:T(8,128)(2,1)} %get-tuple-element.9.seq_i, bf16[4,2,2,16,384]{4,3,2,1,0:T(8,128)(2,1)} %get-tuple-element.10.final, bf16[4,16,384]{2,1,0:T(8,128)(2,1)} %get-tuple-element.11.final_x, ...), custom_call_target="tpu_custom_call" | custom-call | tf_op jit(solution)/shard_map/finish/pallas_call | solution.py:698

commit v8 on v7

--- a/solution.py
+++ b/solution.py
@@ -37,20 +37,24 @@
 
 class Sender:
     def __init__(self, send_sems, recv_sems):
-        self.send_sems, self.recv_sems, self.sent, self.due, self.copies = send_sems, recv_sems, 0, 0, []
+        self.send_sems, self.recv_sems, self.sent, self.due = send_sems, recv_sems, 0, 0
+        self.free, self.copies = [], []
 
     def copy(self, src, dst, to, recv):
+        if not self.free:
+            self.free.append(self.sent)
+            self.sent += 1
+        place = self.free.pop(0)
         copy = pltpu.make_async_remote_copy(
             src_ref=src,
             dst_ref=dst,
-            send_sem=self.send_sems.at[self.sent],
+            send_sem=self.send_sems.at[place],
             recv_sem=self.recv_sems.at[recv],
             device_id=to,
             device_id_type=MESH,
         )
         copy.start()
-        self.sent += 1
-        self.copies.append(copy)
+        self.copies.append((copy, place))
         return copy
 
     def __call__(self, src, dst, to):
@@ -70,10 +74,12 @@
             device_id_type=MESH,
         )
 
-    def finish(self):
-        for copy in self.copies:
+    def finish(self, oldest=None):
+        done = self.copies[:oldest]
+        for copy, place in done:
             copy.wait_send()
-        self.sent, self.copies = 0, []
+            self.free.append(place)
+        self.copies = self.copies[len(done) :]
 
 
 def arrive(copies):
@@ -256,6 +262,7 @@
     rings_x[2].both_in()
     rings_y[2].both_in()
 
+    send.finish(24)
     arrive(halo)
     for j in range(6):
         lanes = slice(128 * j, 128 * j + 128)
@@ -326,9 +333,10 @@
     wide_x[...] = dot(normed, choose_x[...]).astype(BF16)
     wide_y[...] = dot(normed, choose_y[...]).astype(BF16)
     side_of = lax.rem(lax.broadcasted_iota(jnp.int32, (128, 512), 1), 16) // 8
+    own_y = [jnp.where(side_of == i, wide_y[...].astype(F32), 0.0).astype(BF16) for i in range(2)]
+    from_y = dot(jnp.concatenate(own_y, axis=0), qy_full())
     for i in range(2):
-        own_y = jnp.where(side_of == i, wide_y[...].astype(F32), 0.0).astype(BF16)
-        projected = (dot(wide_x[...], qx_full(i)) + dot(own_y, qy_full())).astype(BF16)
+        projected = (dot(wide_x[...], qx_full(i)) + from_y[128 * i : 128 * i + 128]).astype(BF16)
         for piece in range(6):
             kind, head = divmod(6 * i + piece, 4)
             mine[head, (1, 0, 2)[kind]] = projected[:, 128 * piece : 128 * piece + 128]
@@ -356,24 +364,24 @@
     keys = jnp.concatenate([got[:, 0].reshape(512, 128), got_k[...].reshape(512, 128)], axis=0)
     scaling = 1.0 / math.sqrt(128)
 
-    def soft(source):
-        scores = right_dot(got[source, 1], keys) * scaling
+    pairs = (slice(0, 2), slice(2, 4))
+
+    def soft(pair):
+        scores = right_dot(got[pair, 1].reshape(256, 128), keys) * scaling
         powers = jnp.exp(scores - jnp.max(scores, axis=1, keepdims=True))
         probs = powers * (1.0 / jnp.sum(powers, axis=1, keepdims=True))
-        probs_f[source] = probs
-        probs_s[source] = probs.astype(BF16)
+        probs_f[pair] = probs.reshape(2, 128, 1024)
+        probs_s[pair] = probs.astype(BF16).reshape(2, 128, 1024)
 
     def pass_v(k):
         arrive([vd_in[k]])
         send.copy(got.at[sources[k], 2], got_v.at[sources[k]], near, near_v)
 
-    soft(sources[0])
+    soft(pairs[0])
     pass_v(1)
     pass_v(3)
-    soft(sources[1])
-    soft(sources[3])
+    soft(pairs[1])
     pass_v(2)
-    soft(sources[2])
     home = []
     all_queries = got[:, 1].reshape(512, 128)
     all_upward = got[:, 3].reshape(512, 128)
@@ -388,16 +396,15 @@
     for k in (1, 3, 2):
         block = pl.ds(0, 2)
         home.append(send(outgo.at[xs[k], block], back.at[x, block], device(moved(at, x=k))))
-    for k in (1, 3, 2, 0):
-        i = xs[k]
-        probs = probs_f[i]
-        d_probs = right_dot(got[i, 3], values)
+    for pair in pairs:
+        probs = probs_f[pair].reshape(256, 1024)
+        d_probs = right_dot(got[pair, 3].reshape(256, 128), values)
         inner = jnp.sum(probs * d_probs, axis=1, keepdims=True)
         d_scores = (probs * (d_probs - inner) * scaling).astype(BF16)
-        scores_s[i] = d_scores
-        outgo[i, 2] = dot(d_scores, keys).astype(BF16)
-        if k:
-            home.append(send(outgo.at[i, 2], back.at[x, 2], device(moved(at, x=k))))
+        scores_s[pair] = d_scores.reshape(2, 128, 1024)
+        outgo[pair, 2] = dot(d_scores, keys).astype(BF16).reshape(2, 128, 128)
+    for k in (1, 3, 2):
+        home.append(send(outgo.at[xs[k], 2], back.at[x, 2], device(moved(at, x=k))))
 
     def key_grads(columns):
         d_keys = row_dot(all_queries, scores_s[:, :, columns].reshape(512, 512)).T
@@ -441,8 +448,8 @@
         core_cy[k] = send(py_s.at[:, ys[k]], py_r.at[:, ys[k]], sibling)
     qkv_grads(c, px, py)
     d_x = sum(right_dot(d_halves[i], qx_full(i)) for i in range(2))
-    both = [right_dot(d_half, qy_full()) for d_half in d_halves]
-    d_y = jnp.where(side_of == 0, both[0], both[1])
+    both = right_dot(jnp.concatenate(d_halves, axis=0), qy_full())
+    d_y = jnp.where(side_of == 0, both[0:128], both[128:256])
 
     def sum_cx(k):
         arrive([core_cx[k]])
@@ -461,7 +468,8 @@
     for terms, choose in ((d_x, choose_x), (d_y, choose_y)):
         d_high = terms.astype(BF16)
         d_low = (terms - d_high.astype(F32)).astype(BF16)
-        d_normed += right_dot(d_high, choose[...]) + right_dot(d_low, choose[...])
+        both = right_dot(jnp.concatenate([d_high, d_low], axis=0), choose[...])
+        d_normed += both[0:128] + both[128:256]
     d_feature = upstream[...].astype(F32) + inverse[...] * (
         d_normed - unit[...] * jnp.mean(d_normed * unit[...], axis=1, keepdims=True)
     )
@@ -567,6 +575,7 @@
     sum_a(0)
     sum_b(0)
 
+    send.finish(28)
     rows_f[:, 256:272] = jnp.zeros((6, 16, 128), F32)
     for i in range(4):
         terms = right_dot(d_pre, conv_full(i))
@@ -621,6 +630,7 @@
             scy3[...] = add(scy3, scy2[...], rcy3[...])
             cy4 = three("x", rcy4, lambda k: scy3)
 
+    send.finish(12)
     for h in range(2):
         arrive([a3[h]])
         sa3[h] = add(sa3, sa2[h, zh], ra3[h, 0], ra3[h, 1], ra3[h, 2])
@@ -690,7 +700,7 @@
         out_specs=(vmem,) * 4,
         scratch_shapes=[pltpu.VMEM(shape, BF16) for shape in low]
         + [pltpu.VMEM(shape, F32) for shape in wide]
-        + [pltpu.SemaphoreType.DMA((90,)), pltpu.SemaphoreType.DMA((138,))],
+        + [pltpu.SemaphoreType.DMA((60,)), pltpu.SemaphoreType.DMA((138,))],
         compiler_params=pltpu.CompilerParams(
             collective_id=1, has_side_effects=True, vmem_limit_bytes=60 * 2**20
         ),

time: 118 us -> 117 us (level)
  no operation moved by 1% of the time
where the time goes in v8:
time: 117 us
  Pallas kernels  116 us (99%)
    pallas_call x1, Pallas kernels, layer(): pl.pallas_call(layer_kernel, name='layer', out_shape=tuple((jax.ShapeDtyp...  114 us

profile of v8, /device:TPU:32, one launch (start us, length us, event | category | flops | bytes accessed | tf_op | source)
XLA Modules:
  0.0 116.8 jit_solution(2956802777969240634)
XLA Ops:
  0.6 114.1 %layer.1 = (bf16[256,768]{1,0:T(8,128)(2,1)}, bf16[4,2,2,16,384]{4,3,2,1,0:T(8,128)(2,1)}, bf16[4,16,384]{2,1,0:T(8,128)(2,1)}, bf16[16,768]{1,0:T(8,128)(2,1)}) custom-call(bf16[96,768]{1,0:T(8,128)(2,1)} %conv_s.1, bf16[16,768]{1,0:T(8,128)(2,1)} %dna_s.1, bf16[24,1536]{1,0:T(8,128)(2,1)} %qkv_s.1, bf16[16,768]{1,0:T(8,128)(2,1)} %out_s.1, ...), custom_call_target="tpu_custom_call" | custom-call | tf_op jit(solution)/shard_map/layer/pallas_call | solution.py:692
  114.7 2.0 %finish.1 = (bf16[1,256,768]{2,1,0:T(8,128)(2,1)}, f32[96,768]{1,0:T(8,128)}, f32[16,768]{1,0:T(8,128)}, f32[24,1536]{1,0:T(8,128)}, f32[16,768]{1,0:T(8,128)}) custom-call(bf16[256,768]{1,0:T(8,128)(2,1)} %get-tuple-element.9.seq_i, bf16[4,2,2,16,384]{4,3,2,1,0:T(8,128)(2,1)} %get-tuple-element.10.final, bf16[4,16,384]{2,1,0:T(8,128)(2,1)} %get-tuple-element.11.final_x, ...), custom_call_target="tpu_custom_call" | custom-call | tf_op jit(solution)/shard_map/finish/pallas_call | solution.py:708

commit v9 on v8

--- a/solution.py
+++ b/solution.py
@@ -382,20 +382,20 @@
     pass_v(3)
     soft(pairs[1])
     pass_v(2)
-    home = []
+    home_v, home_q, home_k = [], [], []
     all_queries = got[:, 1].reshape(512, 128)
     all_upward = got[:, 3].reshape(512, 128)
     all_probs = probs_s[...].reshape(512, 1024)
     d_values = row_dot(all_upward, all_probs).T.astype(BF16).reshape(8, 128, 128)
     outgo_v[...] = d_values[4:8]
-    home.append(send.group(back_v, [(outgo_v.at[p["x"]], back_v.at[x], device(p)) for p in across]))
+    home_v.append(send.group(back_v, [(outgo_v.at[p["x"]], back_v.at[x], device(p)) for p in across]))
     outgo[:, 1] = d_values[0:4]
     arrive([from_near_v])
     values = jnp.concatenate([got[:, 2].reshape(512, 128), got_v[...].reshape(512, 128)], axis=0)
     outgo[:, 0] = dot(all_probs, values).astype(BF16).reshape(4, 128, 128)
     for k in (1, 3, 2):
         block = pl.ds(0, 2)
-        home.append(send(outgo.at[xs[k], block], back.at[x, block], device(moved(at, x=k))))
+        home_v.append(send(outgo.at[xs[k], block], back.at[x, block], device(moved(at, x=k))))
     for pair in pairs:
         probs = probs_f[pair].reshape(256, 1024)
         d_probs = right_dot(got[pair, 3].reshape(256, 128), values)
@@ -404,40 +404,58 @@
         scores_s[pair] = d_scores.reshape(2, 128, 1024)
         outgo[pair, 2] = dot(d_scores, keys).astype(BF16).reshape(2, 128, 128)
     for k in (1, 3, 2):
-        home.append(send(outgo.at[xs[k], 2], back.at[x, 2], device(moved(at, x=k))))
+        home_q.append(send(outgo.at[xs[k], 2], back.at[x, 2], device(moved(at, x=k))))
 
     def key_grads(columns):
         d_keys = row_dot(all_queries, scores_s[:, :, columns].reshape(512, 512)).T
         return d_keys.astype(BF16).reshape(4, 128, 128)
 
     outgo_k[...] = key_grads(slice(512, 1024))
-    home.append(send.group(back_k, [(outgo_k.at[p["x"]], back_k.at[x], device(p)) for p in across]))
+    home_k.append(send.group(back_k, [(outgo_k.at[p["x"]], back_k.at[x], device(p)) for p in across]))
     outgo[:, 3] = key_grads(slice(0, 512))
     for k in (1, 3, 2):
-        home.append(send(outgo.at[xs[k], 3], back.at[x, 3], device(moved(at, x=k))))
+        home_k.append(send(outgo.at[xs[k], 3], back.at[x, 3], device(moved(at, x=k))))
     back[x] = outgo[x]
-    arrive(home)
+
+    def columns_of(head, start=0):
+        return slice(start + 128 * head, start + 128 * head + 128)
+
+    arrive(home_v)
+    for head in range(H):
+        attended[:, columns_of(head)] = back[head, 0]
+        total = back[head, 1].astype(F32) + back_v[head].astype(F32)
+        d_proj[:, columns_of(head, 1024)] = total.astype(BF16)
+    attended_t[...] = attended[...].T.reshape(4, 4, 2, 16, 128)
+    for parity, to_b in ((1 - c, pb_s), (c, pb)):
+        left = attended_t[:, :, parity].reshape(256, 128)
+        to_b[:, :, 48:64] = dot(left, upstream[...]).astype(BF16).reshape(4, 4, 16, 768)
+    arrive(home_q)
+    for head in range(H):
+        d_proj[:, columns_of(head)] = back[head, 2]
+
+    def qkv_quarters(parity, to_x, quarters):
+        left = wide_xt[:, :, parity].reshape(256, 128)
+        for q in quarters:
+            block = dot(left, d_proj[:, 384 * q : 384 * q + 384]).astype(BF16)
+            to_x[q] = block.reshape(4, 4, 16, 384)
+
+    qkv_quarters(1 - c, px_s, (0, 3))
+    qkv_quarters(c, px, (0, 3))
+    d_q, d_v = d_proj[:, 0:512], d_proj[:, 1024:1536]
+    d_x = right_dot(d_q, qx_full(0)[:, 0:512]) + right_dot(d_v, qx_full(1)[:, 256:768])
+    d_y0, d_y1 = right_dot(d_q, qy_full()[:, 0:512]), right_dot(d_v, qy_full()[:, 256:768])
+    arrive(home_k)
     send.finish()
     for head in range(H):
-        columns = slice(128 * head, 128 * head + 128)
-        attended[:, columns] = back[head, 0]
-        d_proj[:, columns] = back[head, 2]
-        for start, place, other in ((512, 3, back_k), (1024, 1, back_v)):
-            total = back[head, place].astype(F32) + other[head].astype(F32)
-            d_proj[:, start + 128 * head : start + 128 * head + 128] = total.astype(BF16)
-
-    attended_t[...] = attended[...].T.reshape(4, 4, 2, 16, 128)
-    d_halves = [d_proj[:, 0:768], d_proj[:, 768:1536]]
+        total = back[head, 3].astype(F32) + back_k[head].astype(F32)
+        d_proj[:, columns_of(head, 512)] = total.astype(BF16)
+
     row_side = lax.rem(lax.broadcasted_iota(jnp.int32, (256, 768), 0), 16)
 
     def qkv_grads(parity, to_x, to_y):
-        left = wide_xt[:, :, parity].reshape(256, 128)
-        for i in range(2):
-            block = dot(left, d_halves[i]).astype(BF16)
-            for j in range(2):
-                to_x[2 * i + j] = block[:, 384 * j : 384 * j + 384].reshape(4, 4, 16, 384)
+        qkv_quarters(parity, to_x, (1, 2))
         left = wide_yt[:, :, parity].reshape(256, 128)
-        both = [dot(left, d_half) for d_half in d_halves]
+        both = [dot(left, d_proj[:, 768 * i : 768 * i + 768]) for i in range(2)]
         to_y[...] = jnp.where(row_side < 8, both[0], both[1]).astype(BF16).reshape(4, 4, 16, 768)
 
     order = (2, 1, 3, 0)
@@ -447,9 +465,11 @@
         core_cx[k] = send(px_s.at[:, zs[k]], px_r.at[:, zs[k]], sibling)
         core_cy[k] = send(py_s.at[:, ys[k]], py_r.at[:, ys[k]], sibling)
     qkv_grads(c, px, py)
-    d_x = sum(right_dot(d_halves[i], qx_full(i)) for i in range(2))
-    both = right_dot(jnp.concatenate(d_halves, axis=0), qy_full())
-    d_y = jnp.where(side_of == 0, both[0:128], both[128:256])
+    d_k0, d_k1 = d_proj[:, 512:768], d_proj[:, 768:1024]
+    d_x += right_dot(d_k0, qx_full(0)[:, 512:768]) + right_dot(d_k1, qx_full(1)[:, 0:256])
+    d_y0 += right_dot(d_k0, qy_full()[:, 512:768])
+    d_y1 += right_dot(d_k1, qy_full()[:, 0:256])
+    d_y = jnp.where(side_of == 0, d_y0, d_y1)
 
     def sum_cx(k):
         arrive([core_cx[k]])
@@ -492,8 +512,6 @@
         loop(4, one)
         left = onehot_t[:, :, parity].reshape(256, 128)
         to_b[:, :, 32:48] = dot(left, d_pre).astype(BF16).reshape(4, 4, 16, 768)
-        left = attended_t[:, :, parity].reshape(256, 128)
-        to_b[:, :, 48:64] = dot(left, upstream[...]).astype(BF16).reshape(4, 4, 16, 768)
 
     conv_grads(1 - c, pa_s, pb_s)
     for k in order:

time: 117 us -> 117 us (level)
  no operation moved by 1% of the time
where the time goes in v9:
time: 117 us; the launch traced here: 116 us
  Pallas kernels  116 us (99%)
    pallas_call x1, Pallas kernels, layer(): pl.pallas_call(layer_kernel, name='layer', out_shape=tuple((jax.ShapeDtyp...  114 us

profile of v9, /device:TPU:32, one launch (start us, length us, event | category | flops | bytes accessed | tf_op | source)
XLA Modules:
  0.0 116.4 jit_solution(18119532257929975871)
XLA Ops:
  0.6 113.7 %layer.1 = (bf16[256,768]{1,0:T(8,128)(2,1)}, bf16[4,2,2,16,384]{4,3,2,1,0:T(8,128)(2,1)}, bf16[4,16,384]{2,1,0:T(8,128)(2,1)}, bf16[16,768]{1,0:T(8,128)(2,1)}) custom-call(bf16[96,768]{1,0:T(8,128)(2,1)} %conv_s.1, bf16[16,768]{1,0:T(8,128)(2,1)} %dna_s.1, bf16[24,1536]{1,0:T(8,128)(2,1)} %qkv_s.1, bf16[16,768]{1,0:T(8,128)(2,1)} %out_s.1, ...), custom_call_target="tpu_custom_call" | custom-call | tf_op jit(solution)/shard_map/layer/pallas_call | solution.py:710
  114.3 2.0 %finish.1 = (bf16[1,256,768]{2,1,0:T(8,128)(2,1)}, f32[96,768]{1,0:T(8,128)}, f32[16,768]{1,0:T(8,128)}, f32[24,1536]{1,0:T(8,128)}, f32[16,768]{1,0:T(8,128)}) custom-call(bf16[256,768]{1,0:T(8,128)(2,1)} %get-tuple-element.9.seq_i, bf16[4,2,2,16,384]{4,3,2,1,0:T(8,128)(2,1)} %get-tuple-element.10.final, bf16[4,16,384]{2,1,0:T(8,128)(2,1)} %get-tuple-element.11.final_x, ...), custom_call_target="tpu_custom_call" | custom-call | tf_op jit(solution)/shard_map/finish/pallas_call | solution.py:726

commit v10 on v9

--- a/solution.py
+++ b/solution.py
@@ -159,7 +159,7 @@
     conv_s, dna_s, qkv_s, out_s, rows_in, letters, upstream,
     seq_o, final, final_x, final_y,
     ga, gb, before, after,
-    taps, taps_t, onehot, onehot_t, choose_x, choose_y, wide_x, wide_y, wide_xt, wide_yt, d_proj, attended, attended_t,
+    taps, taps_y, taps_t, onehot, onehot_t, choose_x, choose_y, wide_x, wide_y, wide_xt, wide_yt, d_proj, attended, attended_t,
     mine, got, got_k, got_v, outgo, outgo_k, outgo_v, back, back_k, back_v, probs_s, scores_s,
     pa_s, pb_s, px_s, py_s, pa, pb, px, py, pa_r, pb_r, px_r, py_r,
     fa, na, sa1, ra2, sa2, ra3, sa3, ra4,
@@ -234,6 +234,11 @@
     repeat = (column // 4 == row).astype(F32).astype(BF16)
     repeated = dot(letters[...].astype(F32).astype(BF16), repeat)
     onehot[...] = (repeated == lax.rem(column, 4).astype(F32)).astype(F32).astype(BF16)
+    row = lax.broadcasted_iota(jnp.int32, (768, 512), 0)
+    column = lax.broadcasted_iota(jnp.int32, (768, 512), 1)
+    first_row = column // 16 * 24
+    choose_x[...] = (first_row + lax.rem(column, 16) == row).astype(F32).astype(BF16)
+    choose_y[...] = (first_row + 16 + lax.rem(column, 8) == row).astype(F32).astype(BF16)
     arrive(a1)
     ring_a.start()
     rings_x[0].start()
@@ -271,6 +276,12 @@
         rows_f[j, 264:272] = jnp.where(sq < 7, after[:, lanes].astype(F32)[0:8], 0.0)
         for i in range(4):
             taps[i, :, lanes] = rows_f[j, pl.ds(7 + i, 128, stride=2)].astype(BF16)
+    for i in range(4):
+        whole = taps[i].astype(F32)
+        moved_on = pltpu.roll(whole, 704, 1).astype(BF16)
+        for k in range(4):
+            start = 384 * (k // 2) + 128 * (k % 2)
+            taps_y[k, i] = moved_on[:, start : start + 256] if k % 2 else taps[i, :, start : start + 256]
 
     rings_y[3].far_in()
     pass_b(zs[3])
@@ -285,16 +296,6 @@
     rings_x[2].far_in()
     pass_a(ys[2])
 
-    def transpose_tap(i):
-        taps_t[i] = taps[i].T.reshape(4, 2, 96, 128)
-
-    loop(4, transpose_tap)
-    onehot_t[...] = onehot[...].T.reshape(4, 4, 2, 16, 128)
-    row = lax.broadcasted_iota(jnp.int32, (768, 512), 0)
-    column = lax.broadcasted_iota(jnp.int32, (768, 512), 1)
-    first_row = column // 16 * 24
-    choose_x[...] = (first_row + lax.rem(column, 16) == row).astype(F32).astype(BF16)
-    choose_y[...] = (first_row + 16 + lax.rem(column, 8) == row).astype(F32).astype(BF16)
     arrive(core[:-1])
 
     def conv_full(i):
@@ -313,12 +314,20 @@
     out_full = gb[:, :, :, 48:64].reshape(512, 768)
     d_attend = right_dot(upstream[...], out_full).astype(BF16)
     slope[...] = dot(onehot[...], dna_full)
+
+    def y_block(k):
+        total = 0.0
+        for i in range(4):
+            first = ga[i, ys[k], :, :, :, 0:768].reshape(2, 64, 768)
+            block = jnp.concatenate([first, gb[i, ys[k], :, 0:32]], axis=1).reshape(192, 768)
+            block = jnp.concatenate([block, jnp.zeros((64, 768), BF16)], axis=0)
+            total += dot(taps_y[ys[k], i], block)
+        slope[...] += total
+
+    for k in (0, 3, 1):
+        y_block(k)
     arrive(core[-1:])
-
-    def one_tap(i):
-        slope[...] += dot(taps[i], conv_full(i))
-
-    loop(4, one_tap)
+    y_block(2)
     pre = slope[...]
     bend = jnp.tanh(math.sqrt(2.0 / math.pi) * (pre + 0.044715 * (pre * pre * pre)))
     share = 0.5 * (1.0 + bend)
@@ -358,6 +367,11 @@
     for k in (1, 3, 2):
         arrive([kq_in[k]])
         send.copy(got.at[sources[k], 0], got_k.at[sources[k]], near, near_k)
+    def transpose_tap(i):
+        taps_t[i] = taps[i].T.reshape(4, 2, 96, 128)
+
+    loop(4, transpose_tap)
+    onehot_t[...] = onehot[...].T.reshape(4, 4, 2, 16, 128)
     wide_xt[...] = wide_x[...].T.reshape(4, 4, 2, 16, 128)
     wide_yt[...] = wide_y[...].T.reshape(4, 4, 2, 16, 128)
     arrive([from_near_k])
@@ -693,7 +707,7 @@
     vmem = pl.BlockSpec(memory_space=pltpu.VMEM)
     low = [
         (4, 4, 2, 4, 16, 1152), (4, 4, 2, 80, 768), (16, 768), (16, 768),
-        (4, 128, 768), (4, 4, 2, 96, 128), (128, 512), (4, 4, 2, 16, 128), (768, 512), (768, 512),
+        (4, 128, 768), (4, 4, 128, 256), (4, 4, 2, 96, 128), (128, 512), (4, 4, 2, 16, 128), (768, 512), (768, 512),
         (128, 512), (128, 512), (4, 4, 2, 16, 128), (4, 4, 2, 16, 128), (128, 1536), (128, 512), (4, 4, 2, 16, 128),
         (4, 4, 128, 128), (4, 4, 128, 128), (4, 128, 128), (4, 128, 128), (4, 4, 128, 128), (4, 128, 128), (4, 128, 128),
         (4, 4, 128, 128), (4, 128, 128), (4, 128, 128),

time: 117 us -> 116 us (level)
  no operation moved by 1% of the time
where the time goes in v10:
time: 116 us
  Pallas kernels  115 us (99%)
    pallas_call x1, Pallas kernels, layer(): pl.pallas_call(layer_kernel, name='layer', out_shape=tuple((jax.ShapeDtyp...  113 us

profile of v10, /device:TPU:32, one launch (start us, length us, event | category | flops | bytes accessed | tf_op | source)
XLA Modules:
  0.0 116.1 jit_solution(6217240517752078390)
XLA Ops:
  0.6 113.4 %layer.1 = (bf16[256,768]{1,0:T(8,128)(2,1)}, bf16[4,2,2,16,384]{4,3,2,1,0:T(8,128)(2,1)}, bf16[4,16,384]{2,1,0:T(8,128)(2,1)}, bf16[16,768]{1,0:T(8,128)(2,1)}) custom-call(bf16[96,768]{1,0:T(8,128)(2,1)} %conv_s.1, bf16[16,768]{1,0:T(8,128)(2,1)} %dna_s.1, bf16[24,1536]{1,0:T(8,128)(2,1)} %qkv_s.1, bf16[16,768]{1,0:T(8,128)(2,1)} %out_s.1, ...), custom_call_target="tpu_custom_call" | custom-call | tf_op jit(solution)/shard_map/layer/pallas_call | solution.py:724
  114.0 2.0 %finish.1 = (bf16[1,256,768]{2,1,0:T(8,128)(2,1)}, f32[96,768]{1,0:T(8,128)}, f32[16,768]{1,0:T(8,128)}, f32[24,1536]{1,0:T(8,128)}, f32[16,768]{1,0:T(8,128)}) custom-call(bf16[256,768]{1,0:T(8,128)(2,1)} %get-tuple-element.9.seq_i, bf16[4,2,2,16,384]{4,3,2,1,0:T(8,128)(2,1)} %get-tuple-element.10.final, bf16[4,16,384]{2,1,0:T(8,128)(2,1)} %get-tuple-element.11.final_x, ...), custom_call_target="tpu_custom_call" | custom-call | tf_op jit(solution)/shard_map/finish/pallas_call | solution.py:740

commit v11 on v10

--- a/solution.py
+++ b/solution.py
@@ -458,8 +458,8 @@
     d_q, d_v = d_proj[:, 0:512], d_proj[:, 1024:1536]
     d_x = right_dot(d_q, qx_full(0)[:, 0:512]) + right_dot(d_v, qx_full(1)[:, 256:768])
     d_y0, d_y1 = right_dot(d_q, qy_full()[:, 0:512]), right_dot(d_v, qy_full()[:, 256:768])
+    send.finish(-7)
     arrive(home_k)
-    send.finish()
     for head in range(H):
         total = back[head, 3].astype(F32) + back_k[head].astype(F32)
         d_proj[:, columns_of(head, 512)] = total.astype(BF16)
@@ -678,10 +678,11 @@
             final_y[...] = add(final_y, scy3[...], rcy4[0], rcy4[1], rcy4[2])
     for h in range(2):
         arrive([a4[h]])
-        final[x, 0, h] = add(final, sa3[h], ra4[h])
+        final[x, h, 0] = add(final, sa3[h], ra4[h])
         arrive([b4[h]])
-        final[x, 1, h] = add(final, sb3[h], rb4[h])
-    spread += [send(final.at[x], final.at[x], device(moved(at, x=k))) for k in (1, 2, 3)]
+        final[x, h, 1] = add(final, sb3[h], rb4[h])
+        spread += [send(final.at[x, h], final.at[x, h], device(moved(at, x=k))) for k in (1, 3, 2)]
+    send.finish(-6)
     arrive(spread)
     send.finish()
 
@@ -691,11 +692,11 @@
     for h in range(2):
         columns = slice(384 * h, 384 * h + 384)
         for q in range(4):
-            conv_o[16 * q : 16 * q + 16, columns] = final[q, 0, h].astype(F32)
-        conv_o[64:80, columns] = final[0, 1, h].astype(F32)
-        conv_o[80:96, columns] = final[1, 1, h].astype(F32)
-        dna_o[:, columns] = final[2, 1, h].astype(F32)
-        out_o[:, columns] = final[3, 1, h].astype(F32)
+            conv_o[16 * q : 16 * q + 16, columns] = final[q, h, 0].astype(F32)
+        conv_o[64:80, columns] = final[0, h, 1].astype(F32)
+        conv_o[80:96, columns] = final[1, h, 1].astype(F32)
+        dna_o[:, columns] = final[2, h, 1].astype(F32)
+        out_o[:, columns] = final[3, h, 1].astype(F32)
     for q in range(4):
         qkv_o[0:16, 384 * q : 384 * q + 384] = final_x[q].astype(F32)
     last_rows = final_y[...].astype(F32)
@@ -732,7 +733,7 @@
         out_specs=(vmem,) * 4,
         scratch_shapes=[pltpu.VMEM(shape, BF16) for shape in low]
         + [pltpu.VMEM(shape, F32) for shape in wide]
-        + [pltpu.SemaphoreType.DMA((60,)), pltpu.SemaphoreType.DMA((138,))],
+        + [pltpu.SemaphoreType.DMA((60,)), pltpu.SemaphoreType.DMA((141,))],
         compiler_params=pltpu.CompilerParams(
             collective_id=1, has_side_effects=True, vmem_limit_bytes=60 * 2**20
         ),

time: 116 us -> 115 us (level)
  no operation moved by 1% of the time
where the time goes in v11:
time: 115 us
  Pallas kernels  114 us (99%)
    pallas_call x1, Pallas kernels, layer(): pl.pallas_call(layer_kernel, name='layer', out_shape=tuple((jax.ShapeDtyp...  112 us

profile of v11, /device:TPU:32, one launch (start us, length us, event | category | flops | bytes accessed | tf_op | source)
XLA Modules:
  0.0 115.0 jit_solution(6353560027363737999)
XLA Ops:
  0.6 112.3 %layer.1 = (bf16[256,768]{1,0:T(8,128)(2,1)}, bf16[4,2,2,16,384]{4,3,2,1,0:T(8,128)(2,1)}, bf16[4,16,384]{2,1,0:T(8,128)(2,1)}, bf16[16,768]{1,0:T(8,128)(2,1)}) custom-call(bf16[96,768]{1,0:T(8,128)(2,1)} %conv_s.1, bf16[16,768]{1,0:T(8,128)(2,1)} %dna_s.1, bf16[24,1536]{1,0:T(8,128)(2,1)} %qkv_s.1, bf16[16,768]{1,0:T(8,128)(2,1)} %out_s.1, ...), custom_call_target="tpu_custom_call" | custom-call | tf_op jit(solution)/shard_map/layer/pallas_call | solution.py:725
  113.0 2.0 %finish.1 = (bf16[1,256,768]{2,1,0:T(8,128)(2,1)}, f32[96,768]{1,0:T(8,128)}, f32[16,768]{1,0:T(8,128)}, f32[24,1536]{1,0:T(8,128)}, f32[16,768]{1,0:T(8,128)}) custom-call(bf16[256,768]{1,0:T(8,128)(2,1)} %get-tuple-element.9.seq_i, bf16[4,2,2,16,384]{4,3,2,1,0:T(8,128)(2,1)} %get-tuple-element.10.final, bf16[4,16,384]{2,1,0:T(8,128)(2,1)} %get-tuple-element.11.final_x, ...), custom_call_target="tpu_custom_call" | custom-call | tf_op jit(solution)/shard_map/finish/pallas_call | solution.py:741

commit v12 on v10

--- a/solution.py
+++ b/solution.py
@@ -593,7 +593,7 @@
 
     def three(axis, whole, source):
         return send.group(
-            whole, [(source(k), whole.at[k - 1], device(moved(at, **{axis: k}))) for k in (1, 3, 2)]
+            whole, [(source(k), whole.at[k - 1], device(moved(at, **{axis: k}))) for k in (2, 1, 3)]
         )
 
     sum_cx(0)

time: 116 us -> 116 us (level)
  no operation moved by 1% of the time
where the time goes in v12:
time: 116 us
  Pallas kernels  115 us (99%)
    pallas_call x1, Pallas kernels, layer(): pl.pallas_call(layer_kernel, name='layer', out_shape=tuple((jax.ShapeDtyp...  113 us

profile of v12, /device:TPU:32, one launch (start us, length us, event | category | flops | bytes accessed | tf_op | source)
XLA Modules:
  0.0 115.8 jit_solution(14506582162439032593)
XLA Ops:
  0.6 113.1 %layer.1 = (bf16[256,768]{1,0:T(8,128)(2,1)}, bf16[4,2,2,16,384]{4,3,2,1,0:T(8,128)(2,1)}, bf16[4,16,384]{2,1,0:T(8,128)(2,1)}, bf16[16,768]{1,0:T(8,128)(2,1)}) custom-call(bf16[96,768]{1,0:T(8,128)(2,1)} %conv_s.1, bf16[16,768]{1,0:T(8,128)(2,1)} %dna_s.1, bf16[24,1536]{1,0:T(8,128)(2,1)} %qkv_s.1, bf16[16,768]{1,0:T(8,128)(2,1)} %out_s.1, ...), custom_call_target="tpu_custom_call" | custom-call | tf_op jit(solution)/shard_map/layer/pallas_call | solution.py:724
  113.8 2.0 %finish.1 = (bf16[1,256,768]{2,1,0:T(8,128)(2,1)}, f32[96,768]{1,0:T(8,128)}, f32[16,768]{1,0:T(8,128)}, f32[24,1536]{1,0:T(8,128)}, f32[16,768]{1,0:T(8,128)}) custom-call(bf16[256,768]{1,0:T(8,128)(2,1)} %get-tuple-element.9.seq_i, bf16[4,2,2,16,384]{4,3,2,1,0:T(8,128)(2,1)} %get-tuple-element.10.final, bf16[4,16,384]{2,1,0:T(8,128)(2,1)} %get-tuple-element.11.final_x, ...), custom_call_target="tpu_custom_call" | custom-call | tf_op jit(solution)/shard_map/finish/pallas_call | solution.py:740
